TPU v7x, 256 devices: a whole 4x4x8 slice. The times are simulated.
256 devices in a mesh: kvseq: 16 (over x, y_hi, core), kvhead: 8 (over z), section: 2 (over y_lo).
Axes of the slice: x: 4, y: 4 (y_hi: 2, y_lo: 2; y = y_hi * 2 + y_lo), z: 8, core: 2. Of those that a mesh axis runs over, the one named last changes fastest.
Arguments:
- hidden_in: bfloat16 [2, 8, 16384], P(None, None, 'kvseq')
- lengths: int32 [8], replicated, may hold values from 1 to 16384, as said below
- norm_gain: bfloat16 [2, 16384], P('section', 'kvseq'), may hold values from 0.099609375 to 1.8984375
- w_query: bfloat16 [2, 16384, 16384], P('section', 'kvseq', 'kvhead')
- w_keyval: bfloat16 [2, 16384, 8, 256], P('section', 'kvseq', 'kvhead')
- w_out: bfloat16 [2, 16384, 16384], P('section', 'kvhead', 'kvseq'), may hold values from -0.1875 to 0.1875
- kv_cache: bfloat16 [2, 8, 8, 16384, 256], P('section', 'kvhead', None, 'kvseq')
Outputs:
- layer_out: bfloat16 [2, 2, 8, 16384], P('section', None, None, 'kvseq')
Inputs may be any that keep to these rules, and one draw needn't show every extreme that they name: `lengths`: some row has length 16384.
All inputs are finite; a program needn't handle non-finite values.
Results may differ from a plain program's by a relative error of at most 0.017.
Values may be sent and summed in bfloat16 or wider, within the bound.
No kernel may reach another device: no remote copies, remote signals or barrier semaphores. Data moves between devices by JAX's collectives and lax.ppermute only.
A program may use at most 64 MiB of HBM per device.

v0:
```python
import jax
import jax.numpy as jnp
from jax import lax
from jax.sharding import PartitionSpec as P

D = 16384
HEAD_DIM = 128


NEG_FLOOR = -1e30
EPSILON = 1e-05


def joined(value, axis, join):
    pieces = jax.tree.map(lambda part: lax.all_gather(part, axis), value)
    head = jax.tree.map(lambda part: part[0], pieces)
    tail = jax.tree.map(lambda part: part[1:], pieces)
    subtotal, _ = lax.scan(lambda subtotal, section: (join(subtotal, section), None), head, tail)
    return subtotal


def shifted(value, axis, steps):
    count = lax.axis_size(axis)
    initial, last = (max(0, -steps), min(count, count - steps))
    return lax.ppermute(value, axis, [(source, source + steps) for source in range(initial, last)])


def combine_pair(left_part, right_part):
    left_max, left_total, left_acc = left_part
    right_max, right_total, right_acc = right_part
    joint_max = jnp.maximum(left_max, right_max)
    left_scale = jnp.exp(left_max - joint_max)
    right_scale = jnp.exp(right_max - joint_max)
    joint_total = left_total * left_scale + right_total * right_scale
    joint_acc = left_acc * left_scale[..., None] + right_acc * right_scale[..., None]
    return (joint_max, joint_total, joint_acc)


def local_partials(queries, cache_block, lengths, offset):
    key_rows = cache_block[..., :HEAD_DIM]
    value_rows = cache_block[..., HEAD_DIM:]
    scores = jnp.einsum("rgd,rcd->rgc", queries, key_rows, preferred_element_type=jnp.float32)
    position = offset + jnp.arange(cache_block.shape[1], dtype=jnp.int32)
    in_range = position[None, None, :] < lengths[:, None, None]
    block_max = jnp.max(jnp.where(in_range, scores, NEG_FLOOR), axis=-1)
    weights = jnp.where(in_range, jnp.exp(scores - block_max[..., None]), 0.0)
    block_total = jnp.sum(weights, axis=-1)
    block_acc = jnp.einsum(
        "rgc,rcd->rgd", weights.astype(jnp.bfloat16), value_rows, preferred_element_type=jnp.float32
    )
    return (block_max, block_total, block_acc)


def finish(run_max, run_total, run_acc, queries, recent, fresh_mask):
    recent_keys = recent[..., :HEAD_DIM]
    recent_vals = recent[..., HEAD_DIM:].astype(jnp.float32)
    new_scores = jnp.einsum(
        "rgd,nrd->rgn", queries, recent_keys, preferred_element_type=jnp.float32
    )
    new_scores = jnp.where(fresh_mask[None, None, :], new_scores, NEG_FLOOR)
    row_top = jnp.maximum(run_max, jnp.max(new_scores, axis=-1))
    old_scale = jnp.exp(run_max - row_top)
    new_weights = jnp.exp(new_scores - row_top[..., None])
    numerator = run_acc * old_scale[..., None] + jnp.einsum(
        "rgn,nrd->rgd", new_weights, recent_vals
    )
    denominator = run_total * old_scale + jnp.sum(new_weights, axis=-1)
    return (numerator / denominator[..., None]).astype(jnp.bfloat16)


def per_device(hidden_in, lengths, norm_gain, w_query, w_keyval, w_out, kv_cache):
    section_count = lax.axis_size("section")
    section_id = lax.axis_index("section")
    seq_id = lax.axis_index("kvseq")
    steps_total, row_count, local_width = hidden_in.shape
    group_width = w_query.shape[2]
    group_size = group_width // HEAD_DIM
    block_len = kv_cache.shape[3]
    gain_row = norm_gain[0].astype(jnp.float32)
    query_mat = w_query[0]
    keyval_mat = w_keyval[0, :, 0, :]
    out_mat = w_out[0]
    cache_block = kv_cache[0, 0]
    offset = seq_id * block_len
    recent = jnp.zeros((steps_total, row_count, 2 * HEAD_DIM), jnp.bfloat16)
    results = jnp.zeros((steps_total, row_count, local_width), jnp.bfloat16)
    received = jnp.zeros((row_count, local_width), jnp.bfloat16)
    step_ids = jnp.arange(steps_total, dtype=jnp.int32)
    slot_count = steps_total + section_count - 1
    for slot_no in range(slot_count):
        step_no = slot_no - section_id
        usable = (step_no >= 0) & (step_no < steps_total)
        safe_step = jnp.clip(step_no, 0, steps_total - 1)
        arriving = hidden_in[min(slot_no, steps_total - 1)]
        hidden = jnp.where(section_id == 0, arriving, received)
        scaled = (hidden.astype(jnp.float32) * gain_row).astype(jnp.bfloat16)
        squares = jnp.sum(jnp.square(hidden.astype(jnp.float32)), axis=-1)
        query_part = jnp.dot(scaled, query_mat, preferred_element_type=jnp.float32)
        keyval_part = jnp.dot(scaled, keyval_mat, preferred_element_type=jnp.float32)
        query_sum, keyval_sum, square_sum = lax.psum((query_part, keyval_part, squares), "kvseq")
        inv_rms = lax.rsqrt(square_sum / D + EPSILON)
        project_queries = (query_sum * inv_rms[:, None] * HEAD_DIM ** (-0.5)).astype(jnp.bfloat16)
        keyvals = (keyval_sum * inv_rms[:, None]).astype(jnp.bfloat16)
        queries, keyvals = (project_queries.reshape(row_count, group_size, HEAD_DIM), keyvals)
        updated = lax.dynamic_update_slice_in_dim(recent, keyvals[None], safe_step, 0)
        fresh_mask = step_ids <= safe_step
        run_max, run_total, run_acc = local_partials(queries, cache_block, lengths, offset)
        joint_max, joint_total, joint_acc = joined(
            (run_max, run_total, run_acc), "kvseq", combine_pair
        )
        attended = finish(joint_max, joint_total, joint_acc, queries, updated, fresh_mask)
        attended = attended.reshape(row_count, group_width)
        partial_out = jnp.dot(attended, out_mat, preferred_element_type=jnp.float32)
        head_total = lax.psum(partial_out, "kvhead")
        produced = (hidden.astype(jnp.float32) + head_total).astype(jnp.bfloat16)
        recent = jnp.where(usable, updated, recent)
        results = jnp.where(
            usable, lax.dynamic_update_slice_in_dim(results, produced[None], safe_step, 0), results
        )
        if slot_no + 1 < slot_count:
            received = shifted(produced, "section", 1)
    return results[None]


def solution(mesh):
    placed = (
        P(None, None, "kvseq"),
        P(),
        P("section", "kvseq"),
        P("section", "kvseq", "kvhead"),
        P("section", "kvseq", "kvhead", None),
        P("section", "kvhead", "kvseq"),
        P("section", "kvhead", None, "kvseq", None),
    )
    return jax.shard_map(
        per_device,
        mesh=mesh,
        in_specs=placed,
        out_specs=P("section", None, None, "kvseq"),
        check_vma=False,
    )
```

profile of v0, /device:TPU:24, one launch (start us, length us, event | category | flops | bytes accessed | tf_op | source)
XLA Modules:
  0.0 705.3 jit_solution(172376872959950387)
XLA Ops:
  6.6 0.8 mul.219
  7.3 3.5 fusion.19
  10.9 0.1 fusion.68
  11.0 0.2 fusion.46
  11.3 33.4 %all-reduce.2 = (f32[8]{0:T(128)S(1)}, f32[8,256]{1,0:T(8,128)S(1)}) all-reduce(f32[8]{0:T(128)S(1)} %fusion.68, f32[8,256]{1,0:T(8,128)S(1)} %fusion.46), channel_id=1, replica_groups=mesh['kvseq'=16,'kvhead'=8,'section'=2] {'kvseq'}, use_global_device_ids=true, to_apply=%region_2.3 | all-reduce | flops 2056 | bytes 16448 | tf_op jit(solution)/shard_map/psum | solution.py:100
  44.7 99.1 %all-reduce.7.cloned.1.call-done = f32[8,2048]{1,0:T(8,128)} async-done(((f32[8,2048]{1,0:T(8,128)}), f32[8,2048]{1,0:T(8,128)}) %all-reduce.7.cloned.1.call-update) | async-done | bytes 65552 | tf_op jit(solution)/shard_map/psum | solution.py:100
  143.9 0.9 fusion.77
  144.8 2.3 select_reduce_fusion.2
  147.1 2.7 fusion.25
  150.0 22.7 %all-gather = f32[128,16]{1,0:T(8,128)S(1)} all-gather(f32[8,16]{1,0:T(8,128)S(1)} %get-tuple-element.205), channel_id=2, replica_groups=mesh['kvseq'=16,'kvhead'=8,'section'=2] {'kvseq'}, dimensions={0}, use_global_device_ids=true | all-gather | bytes 8704 | tf_op jit(solution)/shard_map/all_gather | solution.py:15
  172.8 0.2 fusion.49
  173.0 19.2 %all-gather.1 = f32[128,16]{1,0:T(8,128)S(1)} all-gather(f32[8,16]{1,0:T(8,128)S(1)} %fusion.49), channel_id=3, replica_groups=mesh['kvseq'=16,'kvhead'=8,'section'=2] {'kvseq'}, dimensions={0}, use_global_device_ids=true | all-gather | bytes 8704 | tf_op jit(solution)/shard_map/all_gather | solution.py:15
  192.2 0.1 fusion.129
  192.4 6.5 all-gather.13.cloned.1.call-done
  198.9 0.8 slice.139
  199.8 1.3 slice.142
  201.0 2.4 while.42
  203.5 0.2 fusion.41
  203.7 2.8 fusion.13
  206.5 30.2 %psum.87 = f32[8,1024]{1,0:T(8,128)S(1)} all-reduce(f32[8,1024]{1,0:T(8,128)S(1)} %fusion.13), channel_id=1, replica_groups=mesh['kvseq'=16,'kvhead'=8,'section'=2] {'kvhead'}, use_global_device_ids=true, to_apply=%region_10.11 | all-reduce | flops 8192 | bytes 65536 | tf_op jit(solution)/shard_map/psum | solution.py:114
  236.8 1.3 collective-permute-start
  238.1 4.3 collective-permute-done
  242.4 0.1 fusion.72
  242.5 0.2 fusion.44
  242.7 3.5 fusion.17
  246.3 30.4 %all-reduce.1 = (f32[8]{0:T(128)S(1)}, f32[8,256]{1,0:T(8,128)S(1)}) all-reduce(f32[8]{0:T(128)S(1)} %get-tuple-element.199, f32[8,256]{1,0:T(8,128)S(1)} %fusion.44), channel_id=1, replica_groups=mesh['kvseq'=16,'kvhead'=8,'section'=2] {'kvseq'}, use_global_device_ids=true, to_apply=%region_13.14 | all-reduce | flops 2056 | bytes 16448 | tf_op jit(solution)/shard_map/psum | solution.py:100
  276.6 97.8 %all-reduce.9.cloned.1.call-done = f32[8,2048]{1,0:T(8,128)} async-done(((f32[8,2048]{1,0:T(8,128)}), f32[8,2048]{1,0:T(8,128)}) %all-reduce.9.cloned.1.call-update) | async-done | bytes 65552 | tf_op jit(solution)/shard_map/psum | solution.py:100
  374.4 0.9 fusion.78
  375.3 2.3 select_reduce_fusion.1
  377.7 2.7 fusion.23
  380.6 22.7 %all-gather.3 = f32[128,16]{1,0:T(8,128)S(1)} all-gather(f32[8,16]{1,0:T(8,128)S(1)} %get-tuple-element.209), channel_id=5, replica_groups=mesh['kvseq'=16,'kvhead'=8,'section'=2] {'kvseq'}, dimensions={0}, use_global_device_ids=true | all-gather | bytes 8704 | tf_op jit(solution)/shard_map/all_gather | solution.py:15
  403.3 0.2 fusion.51
  403.6 19.2 %all-gather.4 = f32[128,16]{1,0:T(8,128)S(1)} all-gather(f32[8,16]{1,0:T(8,128)S(1)} %fusion.51), channel_id=6, replica_groups=mesh['kvseq'=16,'kvhead'=8,'section'=2] {'kvseq'}, dimensions={0}, use_global_device_ids=true | all-gather | bytes 8704 | tf_op jit(solution)/shard_map/all_gather | solution.py:15
  422.8 0.1 fusion.130
  423.0 6.5 all-gather.15.cloned.1.call-done
  429.5 0.8 slice.147
  430.3 1.3 slice.150
  431.6 2.4 while.43
  434.0 0.2 fusion.40
  434.3 2.8 fusion.11
  437.1 30.2 %psum.91 = f32[8,1024]{1,0:T(8,128)S(1)} all-reduce(f32[8,1024]{1,0:T(8,128)S(1)} %fusion.11), channel_id=1, replica_groups=mesh['kvseq'=16,'kvhead'=8,'section'=2] {'kvhead'}, use_global_device_ids=true, to_apply=%region_21.22 | all-reduce | flops 8192 | bytes 65536 | tf_op jit(solution)/shard_map/psum | solution.py:114
  467.3 1.3 collective-permute-start.1
  468.6 4.3 collective-permute-done.1
  473.0 0.1 fusion.75
  473.1 0.2 fusion.42
  473.3 3.5 fusion.15
  476.8 30.4 %all-reduce = (f32[8]{0:T(128)S(1)}, f32[8,256]{1,0:T(8,128)S(1)}) all-reduce(f32[8]{0:T(128)S(1)} %get-tuple-element.193, f32[8,256]{1,0:T(8,128)S(1)} %fusion.42), channel_id=1, replica_groups=mesh['kvseq'=16,'kvhead'=8,'section'=2] {'kvseq'}, use_global_device_ids=true, to_apply=%region_24.25 | all-reduce | flops 2056 | bytes 16448 | tf_op jit(solution)/shard_map/psum | solution.py:100
  507.2 97.8 %all-reduce.11.cloned.1.call-done = f32[8,2048]{1,0:T(8,128)} async-done(((f32[8,2048]{1,0:T(8,128)}), f32[8,2048]{1,0:T(8,128)}) %all-reduce.11.cloned.1.call-update) | async-done | bytes 65552 | tf_op jit(solution)/shard_map/psum | solution.py:100
  605.0 0.9 fusion.79
  605.9 2.3 select_reduce_fusion
  608.2 2.7 fusion.21
  610.9 0.6 copy.116
  611.7 22.7 %all-gather.6 = f32[128,16]{1,0:T(8,128)S(1)} all-gather(f32[8,16]{1,0:T(8,128)S(1)} %get-tuple-element.213), channel_id=8, replica_groups=mesh['kvseq'=16,'kvhead'=8,'section'=2] {'kvseq'}, dimensions={0}, use_global_device_ids=true | all-gather | bytes 8704 | tf_op jit(solution)/shard_map/all_gather | solution.py:15
  634.4 0.2 fusion.53
  634.7 19.2 %all-gather.7 = f32[128,16]{1,0:T(8,128)S(1)} all-gather(f32[8,16]{1,0:T(8,128)S(1)} %fusion.53), channel_id=9, replica_groups=mesh['kvseq'=16,'kvhead'=8,'section'=2] {'kvseq'}, dimensions={0}, use_global_device_ids=true | all-gather | bytes 8704 | tf_op jit(solution)/shard_map/all_gather | solution.py:15
  653.9 0.1 fusion.131
  654.1 5.9 all-gather.17.cloned.1.call-done
  660.0 0.8 slice.155
  660.8 1.3 slice.158
  662.1 2.4 while.44
  664.6 0.2 fusion.39
  664.8 2.8 fusion.9
  667.6 30.2 %psum.95 = f32[8,1024]{1,0:T(8,128)S(1)} all-reduce(f32[8,1024]{1,0:T(8,128)S(1)} %fusion.9), channel_id=1, replica_groups=mesh['kvseq'=16,'kvhead'=8,'section'=2] {'kvhead'}, use_global_device_ids=true, to_apply=%region_32.33 | all-reduce | flops 8192 | bytes 65536 | tf_op jit(solution)/shard_map/psum | solution.py:114
  697.8 0.6 fusion.95
  (152 shorter events, 7.1 us)
Async XLA Ops:
  6.5 4.5 copy-start
  6.5 4.3 copy-start.1
  6.5 4.7 copy-start.2
  6.5 137.3 %all-reduce.7.cloned.1.call-start = ((), (), s32[]{:S(2)}) async-start(), calls=%async_computation | async-start | bytes 131072 | tf_op jit(solution)/shard_map/psum | solution.py:100
  10.8 188.1 %all-gather.13.cloned.1.call-start = ((), (), s32[]{:S(2)}) async-start(), calls=%async_computation.3 | async-start | bytes 1114112 | tf_op jit(solution)/shard_map/all_gather | solution.py:15
  149.8 224.6 %all-reduce.9.cloned.1.call-start = ((), (), s32[]{:S(2)}) async-start(), calls=%async_computation.1 | async-start | bytes 131072 | tf_op jit(solution)/shard_map/psum | solution.py:100
  236.8 5.6 collective-permute-start
  246.2 183.3 %all-gather.15.cloned.1.call-start = ((), (), s32[]{:S(2)}) async-start(), calls=%async_computation.4 | async-start | bytes 1114112 | tf_op jit(solution)/shard_map/all_gather | solution.py:15
  380.4 224.6 %all-reduce.11.cloned.1.call-start = ((), (), s32[]{:S(2)}) async-start(), calls=%async_computation.2 | async-start | bytes 131072 | tf_op jit(solution)/shard_map/psum | solution.py:100
  467.3 5.6 collective-permute-start.1
  476.8 183.2 %all-gather.17.cloned.1.call-start = ((), (), s32[]{:S(2)}) async-start(), calls=%async_computation.5 | async-start | bytes 1114112 | tf_op jit(solution)/shard_map/all_gather | solution.py:15
Sparse Core Ops, SparseCore 0:
  10.9 132.8 all-reduce.6
  149.9 48.9 all-gather.12
  246.3 128.0 all-reduce.8
  380.5 48.9 all-gather.14
  476.9 128.0 all-reduce.10
  611.0 48.9 all-gather.16
where the time goes:
time: 708 us; the launch traced here: 705 us
  waiting for transfers between devices  322 us (45%)
  blocking collectives  311 us (44%)
  matrix products  35.5 us (5%)
  between operations  13.8 us (2%)
  other arithmetic  11.7 us (2%)
  local copies, waits for them, and re-layouts  7.22 us (1%)
    psum x3, waiting for transfers between devices, per_device(): lax.psum((query_part, keyval_part, squares), 'kvseq')  295 us
    all_gather x6, blocking collectives, joined(): pieces = jax.tree.map(lambda part: lax.all_gather(part, axis), value)  126 us
    psum x3, blocking collectives, per_device(): lax.psum((query_part, keyval_part, squares), 'kvseq')  94.2 us
    psum x3, blocking collectives, per_device(): head_total = lax.psum(partial_out, 'kvhead')  90.6 us
    all_gather x3, waiting for transfers between devices, joined(): pieces = jax.tree.map(lambda part: lax.all_gather(part, axis), value)  18.9 us
  transfers between devices with their start and end apart: 8, of which 8 were waited for; matrix products, arithmetic and copies ran while one was open for 0% of the time, Pallas kernels for 0%

commit v1 on v0

v1 whole, which is shorter than its diff:
```python
import functools

import jax
import jax.numpy as jnp
from jax import lax
from jax.experimental import pallas as pl
from jax.experimental.pallas import tpu as pltpu
from jax.sharding import PartitionSpec as P

D = 16384
HEAD_DIM = 128
NEG_FLOOR = -1e30
EPSILON = 1e-05
F32 = jnp.float32
BF16 = jnp.bfloat16
VMEM = pl.BlockSpec(memory_space=pltpu.VMEM)
SMEM = pl.BlockSpec(memory_space=pltpu.SMEM)
HALF = 1024
WIDE = HALF + 2 * HEAD_DIM
ROWS = 16
STAT = 8


def kvseq_perm(value, move):
    pairs = []
    for source in range(16):
        x, y, core = move(source // 4, (source // 2) % 2, source % 2)
        pairs.append((source, (x % 4) * 4 + y * 2 + core))
    return lax.ppermute(value, "kvseq", pairs)


def other_core(value):
    return kvseq_perm(value, lambda x, y, c: (x, y, 1 - c))


def z_perm(value, even, odd):
    pairs = [(z, (z + (odd if z % 2 else even)) % 8) for z in range(8)]
    return lax.ppermute(value, "kvhead", pairs)


def z_section_perm(value, flip):
    pairs = [(z * 2 + s, (z ^ flip) * 2 + 1 - s) for z in range(8) for s in range(2)]
    return lax.ppermute(value, ("kvhead", "section"), pairs)


def over_chips(value, join):
    value = join(value, kvseq_perm(value, lambda x, y, c: (x ^ 1, y, c)))
    value = join(value, kvseq_perm(value, lambda x, y, c: (3 - x, y, c)))
    return join(value, kvseq_perm(value, lambda x, y, c: (x, 1 - y, c)))


def project_kernel(ids_ref, hidden_ref, gain_ref, query_ref, keyval_ref, out_ref):
    hidden = hidden_ref[...].astype(F32)
    scaled = (hidden * gain_ref[...].astype(F32)).astype(BF16)
    squares = jnp.sum(hidden * hidden, axis=-1, keepdims=True)
    core = ids_ref[1]
    for part in range(2):
        half = core if part == 0 else 1 - core
        columns = pl.ds(pl.multiple_of(half * HALF, HALF), HALF)
        out_ref[part, :, :HALF] = jnp.dot(scaled, query_ref[:, columns], preferred_element_type=F32)
        columns = pl.ds(pl.multiple_of(half * HEAD_DIM, HEAD_DIM), HEAD_DIM)
        out_ref[part, :, HALF : HALF + HEAD_DIM] = jnp.dot(
            scaled, keyval_ref[:, columns], preferred_element_type=F32
        )
        out_ref[part, :, HALF + HEAD_DIM :] = jnp.broadcast_to(squares, (ROWS, HEAD_DIM))


def attend_kernel(ids_ref, len_ref, own_ref, oth_ref, cache_ref, out_ref, q_s, acc_s, stat_s, kv_s):
    seq_id, core = ids_ref[0], ids_ref[1]
    for part, ref in enumerate((own_ref, oth_ref)):
        inv_rms = lax.rsqrt(ref[:, HALF + HEAD_DIM : HALF + HEAD_DIM + 1] / D + EPSILON)
        queries = ref[:, :HALF] * inv_rms * HEAD_DIM ** (-0.5)
        queries = queries.astype(BF16).astype(F32)
        for g in range(8):
            q_s[pl.ds((part * 8 + g) * ROWS, ROWS), :] = queries[:, g * HEAD_DIM : (g + 1) * HEAD_DIM]
        fresh = (ref[:, HALF : HALF + HEAD_DIM] * inv_rms).astype(BF16).astype(F32)
        kv_s[core if part == 0 else 1 - core] = fresh
    lane = lax.broadcasted_iota(jnp.int32, (32, HEAD_DIM), 1)
    position = seq_id * 1024 + lax.broadcasted_iota(jnp.int32, (32, 1024), 1)
    step = lax.broadcasted_iota(jnp.int32, (32, 1), 0) // 16
    holder = seq_id == 0
    for r in range(8):
        q32 = jnp.concatenate(
            [q_s[pl.ds(t * 8 + r, 16, stride=ROWS), :] for t in range(2)], axis=0
        )
        scores = lax.dot_general(
            q32.astype(BF16),
            cache_ref[r, :, :HEAD_DIM],
            (((1,), (1,)), ((), ())),
            preferred_element_type=F32,
        )
        valid = position < len_ref[r]
        top = jnp.max(jnp.where(valid, scores, NEG_FLOOR), axis=-1, keepdims=True)
        weights = jnp.where(valid, jnp.exp(scores - top), 0.0)
        total = jnp.sum(weights, axis=-1, keepdims=True)
        acc = jnp.dot(weights.astype(BF16), cache_ref[r, :, HEAD_DIM:], preferred_element_type=F32)
        fresh_scores = []
        new_top = top
        for s in range(2):
            key = kv_s[0, pl.ds(s * 8 + r, 1), :]
            score = jnp.sum(q32 * key, axis=-1, keepdims=True)
            seen = (step >= s) & holder
            score = jnp.where(seen, score, NEG_FLOOR)
            new_top = jnp.maximum(new_top, score)
            fresh_scores.append((seen, score))
        scale = jnp.exp(top - new_top)
        acc = acc * scale
        total = total * scale
        for s in range(2):
            seen, score = fresh_scores[s]
            weight = jnp.where(seen, jnp.exp(score - new_top), 0.0)
            acc = acc + weight * kv_s[1, pl.ds(s * 8 + r, 1), :]
            total = total + weight
        stats = jnp.where(lane == 0, new_top, jnp.where(lane == 1, total, 0.0))
        for t in range(2):
            acc_s[pl.ds(t * 8 + r, 16, stride=ROWS), :] = acc[t * 16 : (t + 1) * 16]
            stat_s[pl.ds(t * 8 + r, 16, stride=ROWS), :] = stats[t * 16 : (t + 1) * 16]
    for part in range(2):
        rows = pl.ds(part * 128, 128)
        out_ref[part, :HEAD_DIM, :] = acc_s[rows, :].T
        out_ref[part, HEAD_DIM:, :] = stat_s[rows, :].T[:STAT]


def output_kernel(ids_ref, own_ref, oth_ref, w_ref, out_ref):
    core = ids_ref[1]
    result = None
    for part, ref in enumerate((own_ref, oth_ref)):
        half = core if part == 0 else 1 - core
        attended = (ref[:HEAD_DIM, :] / ref[HEAD_DIM + 1 : HEAD_DIM + 2, :]).T.astype(BF16)
        attended = jnp.concatenate([attended[g * ROWS : (g + 1) * ROWS] for g in range(8)], axis=1)
        rows = pl.ds(pl.multiple_of(half * HALF, HALF), HALF)
        term = jnp.dot(attended, w_ref[rows, :], preferred_element_type=F32)
        result = term if result is None else result + term
    out_ref[...] = result


def merge(left, right):
    left_max, right_max = left[HEAD_DIM : HEAD_DIM + 1], right[HEAD_DIM : HEAD_DIM + 1]
    top = jnp.maximum(left_max, right_max)
    left_scale, right_scale = jnp.exp(left_max - top), jnp.exp(right_max - top)
    row = lax.broadcasted_iota(jnp.int32, left.shape, 0)
    return jnp.where(row == HEAD_DIM, top, left * left_scale + right * right_scale)


def in_vmem(value):
    return pltpu.with_memory_space_constraint(value, pltpu.VMEM)


def per_device(hidden_in, lengths, norm_gain, w_query, w_keyval, w_out, kv_cache):
    section_id = lax.axis_index("section")
    seq_id = lax.axis_index("kvseq")
    core = seq_id % 2
    ids = jnp.stack([seq_id, core]).astype(jnp.int32)
    width = hidden_in.shape[2]
    w_query, w_keyval = in_vmem(w_query[0]), in_vmem(w_keyval[0, :, 0, :])
    w_out, cache = in_vmem(w_out[0]), in_vmem(kv_cache[0, 0])
    params = pltpu.CompilerParams(vmem_limit_bytes=24 * 2**20)

    def partial_layer(hidden):
        halves = pl.pallas_call(
            project_kernel,
            out_shape=jax.ShapeDtypeStruct((2, ROWS, WIDE), F32),
            in_specs=[SMEM] + [VMEM] * 4,
            out_specs=VMEM,
            compiler_params=params,
            name="project",
        )(ids, hidden, norm_gain, w_query, w_keyval)
        own = halves[0] + other_core(halves[1])
        own = over_chips(own, lambda a, b: a + b)
        oth = other_core(own)
        parts = pl.pallas_call(
            attend_kernel,
            out_shape=jax.ShapeDtypeStruct((2, HEAD_DIM + STAT, HEAD_DIM), F32),
            in_specs=[SMEM, SMEM] + [VMEM] * 3,
            out_specs=VMEM,
            scratch_shapes=[
                pltpu.VMEM((256, HEAD_DIM), F32),
                pltpu.VMEM((256, HEAD_DIM), F32),
                pltpu.VMEM((256, HEAD_DIM), F32),
                pltpu.VMEM((2, ROWS, HEAD_DIM), F32),
            ],
            compiler_params=params,
            name="attend",
        )(ids, lengths, own, oth, cache)
        own = merge(parts[0], other_core(parts[1]))
        own = over_chips(own, merge)
        oth = other_core(own)
        return pl.pallas_call(
            output_kernel,
            out_shape=jax.ShapeDtypeStruct((ROWS, width), F32),
            in_specs=[SMEM] + [VMEM] * 3,
            out_specs=VMEM,
            compiler_params=params,
            name="output",
        )(ids, own, oth, w_out)

    def over_heads(pair):
        near, far, opposite = z_perm(pair, -1, 1), z_perm(pair, -2, 2), z_perm(pair, -3, 3)
        return (pair + opposite) + (near + far)

    hidden = hidden_in.reshape(ROWS, width)
    partial = partial_layer(hidden)
    pair = z_section_perm(partial, 0) + z_section_perm(partial, 1)
    hidden = (hidden.astype(F32) + over_heads(pair)).astype(BF16)
    first = lax.ppermute(hidden, "section", [(0, 1), (1, 0)])
    partial = partial_layer(hidden)
    pair = partial + lax.ppermute(partial, "kvhead", [(z, z ^ 1) for z in range(8)])
    second = (hidden.astype(F32) + over_heads(pair)).astype(BF16)
    result = jnp.where(section_id == 0, first, second)
    return result.reshape(hidden_in.shape)[None]


def solution(mesh):
    placed = (
        P(None, None, "kvseq"),
        P(),
        P("section", "kvseq"),
        P("section", "kvseq", "kvhead"),
        P("section", "kvseq", "kvhead", None),
        P("section", "kvhead", "kvseq"),
        P("section", "kvhead", None, "kvseq", None),
    )
    return jax.shard_map(
        per_device,
        mesh=mesh,
        in_specs=placed,
        out_specs=P("section", None, None, "kvseq"),
        check_vma=False,
    )
```

time: 708 us -> 129 us (0.18)
  blocking collectives: 311 us -> 0 us
  waiting for transfers between devices: 322 us -> 69.6 us
  starting transfers between devices: 2.8 us -> 39.9 us
  matrix products: 35.5 us -> 0 us
  between operations: 13.8 us -> 0.28 us
  Pallas kernels: 0 us -> 11.9 us
  other arithmetic: 11.7 us -> 1.65 us
    psum x3 -> x0, waiting for transfers between devices: 295 us -> none  [per_device(): lax.psum((query_part, keyval_part, squares), 'kvseq')]
    psum x6 -> x0, blocking collectives: 185 us -> none  [the longest x3 94.2 us: per_device(): lax.psum((query_part, keyval_part, squares), 'kvseq')]
    all_gather x6 -> x0, blocking collectives: 126 us -> none  [joined(): pieces = jax.tree.map(lambda part: lax.all_gather(part, axis), value)]
    ppermute x2 -> x30, waiting for transfers between devices: 8.67 us -> 69.6 us  [the longest x20 56.1 us: kvseq_perm(): return lax.ppermute(value, 'kvseq', pairs)]
    ppermute x2 -> x30, starting transfers between devices: 2.58 us -> 39.9 us  [the longest x20 19.4 us: kvseq_perm(): return lax.ppermute(value, 'kvseq', pairs)]
    dot_general x21 -> x0, matrix products: 35.5 us -> none  [the longest x3 10.4 us: per_device(): query_part = jnp.dot(scaled, query_mat, preferred_element_type=jnp.float32)]
    all_gather x3 -> x0, waiting for transfers between devices: 18.9 us -> none  [joined(): pieces = jax.tree.map(lambda part: lax.all_gather(part, axis), value)]
    pallas_call x0 -> x6, Pallas kernels: none -> 11.9 us  [the longest x2 6.9 us: partial_layer(): pl.pallas_call(attend_kernel, out_shape=jax.ShapeDtypeStruct((2, HEAD_DIM...]
  transfers between devices with their start and end apart: 8 -> 30, of which waited for: 8 -> 28; matrix products, arithmetic and copies ran while one was open for 0% -> 0% of each run, Pallas kernels for 0% -> 0%
where the time goes in v1:
time: 129 us; the launch traced here: 128 us
  waiting for transfers between devices  69.6 us (54%)
  starting transfers between devices  39.9 us (31%)
  Pallas kernels  11.9 us (9%)
  local copies, waits for them, and re-layouts  5.01 us (4%)
  other arithmetic  1.65 us (1%)
    ppermute x20, waiting for transfers between devices, kvseq_perm(): return lax.ppermute(value, 'kvseq', pairs)  56.1 us
    ppermute x20, starting transfers between devices, kvseq_perm(): return lax.ppermute(value, 'kvseq', pairs)  19.4 us
    ppermute x6, starting transfers between devices, z_perm(): return lax.ppermute(value, 'kvhead', pairs)  13.2 us
    pallas_call x2, Pallas kernels, partial_layer(): pl.pallas_call(attend_kernel, out_shape=jax.ShapeDtypeStruct((2, HEAD_DIM...  6.9 us
    ppermute x6, waiting for transfers between devices, z_perm(): return lax.ppermute(value, 'kvhead', pairs)  5.92 us
    unnamed x20, local copies, waits for them, and re-layouts  4.97 us
    ppermute x2, starting transfers between devices, z_section_perm(): return lax.ppermute(value, ('kvhead', 'section'), pairs)  3.39 us
    ppermute x1, waiting for transfers between devices, per_device(): first = lax.ppermute(hidden, 'section', [(0, 1), (1, 0)])  2.63 us
  transfers between devices with their start and end apart: 30, of which 28 were waited for; matrix products, arithmetic and copies ran while one was open for 0% of the time, Pallas kernels for 0%

profile of v1, /device:TPU:24, one launch (start us, length us, event | category | flops | bytes accessed | tf_op | source)
XLA Modules:
  0.0 128.3 jit_solution(2374945090503378708)
XLA Ops:
  0.1 2.3 %copy-done.1 = bf16[1,1024,2048]{2,1,0:T(8,128)(2,1)S(1)} copy-done((bf16[1,1024,2048]{2,1,0:T(8,128)(2,1)S(1)}, bf16[1,1024,2048]{2,1,0:T(8,128)(2,1)}, u32[]{:S(2)}) %copy-start.1) | copy-done | bytes 4194328
  2.4 1.2 copy-done.4
  3.6 0.8 copy-done.6
  4.3 0.7 copy-done.8
  5.0 1.3 project.2
  6.4 1.3 collective-permute-done
  7.7 1.6 %collective-permute-start.1 = (f32[16,1280]{1,0:T(8,128)S(1)}, f32[16,1280]{1,0:T(8,128)S(1)}, u32[]{:S(2)}, u32[]{:S(2)}) collective-permute-start(f32[16,1280]{1,0:T(8,128)S(1)} %fusion.1), channel_id=1, source_target_pairs={{0,64},{16,80},{32,96},{48,112},{64,0},{80,16},{96,32},{112,48},{1... | collective-permute-start | bytes 245768 | tf_op jit(solution)/shard_map/ppermute | solution.py:29
  9.3 3.0 %collective-permute-done.1 = f32[16,1280]{1,0:T(8,128)S(1)} collective-permute-done((f32[16,1280]{1,0:T(8,128)S(1)}, f32[16,1280]{1,0:T(8,128)S(1)}, u32[]{:S(2)}, u32[]{:S(2)}) %collective-permute-start.1) | collective-permute-done | bytes 81952 | tf_op jit(solution)/shard_map/ppermute | solution.py:29
  12.3 2.8 %collective-permute-start.2 = (f32[16,1280]{1,0:T(8,128)S(1)}, f32[16,1280]{1,0:T(8,128)S(1)}, u32[]{:S(2)}, u32[]{:S(2)}) collective-permute-start(f32[16,1280]{1,0:T(8,128)S(1)} %add.84), channel_id=1, source_target_pairs={{0,192},{16,208},{32,224},{48,240},{64,128},{80,144},{96,160},{112... | collective-permute-start | bytes 245768 | tf_op jit(solution)/shard_map/ppermute | solution.py:29
  15.1 2.9 %collective-permute-done.2 = f32[16,1280]{1,0:T(8,128)S(1)} collective-permute-done((f32[16,1280]{1,0:T(8,128)S(1)}, f32[16,1280]{1,0:T(8,128)S(1)}, u32[]{:S(2)}, u32[]{:S(2)}) %collective-permute-start.2) | collective-permute-done | bytes 81952 | tf_op jit(solution)/shard_map/ppermute | solution.py:29
  18.1 1.3 %collective-permute-start.3 = (f32[16,1280]{1,0:T(8,128)S(1)}, f32[16,1280]{1,0:T(8,128)S(1)}, u32[]{:S(2)}, u32[]{:S(2)}) collective-permute-start(f32[16,1280]{1,0:T(8,128)S(1)} %add.85), channel_id=1, source_target_pairs={{0,32},{16,48},{32,0},{48,16},{64,96},{80,112},{96,64},{112,80},{1... | collective-permute-start | bytes 245768 | tf_op jit(solution)/shard_map/ppermute | solution.py:29
  19.4 4.7 %collective-permute-done.3 = f32[16,1280]{1,0:T(8,128)S(1)} collective-permute-done((f32[16,1280]{1,0:T(8,128)S(1)}, f32[16,1280]{1,0:T(8,128)S(1)}, u32[]{:S(2)}, u32[]{:S(2)}) %collective-permute-start.3) | collective-permute-done | bytes 81952 | tf_op jit(solution)/shard_map/ppermute | solution.py:29
  24.2 1.3 collective-permute-done.4.oth_ref
  25.5 3.4 %attend.2 = f32[2,136,128]{2,1,0:T(8,128)S(1)} custom-call(s32[2]{0:T(128)S(1)} %pad_add_fusion.ids_ref, s32[8]{0:T(128)S(1)} %copy-done.9, f32[16,1280]{1,0:T(8,128)S(1)} %add.86.own_ref, f32[16,1280]{1,0:T(8,128)S(1)} %collective-permute-done.4.oth_ref, bf16[8,1024,256]{2,1,0:T(8,128)(2,1)S(1)} %bitcast.114), custom_call_target="tpu_custom_call" | custom-call | tf_op jit(solution)/shard_map/attend/pallas_call | solution.py:171
  29.0 0.2 collective-permute-start.5
  29.2 1.1 collective-permute-done.5
  30.3 0.1 fusion.7
  30.4 0.4 collective-permute-start.6
  30.8 4.0 %collective-permute-done.6 = f32[136,128]{1,0:T(8,128)S(1)} collective-permute-done((f32[136,128]{1,0:T(8,128)S(1)}, f32[136,128]{1,0:T(8,128)S(1)}, u32[]{:S(2)}, u32[]{:S(2)}) %collective-permute-start.6) | collective-permute-done | bytes 69664 | tf_op jit(solution)/shard_map/ppermute | solution.py:29
  34.9 2.8 %collective-permute-start.7 = (f32[136,128]{1,0:T(8,128)S(1)}, f32[136,128]{1,0:T(8,128)S(1)}, u32[]{:S(2)}, u32[]{:S(2)}) collective-permute-start(f32[136,128]{1,0:T(8,128)S(1)} %add_select_fusion.5), channel_id=1, source_target_pairs={{0,192},{16,208},{32,224},{48,240},{64,128},{80,144},{96,160},{112... | collective-permute-start | bytes 208904 | tf_op jit(solution)/shard_map/ppermute | solution.py:29
  37.8 2.8 %collective-permute-done.7 = f32[136,128]{1,0:T(8,128)S(1)} collective-permute-done((f32[136,128]{1,0:T(8,128)S(1)}, f32[136,128]{1,0:T(8,128)S(1)}, u32[]{:S(2)}, u32[]{:S(2)}) %collective-permute-start.7) | collective-permute-done | bytes 69664 | tf_op jit(solution)/shard_map/ppermute | solution.py:29
  40.6 1.3 %collective-permute-start.8 = (f32[136,128]{1,0:T(8,128)S(1)}, f32[136,128]{1,0:T(8,128)S(1)}, u32[]{:S(2)}, u32[]{:S(2)}) collective-permute-start(f32[136,128]{1,0:T(8,128)S(1)} %add_select_fusion.4), channel_id=1, source_target_pairs={{0,32},{16,48},{32,0},{48,16},{64,96},{80,112},{96,64},{112,80},{1... | collective-permute-start | bytes 208904 | tf_op jit(solution)/shard_map/ppermute | solution.py:29
  42.0 4.6 %collective-permute-done.8 = f32[136,128]{1,0:T(8,128)S(1)} collective-permute-done((f32[136,128]{1,0:T(8,128)S(1)}, f32[136,128]{1,0:T(8,128)S(1)}, u32[]{:S(2)}, u32[]{:S(2)}) %collective-permute-start.8) | collective-permute-done | bytes 69664 | tf_op jit(solution)/shard_map/ppermute | solution.py:29
  46.8 1.2 collective-permute-done.9.oth_ref
  48.0 1.2 output.2
  49.2 0.8 collective-permute-start.10
  50.0 2.6 %collective-permute-start.11 = (f32[16,1024]{1,0:T(8,128)S(1)}, f32[16,1024]{1,0:T(8,128)S(1)}, u32[]{:S(2)}, u32[]{:S(2)}) collective-permute-start(f32[16,1024]{1,0:T(8,128)S(1)} %output.2), channel_id=1, source_target_pairs={{0,3},{1,2},{2,1},{3,0},{4,7},{5,6},{6,5},{7,4},{8,11},{9,10},{10,... | collective-permute-start | bytes 196616 | tf_op jit(solution)/shard_map/ppermute | solution.py:43
  52.6 1.6 %collective-permute-done.10 = f32[16,1024]{1,0:T(8,128)S(1)} collective-permute-done((f32[16,1024]{1,0:T(8,128)S(1)}, f32[16,1024]{1,0:T(8,128)S(1)}, u32[]{:S(2)}, u32[]{:S(2)}) %collective-permute-start.10) | collective-permute-done | bytes 65568 | tf_op jit(solution)/shard_map/ppermute | solution.py:43
  54.2 0.9 collective-permute-done.11
  55.2 6.8 %collective-permute-start.12 = (f32[16,1024]{1,0:T(8,128)S(1)}, f32[16,1024]{1,0:T(8,128)S(1)}, u32[]{:S(2)}, u32[]{:S(2)}) collective-permute-start(f32[16,1024]{1,0:T(8,128)S(1)} %add.91), channel_id=1, source_target_pairs={{0,10},{2,8},{4,14},{6,12},{8,2},{10,0},{12,6},{14,4},{1,11},{3,9}... | collective-permute-start | bytes 196616 | tf_op jit(solution)/shard_map/ppermute | solution.py:38
  62.0 0.7 collective-permute-start.14
  62.7 1.9 %collective-permute-done.12 = f32[16,1024]{1,0:T(8,128)S(1)} collective-permute-done((f32[16,1024]{1,0:T(8,128)S(1)}, f32[16,1024]{1,0:T(8,128)S(1)}, u32[]{:S(2)}, u32[]{:S(2)}) %collective-permute-start.12) | collective-permute-done | bytes 65568 | tf_op jit(solution)/shard_map/ppermute | solution.py:38
  64.6 2.9 %collective-permute-done.13 = f32[16,1024]{1,0:T(8,128)S(1)} collective-permute-done((f32[16,1024]{1,0:T(8,128)S(1)}, f32[16,1024]{1,0:T(8,128)S(1)}, u32[]{:S(2)}, u32[]{:S(2)}) %collective-permute-start.13) | collective-permute-done | bytes 65568 | tf_op jit(solution)/shard_map/ppermute | solution.py:38
  67.5 0.3 collective-permute-done.14
  67.9 1.3 project.3
  69.2 0.3 collective-permute-start.16
  69.4 1.3 collective-permute-done.16
  70.8 4.5 %collective-permute-done.17 = f32[16,1280]{1,0:T(8,128)S(1)} collective-permute-done((f32[16,1280]{1,0:T(8,128)S(1)}, f32[16,1280]{1,0:T(8,128)S(1)}, u32[]{:S(2)}, u32[]{:S(2)}) %collective-permute-start.17) | collective-permute-done | bytes 81952 | tf_op jit(solution)/shard_map/ppermute | solution.py:29
  75.3 2.8 %collective-permute-start.18 = (f32[16,1280]{1,0:T(8,128)S(1)}, f32[16,1280]{1,0:T(8,128)S(1)}, u32[]{:S(2)}, u32[]{:S(2)}) collective-permute-start(f32[16,1280]{1,0:T(8,128)S(1)} %add.97), channel_id=1, source_target_pairs={{0,192},{16,208},{32,224},{48,240},{64,128},{80,144},{96,160},{112... | collective-permute-start | bytes 245768 | tf_op jit(solution)/shard_map/ppermute | solution.py:29
  78.2 2.9 %collective-permute-done.18 = f32[16,1280]{1,0:T(8,128)S(1)} collective-permute-done((f32[16,1280]{1,0:T(8,128)S(1)}, f32[16,1280]{1,0:T(8,128)S(1)}, u32[]{:S(2)}, u32[]{:S(2)}) %collective-permute-start.18) | collective-permute-done | bytes 81952 | tf_op jit(solution)/shard_map/ppermute | solution.py:29
  81.1 1.0 collective-permute-start.19
  82.1 5.0 %collective-permute-done.19 = f32[16,1280]{1,0:T(8,128)S(1)} collective-permute-done((f32[16,1280]{1,0:T(8,128)S(1)}, f32[16,1280]{1,0:T(8,128)S(1)}, u32[]{:S(2)}, u32[]{:S(2)}) %collective-permute-start.19) | collective-permute-done | bytes 81952 | tf_op jit(solution)/shard_map/ppermute | solution.py:29
  87.2 1.3 collective-permute-done.20.oth_ref
  88.5 3.4 %attend.3 = f32[2,136,128]{2,1,0:T(8,128)S(1)} custom-call(s32[2]{0:T(128)S(1)} %pad_add_fusion.ids_ref, s32[8]{0:T(128)S(1)} %copy-done.9, f32[16,1280]{1,0:T(8,128)S(1)} %add.99.own_ref, f32[16,1280]{1,0:T(8,128)S(1)} %collective-permute-done.20.oth_ref, bf16[8,1024,256]{2,1,0:T(8,128)(2,1)S(1)} %bitcast.115), custom_call_target="tpu_custom_call" | custom-call | tf_op jit(solution)/shard_map/attend/pallas_call | solution.py:171
  92.0 0.2 collective-permute-start.21
  92.2 1.1 collective-permute-done.21
  93.5 4.3 %collective-permute-done.22 = f32[136,128]{1,0:T(8,128)S(1)} collective-permute-done((f32[136,128]{1,0:T(8,128)S(1)}, f32[136,128]{1,0:T(8,128)S(1)}, u32[]{:S(2)}, u32[]{:S(2)}) %collective-permute-start.22) | collective-permute-done | bytes 69664 | tf_op jit(solution)/shard_map/ppermute | solution.py:29
  97.9 2.8 %collective-permute-start.23 = (f32[136,128]{1,0:T(8,128)S(1)}, f32[136,128]{1,0:T(8,128)S(1)}, u32[]{:S(2)}, u32[]{:S(2)}) collective-permute-start(f32[136,128]{1,0:T(8,128)S(1)} %add_select_fusion.2), channel_id=1, source_target_pairs={{0,192},{16,208},{32,224},{48,240},{64,128},{80,144},{96,160},{112... | collective-permute-start | bytes 208904 | tf_op jit(solution)/shard_map/ppermute | solution.py:29
  100.8 2.8 %collective-permute-done.23 = f32[136,128]{1,0:T(8,128)S(1)} collective-permute-done((f32[136,128]{1,0:T(8,128)S(1)}, f32[136,128]{1,0:T(8,128)S(1)}, u32[]{:S(2)}, u32[]{:S(2)}) %collective-permute-start.23) | collective-permute-done | bytes 69664 | tf_op jit(solution)/shard_map/ppermute | solution.py:29
  103.5 0.1 add_select_fusion.1
  103.6 1.0 collective-permute-start.24
  104.7 4.9 %collective-permute-done.24 = f32[136,128]{1,0:T(8,128)S(1)} collective-permute-done((f32[136,128]{1,0:T(8,128)S(1)}, f32[136,128]{1,0:T(8,128)S(1)}, u32[]{:S(2)}, u32[]{:S(2)}) %collective-permute-start.24) | collective-permute-done | bytes 69664 | tf_op jit(solution)/shard_map/ppermute | solution.py:29
  109.5 0.1 add_select_fusion.own_ref
  109.7 1.2 collective-permute-done.25.oth_ref
  111.0 1.2 output.3
  112.2 2.6 %collective-permute-start.26 = (f32[16,1024]{1,0:T(8,128)S(1)}, f32[16,1024]{1,0:T(8,128)S(1)}, u32[]{:S(2)}, u32[]{:S(2)}) collective-permute-start(f32[16,1024]{1,0:T(8,128)S(1)} %output.3), channel_id=1, source_target_pairs={{0,2},{2,0},{4,6},{6,4},{8,10},{10,8},{12,14},{14,12},{1,3},{3,1},... | collective-permute-start | bytes 196616 | tf_op jit(solution)/shard_map/ppermute | solution.py:207
  114.8 2.4 %collective-permute-done.26 = f32[16,1024]{1,0:T(8,128)S(1)} collective-permute-done((f32[16,1024]{1,0:T(8,128)S(1)}, f32[16,1024]{1,0:T(8,128)S(1)}, u32[]{:S(2)}, u32[]{:S(2)}) %collective-permute-start.26) | collective-permute-done | bytes 65568 | tf_op jit(solution)/shard_map/ppermute | solution.py:207
  117.3 3.1 %collective-permute-start.27 = (f32[16,1024]{1,0:T(8,128)S(1)}, f32[16,1024]{1,0:T(8,128)S(1)}, u32[]{:S(2)}, u32[]{:S(2)}) collective-permute-start(f32[16,1024]{1,0:T(8,128)S(1)} %add.104), channel_id=1, source_target_pairs={{0,10},{2,8},{4,14},{6,12},{8,2},{10,0},{12,6},{14,4},{1,11},{3,9}... | collective-permute-start | bytes 196616 | tf_op jit(solution)/shard_map/ppermute | solution.py:38
  120.4 1.9 %collective-permute-start.28 = (f32[16,1024]{1,0:T(8,128)S(1)}, f32[16,1024]{1,0:T(8,128)S(1)}, u32[]{:S(2)}, u32[]{:S(2)}) collective-permute-start(f32[16,1024]{1,0:T(8,128)S(1)} %add.104), channel_id=1, source_target_pairs={{0,14},{2,4},{4,2},{6,8},{8,6},{10,12},{12,10},{14,0},{1,15},{3,5}... | collective-permute-start | bytes 196616 | tf_op jit(solution)/shard_map/ppermute | solution.py:38
  122.3 0.6 collective-permute-start.29
  122.9 1.3 collective-permute-start.15
  124.2 2.6 %collective-permute-done.15 = bf16[16,1024]{1,0:T(8,128)(2,1)S(1)} collective-permute-done((bf16[16,1024]{1,0:T(8,128)(2,1)S(1)}, bf16[16,1024]{1,0:T(8,128)(2,1)S(1)}, u32[]{:S(2)}, u32[]{:S(2)}) %collective-permute-start.15) | collective-permute-done | bytes 32800 | tf_op jit(solution)/shard_map/ppermute | solution.py:205
  126.9 0.8 collective-permute-done.29
  127.6 0.6 fusion.9
  (56 shorter events, 1.5 us)
Async XLA Ops:
  0.0 25.5 %copy-start.9 = (s32[8]{0:T(128)S(1)}, s32[8]{0:T(128)}, u32[]{:S(2)}) copy-start(s32[8]{0:T(128)} %len_ref.3) | copy-start | bytes 100
  0.0 25.5 %copy-start = (bf16[1,1,8,1024,256]{4,3,2,1,0:T(8,128)(2,1)S(1)}, bf16[1,1,8,1024,256]{4,3,2,1,0:T(8,128)(2,1)}, u32[]{:S(2)}) copy-start(bf16[1,1,8,1024,256]{4,3,2,1,0:T(8,128)(2,1)} %param.13) | copy-start | bytes 12582916
  0.1 2.3 %copy-start.1 = (bf16[1,1024,2048]{2,1,0:T(8,128)(2,1)S(1)}, bf16[1,1024,2048]{2,1,0:T(8,128)(2,1)}, u32[]{:S(2)}) copy-start(bf16[1,1024,2048]{2,1,0:T(8,128)(2,1)} %param.10) | copy-start | bytes 12582916
  2.4 1.2 copy-start.4
  3.6 0.8 copy-start.6
  4.3 0.7 copy-start.8
  6.3 41.7 %copy-start.3 = (bf16[1,2048,1024]{2,1,0:T(8,128)(2,1)S(1)}, bf16[1,2048,1024]{2,1,0:T(8,128)(2,1)}, u32[]{:S(2)}) copy-start(bf16[1,2048,1024]{2,1,0:T(8,128)(2,1)} %param.12) | copy-start | bytes 12582916
  6.3 1.4 %collective-permute-start = (f32[16,1280]{1,0:T(8,128)S(1)}, f32[16,1280]{1,0:T(8,128)S(1)}, u32[]{:S(2)}, u32[]{:S(2)}) collective-permute-start(f32[16,1280]{1,0:T(8,128)S(1)} %slice_bitcast_fusion.2), channel_id=1, source_target_pairs={{0,16},{16,0},{32,48},{48,32},{64,80},{80,64},{96,112},{112,96},{1... | collective-permute-start | bytes 245768 | tf_op jit(solution)/shard_map/ppermute | solution.py:29
  7.7 4.6 %collective-permute-start.1 = (f32[16,1280]{1,0:T(8,128)S(1)}, f32[16,1280]{1,0:T(8,128)S(1)}, u32[]{:S(2)}, u32[]{:S(2)}) collective-permute-start(f32[16,1280]{1,0:T(8,128)S(1)} %fusion.1), channel_id=1, source_target_pairs={{0,64},{16,80},{32,96},{48,112},{64,0},{80,16},{96,32},{112,48},{1... | collective-permute-start | bytes 245768 | tf_op jit(solution)/shard_map/ppermute | solution.py:29
  12.3 5.7 %collective-permute-start.2 = (f32[16,1280]{1,0:T(8,128)S(1)}, f32[16,1280]{1,0:T(8,128)S(1)}, u32[]{:S(2)}, u32[]{:S(2)}) collective-permute-start(f32[16,1280]{1,0:T(8,128)S(1)} %add.84), channel_id=1, source_target_pairs={{0,192},{16,208},{32,224},{48,240},{64,128},{80,144},{96,160},{112... | collective-permute-start | bytes 245768 | tf_op jit(solution)/shard_map/ppermute | solution.py:29
  18.1 6.0 %collective-permute-start.3 = (f32[16,1280]{1,0:T(8,128)S(1)}, f32[16,1280]{1,0:T(8,128)S(1)}, u32[]{:S(2)}, u32[]{:S(2)}) collective-permute-start(f32[16,1280]{1,0:T(8,128)S(1)} %add.85), channel_id=1, source_target_pairs={{0,32},{16,48},{32,0},{48,16},{64,96},{80,112},{96,64},{112,80},{1... | collective-permute-start | bytes 245768 | tf_op jit(solution)/shard_map/ppermute | solution.py:29
  24.1 1.4 %collective-permute-start.4 = (f32[16,1280]{1,0:T(8,128)S(1)}, f32[16,1280]{1,0:T(8,128)S(1)}, u32[]{:S(2)}, u32[]{:S(2)}) collective-permute-start(f32[16,1280]{1,0:T(8,128)S(1)} %add.86.own_ref), channel_id=1, source_target_pairs={{0,16},{16,0},{32,48},{48,32},{64,80},{80,64},{96,112},{112,96},{1... | collective-permute-start | bytes 245768 | tf_op jit(solution)/shard_map/ppermute | solution.py:29
  25.5 42.4 %copy-start.7 = (bf16[2,8,1024]{2,1,0:T(8,128)(2,1)S(1)}, bf16[2,8,1024]{2,1,0:T(8,128)(2,1)}, u32[]{:S(2)}) copy-start(bf16[2,8,1024]{2,1,0:T(8,128)(2,1)} %param.7) | copy-start | bytes 98308
  25.5 42.4 %copy-start.2 = (bf16[1,1024,2048]{2,1,0:T(8,128)(2,1)S(1)}, bf16[1,1024,2048]{2,1,0:T(8,128)(2,1)}, u32[]{:S(2)}) copy-start(bf16[1,1024,2048]{2,1,0:T(8,128)(2,1)} %param.10) | copy-start | bytes 12582916
  25.5 42.4 %copy-start.5 = (bf16[1,1024,1,256]{3,1,2,0:T(8,128)(2,1)S(1)}, bf16[1,1024,1,256]{3,1,2,0:T(8,128)(2,1)}, u32[]{:S(2)}) copy-start(bf16[1,1024,1,256]{3,1,2,0:T(8,128)(2,1)} %param.11) | copy-start | bytes 1572868
  29.0 1.3 %collective-permute-start.5 = (f32[136,128]{1,0:T(8,128)S(1)}, f32[136,128]{1,0:T(8,128)S(1)}, u32[]{:S(2)}, u32[]{:S(2)}) collective-permute-start(f32[136,128]{1,0:T(8,128)S(1)} %slice_bitcast_fusion.7), channel_id=1, source_target_pairs={{0,16},{16,0},{32,48},{48,32},{64,80},{80,64},{96,112},{112,96},{1... | collective-permute-start | bytes 208904 | tf_op jit(solution)/shard_map/ppermute | solution.py:29
  30.4 4.4 %collective-permute-start.6 = (f32[136,128]{1,0:T(8,128)S(1)}, f32[136,128]{1,0:T(8,128)S(1)}, u32[]{:S(2)}, u32[]{:S(2)}) collective-permute-start(f32[136,128]{1,0:T(8,128)S(1)} %fusion.7), channel_id=1, source_target_pairs={{0,64},{16,80},{32,96},{48,112},{64,0},{80,16},{96,32},{112,48},{1... | collective-permute-start | bytes 208904 | tf_op jit(solution)/shard_map/ppermute | solution.py:29
  34.9 5.6 %collective-permute-start.7 = (f32[136,128]{1,0:T(8,128)S(1)}, f32[136,128]{1,0:T(8,128)S(1)}, u32[]{:S(2)}, u32[]{:S(2)}) collective-permute-start(f32[136,128]{1,0:T(8,128)S(1)} %add_select_fusion.5), channel_id=1, source_target_pairs={{0,192},{16,208},{32,224},{48,240},{64,128},{80,144},{96,160},{112... | collective-permute-start | bytes 208904 | tf_op jit(solution)/shard_map/ppermute | solution.py:29
  40.6 5.9 %collective-permute-start.8 = (f32[136,128]{1,0:T(8,128)S(1)}, f32[136,128]{1,0:T(8,128)S(1)}, u32[]{:S(2)}, u32[]{:S(2)}) collective-permute-start(f32[136,128]{1,0:T(8,128)S(1)} %add_select_fusion.4), channel_id=1, source_target_pairs={{0,32},{16,48},{32,0},{48,16},{64,96},{80,112},{96,64},{112,80},{1... | collective-permute-start | bytes 208904 | tf_op jit(solution)/shard_map/ppermute | solution.py:29
  46.7 1.3 %collective-permute-start.9 = (f32[136,128]{1,0:T(8,128)S(1)}, f32[136,128]{1,0:T(8,128)S(1)}, u32[]{:S(2)}, u32[]{:S(2)}) collective-permute-start(f32[136,128]{1,0:T(8,128)S(1)} %add_select_fusion.3.own_ref), channel_id=1, source_target_pairs={{0,16},{16,0},{32,48},{48,32},{64,80},{80,64},{96,112},{112,96},{1... | collective-permute-start | bytes 208904 | tf_op jit(solution)/shard_map/ppermute | solution.py:29
  49.2 5.0 %collective-permute-start.10 = (f32[16,1024]{1,0:T(8,128)S(1)}, f32[16,1024]{1,0:T(8,128)S(1)}, u32[]{:S(2)}, u32[]{:S(2)}) collective-permute-start(f32[16,1024]{1,0:T(8,128)S(1)} %output.2), channel_id=1, source_target_pairs={{0,1},{1,0},{2,3},{3,2},{4,5},{5,4},{6,7},{7,6},{8,9},{9,8},{10,11... | collective-permute-start | bytes 196616 | tf_op jit(solution)/shard_map/ppermute | solution.py:43
  50.0 5.2 %collective-permute-start.11 = (f32[16,1024]{1,0:T(8,128)S(1)}, f32[16,1024]{1,0:T(8,128)S(1)}, u32[]{:S(2)}, u32[]{:S(2)}) collective-permute-start(f32[16,1024]{1,0:T(8,128)S(1)} %output.2), channel_id=1, source_target_pairs={{0,3},{1,2},{2,1},{3,0},{4,7},{5,6},{6,5},{7,4},{8,11},{9,10},{10,... | collective-permute-start | bytes 196616 | tf_op jit(solution)/shard_map/ppermute | solution.py:43
  55.2 9.4 %collective-permute-start.12 = (f32[16,1024]{1,0:T(8,128)S(1)}, f32[16,1024]{1,0:T(8,128)S(1)}, u32[]{:S(2)}, u32[]{:S(2)}) collective-permute-start(f32[16,1024]{1,0:T(8,128)S(1)} %add.91), channel_id=1, source_target_pairs={{0,10},{2,8},{4,14},{6,12},{8,2},{10,0},{12,6},{14,4},{1,11},{3,9}... | collective-permute-start | bytes 196616 | tf_op jit(solution)/shard_map/ppermute | solution.py:38
  62.0 5.5 %collective-permute-start.13 = (f32[16,1024]{1,0:T(8,128)S(1)}, f32[16,1024]{1,0:T(8,128)S(1)}, u32[]{:S(2)}, u32[]{:S(2)}) collective-permute-start(f32[16,1024]{1,0:T(8,128)S(1)} %add.91), channel_id=1, source_target_pairs={{0,14},{2,4},{4,2},{6,8},{8,6},{10,12},{12,10},{14,0},{1,15},{3,5}... | collective-permute-start | bytes 196616 | tf_op jit(solution)/shard_map/ppermute | solution.py:38
  62.0 5.8 %collective-permute-start.14 = (f32[16,1024]{1,0:T(8,128)S(1)}, f32[16,1024]{1,0:T(8,128)S(1)}, u32[]{:S(2)}, u32[]{:S(2)}) collective-permute-start(f32[16,1024]{1,0:T(8,128)S(1)} %add.91), channel_id=1, source_target_pairs={{0,12},{2,6},{4,0},{6,10},{8,4},{10,14},{12,8},{14,2},{1,13},{3,7}... | collective-permute-start | bytes 196616 | tf_op jit(solution)/shard_map/ppermute | solution.py:38
  69.2 1.5 %collective-permute-start.16 = (f32[16,1280]{1,0:T(8,128)S(1)}, f32[16,1280]{1,0:T(8,128)S(1)}, u32[]{:S(2)}, u32[]{:S(2)}) collective-permute-start(f32[16,1280]{1,0:T(8,128)S(1)} %slice_bitcast_fusion), channel_id=1, source_target_pairs={{0,16},{16,0},{32,48},{48,32},{64,80},{80,64},{96,112},{112,96},{1... | collective-permute-start | bytes 245768 | tf_op jit(solution)/shard_map/ppermute | solution.py:29
  70.7 4.6 %collective-permute-start.17 = (f32[16,1280]{1,0:T(8,128)S(1)}, f32[16,1280]{1,0:T(8,128)S(1)}, u32[]{:S(2)}, u32[]{:S(2)}) collective-permute-start(f32[16,1280]{1,0:T(8,128)S(1)} %fusion), channel_id=1, source_target_pairs={{0,64},{16,80},{32,96},{48,112},{64,0},{80,16},{96,32},{112,48},{1... | collective-permute-start | bytes 245768 | tf_op jit(solution)/shard_map/ppermute | solution.py:29
  75.3 5.7 %collective-permute-start.18 = (f32[16,1280]{1,0:T(8,128)S(1)}, f32[16,1280]{1,0:T(8,128)S(1)}, u32[]{:S(2)}, u32[]{:S(2)}) collective-permute-start(f32[16,1280]{1,0:T(8,128)S(1)} %add.97), channel_id=1, source_target_pairs={{0,192},{16,208},{32,224},{48,240},{64,128},{80,144},{96,160},{112... | collective-permute-start | bytes 245768 | tf_op jit(solution)/shard_map/ppermute | solution.py:29
  81.1 6.0 %collective-permute-start.19 = (f32[16,1280]{1,0:T(8,128)S(1)}, f32[16,1280]{1,0:T(8,128)S(1)}, u32[]{:S(2)}, u32[]{:S(2)}) collective-permute-start(f32[16,1280]{1,0:T(8,128)S(1)} %add.98), channel_id=1, source_target_pairs={{0,32},{16,48},{32,0},{48,16},{64,96},{80,112},{96,64},{112,80},{1... | collective-permute-start | bytes 245768 | tf_op jit(solution)/shard_map/ppermute | solution.py:29
  87.1 1.4 %collective-permute-start.20 = (f32[16,1280]{1,0:T(8,128)S(1)}, f32[16,1280]{1,0:T(8,128)S(1)}, u32[]{:S(2)}, u32[]{:S(2)}) collective-permute-start(f32[16,1280]{1,0:T(8,128)S(1)} %add.99.own_ref), channel_id=1, source_target_pairs={{0,16},{16,0},{32,48},{48,32},{64,80},{80,64},{96,112},{112,96},{1... | collective-permute-start | bytes 245768 | tf_op jit(solution)/shard_map/ppermute | solution.py:29
  92.0 1.3 %collective-permute-start.21 = (f32[136,128]{1,0:T(8,128)S(1)}, f32[136,128]{1,0:T(8,128)S(1)}, u32[]{:S(2)}, u32[]{:S(2)}) collective-permute-start(f32[136,128]{1,0:T(8,128)S(1)} %slice_bitcast_fusion.5), channel_id=1, source_target_pairs={{0,16},{16,0},{32,48},{48,32},{64,80},{80,64},{96,112},{112,96},{1... | collective-permute-start | bytes 208904 | tf_op jit(solution)/shard_map/ppermute | solution.py:29
  93.4 4.4 %collective-permute-start.22 = (f32[136,128]{1,0:T(8,128)S(1)}, f32[136,128]{1,0:T(8,128)S(1)}, u32[]{:S(2)}, u32[]{:S(2)}) collective-permute-start(f32[136,128]{1,0:T(8,128)S(1)} %fusion.4), channel_id=1, source_target_pairs={{0,64},{16,80},{32,96},{48,112},{64,0},{80,16},{96,32},{112,48},{1... | collective-permute-start | bytes 208904 | tf_op jit(solution)/shard_map/ppermute | solution.py:29
  97.9 5.6 %collective-permute-start.23 = (f32[136,128]{1,0:T(8,128)S(1)}, f32[136,128]{1,0:T(8,128)S(1)}, u32[]{:S(2)}, u32[]{:S(2)}) collective-permute-start(f32[136,128]{1,0:T(8,128)S(1)} %add_select_fusion.2), channel_id=1, source_target_pairs={{0,192},{16,208},{32,224},{48,240},{64,128},{80,144},{96,160},{112... | collective-permute-start | bytes 208904 | tf_op jit(solution)/shard_map/ppermute | solution.py:29
  103.6 5.9 %collective-permute-start.24 = (f32[136,128]{1,0:T(8,128)S(1)}, f32[136,128]{1,0:T(8,128)S(1)}, u32[]{:S(2)}, u32[]{:S(2)}) collective-permute-start(f32[136,128]{1,0:T(8,128)S(1)} %add_select_fusion.1), channel_id=1, source_target_pairs={{0,32},{16,48},{32,0},{48,16},{64,96},{80,112},{96,64},{112,80},{1... | collective-permute-start | bytes 208904 | tf_op jit(solution)/shard_map/ppermute | solution.py:29
  109.6 1.3 %collective-permute-start.25 = (f32[136,128]{1,0:T(8,128)S(1)}, f32[136,128]{1,0:T(8,128)S(1)}, u32[]{:S(2)}, u32[]{:S(2)}) collective-permute-start(f32[136,128]{1,0:T(8,128)S(1)} %add_select_fusion.own_ref), channel_id=1, source_target_pairs={{0,16},{16,0},{32,48},{48,32},{64,80},{80,64},{96,112},{112,96},{1... | collective-permute-start | bytes 208904 | tf_op jit(solution)/shard_map/ppermute | solution.py:29
  112.2 5.0 %collective-permute-start.26 = (f32[16,1024]{1,0:T(8,128)S(1)}, f32[16,1024]{1,0:T(8,128)S(1)}, u32[]{:S(2)}, u32[]{:S(2)}) collective-permute-start(f32[16,1024]{1,0:T(8,128)S(1)} %output.3), channel_id=1, source_target_pairs={{0,2},{2,0},{4,6},{6,4},{8,10},{10,8},{12,14},{14,12},{1,3},{3,1},... | collective-permute-start | bytes 196616 | tf_op jit(solution)/shard_map/ppermute | solution.py:207
  117.3 9.6 %collective-permute-start.27 = (f32[16,1024]{1,0:T(8,128)S(1)}, f32[16,1024]{1,0:T(8,128)S(1)}, u32[]{:S(2)}, u32[]{:S(2)}) collective-permute-start(f32[16,1024]{1,0:T(8,128)S(1)} %add.104), channel_id=1, source_target_pairs={{0,10},{2,8},{4,14},{6,12},{8,2},{10,0},{12,6},{14,4},{1,11},{3,9}... | collective-permute-start | bytes 196616 | tf_op jit(solution)/shard_map/ppermute | solution.py:38
  120.4 6.5 %collective-permute-start.28 = (f32[16,1024]{1,0:T(8,128)S(1)}, f32[16,1024]{1,0:T(8,128)S(1)}, u32[]{:S(2)}, u32[]{:S(2)}) collective-permute-start(f32[16,1024]{1,0:T(8,128)S(1)} %add.104), channel_id=1, source_target_pairs={{0,14},{2,4},{4,2},{6,8},{8,6},{10,12},{12,10},{14,0},{1,15},{3,5}... | collective-permute-start | bytes 196616 | tf_op jit(solution)/shard_map/ppermute | solution.py:38
  122.3 5.3 %collective-permute-start.29 = (f32[16,1024]{1,0:T(8,128)S(1)}, f32[16,1024]{1,0:T(8,128)S(1)}, u32[]{:S(2)}, u32[]{:S(2)}) collective-permute-start(f32[16,1024]{1,0:T(8,128)S(1)} %add.104), channel_id=1, source_target_pairs={{0,12},{2,6},{4,0},{6,10},{8,4},{10,14},{12,8},{14,2},{1,13},{3,7}... | collective-permute-start | bytes 196616 | tf_op jit(solution)/shard_map/ppermute | solution.py:38
  122.9 3.9 %collective-permute-start.15 = (bf16[16,1024]{1,0:T(8,128)(2,1)S(1)}, bf16[16,1024]{1,0:T(8,128)(2,1)S(1)}, u32[]{:S(2)}, u32[]{:S(2)}) collective-permute-start(bf16[16,1024]{1,0:T(8,128)(2,1)S(1)} %add_convert_fusion.1.hidden_ref), channel_id=1, source_target_pairs={{0,1},{1,0},{2,3},{3,2},{4,5},{5,4},{6,7},{7,6},{8,9},{9,8},{10,11... | collective-permute-start | bytes 98312 | tf_op jit(solution)/shard_map/ppermute | solution.py:205

commit v2 on v1

v2 whole, which is shorter than its diff:
```python
import functools

import jax
import jax.numpy as jnp
from jax import lax
from jax.experimental import pallas as pl
from jax.experimental.pallas import tpu as pltpu
from jax.sharding import PartitionSpec as P

D = 16384
HEAD_DIM = 128
NEG_FLOOR = -1e30
EPSILON = 1e-05
F32 = jnp.float32
BF16 = jnp.bfloat16
VMEM = pl.BlockSpec(memory_space=pltpu.VMEM)
SMEM = pl.BlockSpec(memory_space=pltpu.SMEM)
HBM = pl.BlockSpec(memory_space=pltpu.HBM)
HALF = 1024
WIDE = HALF + 2 * HEAD_DIM
ROWS = 16
STAT = 8


def permute(value, move, active=None):
    pairs = []
    for source in range(256):
        seq, z, section = source // 16, (source // 2) % 8, source % 2
        x, y, core = seq // 4, (seq // 2) % 2, seq % 2
        if active is None or section == active:
            x, y, core, z, section = move(x, y, core, z, section)
        else:
            core = 1 - core
        pairs.append((source, (x * 4 + y * 2 + core) * 16 + (z % 8) * 2 + section))
    return lax.ppermute(value, ("kvseq", "kvhead", "section"), pairs)


def other_core(value):
    return permute(value, lambda x, y, c, z, s: (x, y, 1 - c, z, s))


def over_chips(value, join, active):
    value = join(value, permute(value, lambda x, y, c, z, s: (3 - x, y, c, z, s), active))
    along_x = permute(value, lambda x, y, c, z, s: (x ^ 1, y, c, z, s), active)
    along_y = permute(value, lambda x, y, c, z, s: (x, 1 - y, c, z, s), active)
    along_both = permute(value, lambda x, y, c, z, s: (x ^ 1, 1 - y, c, z, s), active)
    return join(value, along_x, along_y, along_both)


def over_pairs(pair, active):
    def step(far):
        return permute(
            pair, lambda x, y, c, z, s: (x, y, c, z + (-far if z % 2 else far), s), active
        )

    return add(pair, step(3), step(1), step(2))


def add(left, *others):
    if len(others) == 1:
        return left + others[0]
    return (left + others[0]) + (others[1] + others[2])


def scale_rows(hidden, gain):
    hidden = hidden.astype(F32)
    scaled = (hidden * gain.astype(F32)).astype(BF16)
    return scaled, jnp.sum(hidden * hidden, axis=-1, keepdims=True)


def fetch_project_kernel(
    ids_ref, hidden_hbm, gain_hbm, query_hbm, keyval_hbm, first_out, second_out,
    hidden_ref, gain_ref, query_ref, keyval_ref, sems,
):
    core = ids_ref[1]
    chunk = HALF // 2
    copies = [
        pltpu.make_async_copy(hidden_hbm, hidden_ref, sems.at[0]),
        pltpu.make_async_copy(gain_hbm, gain_ref, sems.at[1]),
        pltpu.make_async_copy(keyval_hbm, keyval_ref, sems.at[2]),
    ]
    for part in range(4):
        half = 1 - core if part < 2 else core
        start = pl.multiple_of(half * HALF + part % 2 * chunk, chunk)
        copies.append(
            pltpu.make_async_copy(
                query_hbm.at[:, pl.ds(start, chunk)], query_ref.at[part], sems.at[3 + part]
            )
        )
    for copy in copies:
        copy.start()
    copies[0].wait()
    copies[1].wait()
    scaled, squares = scale_rows(hidden_ref[...], gain_ref[...])
    copies[2].wait()
    for half, out_ref in ((1 - core, first_out), (core, second_out)):
        out_ref[:, HALF + HEAD_DIM :] = jnp.broadcast_to(squares, (ROWS, HEAD_DIM))
        columns = pl.ds(pl.multiple_of(half * HEAD_DIM, HEAD_DIM), HEAD_DIM)
        out_ref[:, HALF : HALF + HEAD_DIM] = jnp.dot(
            scaled, keyval_ref[:, columns], preferred_element_type=F32
        )
    for part in range(4):
        copies[3 + part].wait()
        out_ref = first_out if part < 2 else second_out
        columns = slice(part % 2 * chunk, (part % 2 + 1) * chunk)
        out_ref[:, columns] = jnp.dot(scaled, query_ref[part], preferred_element_type=F32)


def project_half(half, scaled, query_ref, keyval_ref, out_ref):
    columns = pl.ds(pl.multiple_of(half * HALF, HALF), HALF)
    out_ref[:, :HALF] = jnp.dot(scaled, query_ref[:, columns], preferred_element_type=F32)
    columns = pl.ds(pl.multiple_of(half * HEAD_DIM, HEAD_DIM), HEAD_DIM)
    out_ref[:, HALF : HALF + HEAD_DIM] = jnp.dot(
        scaled, keyval_ref[:, columns], preferred_element_type=F32
    )


def project_kernel(ids_ref, hidden_ref, gain_ref, query_ref, keyval_ref, out_ref, scaled_ref):
    scaled, squares = scale_rows(hidden_ref[...], gain_ref[...])
    scaled_ref[...] = scaled
    out_ref[:, HALF + HEAD_DIM :] = jnp.broadcast_to(squares, (ROWS, HEAD_DIM))
    project_half(1 - ids_ref[1], scaled, query_ref, keyval_ref, out_ref)


def project_own_kernel(ids_ref, scaled_ref, first_ref, query_ref, keyval_ref, out_ref):
    out_ref[:, HALF + HEAD_DIM :] = first_ref[:, HALF + HEAD_DIM :]
    project_half(ids_ref[1], scaled_ref[...], query_ref, keyval_ref, out_ref)


def attend_kernel(
    ids_ref, len_ref, own_ref, oth_ref, cache_ref, first_out, second_out,
    q_s, kv_s, score_s, weight_s, acc_s, stat_s,
):
    seq_id, core = ids_ref[0], ids_ref[1]
    for part, ref in enumerate((own_ref, oth_ref)):
        inv_rms = lax.rsqrt(ref[:, HALF + HEAD_DIM : HALF + HEAD_DIM + 1] / D + EPSILON)
        queries = (ref[:, :HALF] * inv_rms * HEAD_DIM ** (-0.5)).astype(BF16).astype(F32)
        for g in range(8):
            q_s[pl.ds((part * 8 + g) * ROWS, ROWS), :] = queries[:, g * HEAD_DIM : (g + 1) * HEAD_DIM]
        fresh = (ref[:, HALF : HALF + HEAD_DIM] * inv_rms).astype(BF16).astype(F32)
        kv_s[core if part == 0 else 1 - core] = fresh
    for r in range(8):
        queries = q_s[pl.ds(r, 32, stride=8), :].astype(BF16)
        score_s[r] = lax.dot_general(
            queries,
            cache_ref[r, :, :HEAD_DIM],
            (((1,), (1,)), ((), ())),
            preferred_element_type=F32,
        )
    lane = lax.broadcasted_iota(jnp.int32, (32, HEAD_DIM), 1)
    position = seq_id * 1024 + lax.broadcasted_iota(jnp.int32, (32, 1024), 1)
    for r in range(8):
        scores = score_s[r]
        valid = position < len_ref[r]
        top = jnp.max(jnp.where(valid, scores, NEG_FLOOR), axis=-1, keepdims=True)
        weights = jnp.where(valid, jnp.exp(scores - top), 0.0)
        weight_s[r] = weights.astype(BF16)
        total = jnp.sum(weights, axis=-1, keepdims=True)
        stat_s[pl.ds(r, 32, stride=8), :] = jnp.where(lane == 0, top, total)
    for r in range(8):
        acc_s[pl.ds(r, 32, stride=8), :] = jnp.dot(
            weight_s[r], cache_ref[r, :, HEAD_DIM:], preferred_element_type=F32
        )
    row = lax.broadcasted_iota(jnp.int32, (HEAD_DIM, 1), 0)
    late = (row // 8) % 2 == 1
    holder = seq_id == 0
    lane = lax.broadcasted_iota(jnp.int32, (HEAD_DIM, HEAD_DIM), 1)
    for part, out_ref in enumerate((first_out, second_out)):
        rows = pl.ds(part * HEAD_DIM, HEAD_DIM)
        queries = q_s[rows, :]
        top, total, acc = stat_s[rows, 0:1], stat_s[rows, 1:2], acc_s[rows, :]
        new_top, fresh = top, []
        for t in range(2):
            key = jnp.concatenate([kv_s[0, pl.ds(t * 8, 8), :]] * 16, axis=0)
            score = jnp.sum(queries * key, axis=-1, keepdims=True)
            seen = (late & holder) if t else (row >= 0) & holder
            fresh.append((seen, score))
            new_top = jnp.maximum(new_top, jnp.where(seen, score, NEG_FLOOR))
        scale = jnp.exp(top - new_top)
        acc, total = acc * scale, total * scale
        for t, (seen, score) in enumerate(fresh):
            weight = jnp.where(seen, jnp.exp(score - new_top), 0.0)
            acc = acc + weight * jnp.concatenate([kv_s[1, pl.ds(t * 8, 8), :]] * 16, axis=0)
            total = total + weight
        out_ref[:HEAD_DIM, :] = acc.T
        out_ref[HEAD_DIM:, :] = jnp.where(lane == 0, new_top, total).T[:STAT]


def output_half(half, ref, w_ref):
    attended = (ref[:HEAD_DIM, :] / ref[HEAD_DIM + 1 : HEAD_DIM + 2, :]).T.astype(BF16)
    attended = jnp.concatenate([attended[g * ROWS : (g + 1) * ROWS] for g in range(8)], axis=1)
    rows = pl.ds(pl.multiple_of(half * HALF, HALF), HALF)
    return jnp.dot(attended, w_ref[rows, :], preferred_element_type=F32)


def output_own_kernel(ids_ref, own_ref, w_ref, out_ref):
    out_ref[...] = output_half(ids_ref[1], own_ref, w_ref)


def output_kernel(ids_ref, term_ref, oth_ref, w_ref, out_ref):
    out_ref[...] = term_ref[...] + output_half(1 - ids_ref[1], oth_ref, w_ref)


def merge(*parts):
    tops = [part[HEAD_DIM : HEAD_DIM + 1] for part in parts]
    top = functools.reduce(jnp.maximum, tops)
    scaled = [part * jnp.exp(own - top) for part, own in zip(parts, tops)]
    row = lax.broadcasted_iota(jnp.int32, parts[0].shape, 0)
    return jnp.where(row == HEAD_DIM, top, add(*scaled))


def in_hbm(value):
    return pltpu.with_memory_space_constraint(value, pltpu.HBM)


def in_vmem(value):
    return pltpu.with_memory_space_constraint(value, pltpu.VMEM)


def per_device(hidden_in, lengths, norm_gain, w_query, w_keyval, w_out, kv_cache):
    section_id = lax.axis_index("section")
    seq_id = lax.axis_index("kvseq")
    core = seq_id % 2
    ids = jnp.stack([seq_id, core]).astype(jnp.int32)
    width = hidden_in.shape[2]
    raw_query, raw_keyval = w_query[0], w_keyval[0, :, 0, :]
    w_query, w_keyval = in_vmem(raw_query), in_vmem(raw_keyval)
    w_out, cache = in_vmem(w_out[0]), in_vmem(kv_cache[0, 0])
    payload = jax.ShapeDtypeStruct((ROWS, WIDE), F32)
    part_shape = jax.ShapeDtypeStruct((HEAD_DIM + STAT, HEAD_DIM), F32)
    row_shape = jax.ShapeDtypeStruct((ROWS, width), F32)
    scaled_shape = jax.ShapeDtypeStruct((ROWS, width), BF16)

    def call(kernel, name, out_shape, in_specs, *args, scratch=()):
        return pl.pallas_call(
            kernel,
            out_shape=out_shape,
            in_specs=in_specs,
            out_specs=jax.tree.map(lambda _: VMEM, out_shape),
            scratch_shapes=scratch,
            compiler_params=pltpu.CompilerParams(vmem_limit_bytes=24 * 2**20),
            name=name,
        )(*args)

    def rest_of_layer(mine, oth, cache, active, extra=None):
        own = over_chips(mine + other_core(oth), add, active)
        if extra is not None:
            own, extra = lax.optimization_barrier((own, extra))
            extra = lax.ppermute(extra, "section", [(0, 1), (1, 0)])
        mine, oth = call(
            attend_kernel, "attend", (part_shape, part_shape), [SMEM, SMEM] + [VMEM] * 3,
            ids, lengths, own, other_core(own), cache,
            scratch=[
                pltpu.VMEM((256, HEAD_DIM), F32),
                pltpu.VMEM((2, ROWS, HEAD_DIM), F32),
                pltpu.VMEM((8, 32, 1024), F32),
                pltpu.VMEM((8, 32, 1024), BF16),
                pltpu.VMEM((256, HEAD_DIM), F32),
                pltpu.VMEM((256, HEAD_DIM), F32),
            ],
        )
        if extra is not None:
            oth, extra = lax.optimization_barrier((oth, extra))
        own = over_chips(merge(mine, other_core(oth)), merge, active)
        oth = other_core(own)
        term = call(
            output_own_kernel, "output_own", row_shape, [SMEM] + [VMEM] * 2, ids, own, w_out
        )
        partial = call(
            output_kernel, "output", row_shape, [SMEM] + [VMEM] * 3, ids, term, oth, w_out
        )
        return partial, extra

    hidden = hidden_in.reshape(ROWS, width)
    oth, mine = call(
        fetch_project_kernel, "project_first", (payload, payload), [SMEM] + [HBM] * 4,
        ids, in_hbm(hidden), in_hbm(norm_gain), in_hbm(raw_query), in_hbm(raw_keyval),
        scratch=[
            pltpu.VMEM((ROWS, width), BF16),
            pltpu.VMEM((1, width), BF16),
            pltpu.VMEM((4, width, HALF // 2), BF16),
            pltpu.VMEM((width, 2 * HEAD_DIM), BF16),
            pltpu.SemaphoreType.DMA((7,)),
        ],
    )
    partial, _ = rest_of_layer(mine, oth, cache, 0)
    pair = permute(partial, lambda x, y, c, z, s: (x, y, c, z, 1 - s))
    pair = pair + permute(partial, lambda x, y, c, z, s: (x, y, c, z + (1 if z % 2 else -1), 1 - s))
    hidden = (hidden.astype(F32) + over_pairs(pair, 1)).astype(BF16)
    oth, scaled = call(
        project_kernel, "project", (payload, scaled_shape), [SMEM] + [VMEM] * 4,
        ids, hidden, norm_gain, w_query, w_keyval,
    )
    mine = call(
        project_own_kernel, "project_own", payload, [SMEM] + [VMEM] * 4,
        ids, scaled, oth, w_query, w_keyval,
    )
    partial, first = rest_of_layer(mine, oth, cache, 1, hidden)
    pair = partial + permute(partial, lambda x, y, c, z, s: (x, y, c, z + (1 if z % 2 else -1), s), 1)
    second = (hidden.astype(F32) + over_pairs(pair, 1)).astype(BF16)
    result = jnp.where(section_id == 0, first, second)
    return result.reshape(hidden_in.shape)[None]


def solution(mesh):
    placed = (
        P(None, None, "kvseq"),
        P(),
        P("section", "kvseq"),
        P("section", "kvseq", "kvhead"),
        P("section", "kvseq", "kvhead", None),
        P("section", "kvhead", "kvseq"),
        P("section", "kvhead", None, "kvseq", None),
    )
    return jax.shard_map(
        per_device,
        mesh=mesh,
        in_specs=placed,
        out_specs=P("section", None, None, "kvseq"),
        check_vma=False,
    )
```

time: 129 us -> 114 us (0.88)
  waiting for transfers between devices: 69.6 us -> 38.7 us
  starting transfers between devices: 39.9 us -> 58.9 us
  local copies, waits for them, and re-layouts: 5.01 us -> 0.03 us
  Pallas kernels: 11.9 us -> 13.8 us
    ppermute x30 -> x34, waiting for transfers between devices: 69.6 us -> 38.7 us  [the longest x33 38.2 us: permute(): return lax.ppermute(value, ('kvseq', 'kvhead', 'section'), pairs)]
    ppermute x30 -> x34, starting transfers between devices: 39.9 us -> 58.9 us  [the longest x33 58.8 us: permute(): return lax.ppermute(value, ('kvseq', 'kvhead', 'section'), pairs)]
    unnamed x20 -> x14, local copies, waits for them, and re-layouts: 4.97 us -> 0.03 us
    pallas_call x6 -> x9, Pallas kernels: 11.9 us -> 13.8 us  [call(): pl.pallas_call(kernel, out_shape=out_shape, in_specs=in_specs, out_specs=...]
  transfers between devices with their start and end apart: 30 -> 34, of which waited for: 28 -> 31; matrix products, arithmetic and copies ran while one was open for 0% -> 0% of each run, Pallas kernels for 0% -> 5%
where the time goes in v2:
time: 114 us; the launch traced here: 113 us
  starting transfers between devices  58.9 us (52%)
  waiting for transfers between devices  38.7 us (34%)
  Pallas kernels  13.8 us (12%)
  other arithmetic  1.49 us (1%)
    ppermute x33, starting transfers between devices, permute(): return lax.ppermute(value, ('kvseq', 'kvhead', 'section'), pairs)  58.8 us
    ppermute x33, waiting for transfers between devices, permute(): return lax.ppermute(value, ('kvseq', 'kvhead', 'section'), pairs)  38.2 us
    pallas_call x9, Pallas kernels, call(): pl.pallas_call(kernel, out_shape=out_shape, in_specs=in_specs, out_specs=...  13.8 us
  transfers between devices with their start and end apart: 34, of which 31 were waited for; matrix products, arithmetic and copies ran while one was open for 0% of the time, Pallas kernels for 5%

profile of v2, /device:TPU:24, one launch (start us, length us, event | category | flops | bytes accessed | tf_op | source)
XLA Modules:
  0.0 113.1 jit_solution(8858768493289845436)
XLA Ops:
  0.1 3.6 %project_first.1 = (f32[16,1280]{1,0:T(8,128)S(1)}, f32[16,1280]{1,0:T(8,128)S(1)}) custom-call(s32[2]{0:T(128)S(1)} %pad_add_fusion.ids_ref, bf16[16,1024]{1,0:T(8,128)(2,1)} %bitcast.64, bf16[1,1024]{1,0:T(2,128)(2,1)} %gain_ref.1, bf16[1024,2048]{1,0:T(8,128)(2,1)} %bitcast.56, bf16[1024,256]{1,0:T(8,128)(2,1)} %bitcast.61), custom_call_target="tpu_custom_call" | custom-call | tf_op jit(solution)/shard_map/project_first/pallas_call | solution.py:235
  3.8 1.3 %collective-permute-done = f32[16,1280]{1,0:T(8,128)S(1)} collective-permute-done((f32[16,1280]{1,0:T(8,128)S(1)}, f32[16,1280]{1,0:T(8,128)S(1)}, u32[]{:S(2)}, u32[]{:S(2)}) %collective-permute-start) | collective-permute-done | bytes 81952 | tf_op jit(solution)/shard_map/ppermute | solution.py:35
  5.0 0.2 collective-permute-start.1
  5.3 1.1 collective-permute-done.1
  6.4 0.2 collective-permute-start.4
  6.7 0.4 collective-permute-start.3
  7.2 0.6 collective-permute-done.4
  7.9 0.4 collective-permute-done.2
  8.3 0.2 collective-permute-start.5
  8.6 1.1 collective-permute-done.5.oth_ref
  9.7 2.2 %attend.2 = (f32[136,128]{1,0:T(8,128)S(1)}, f32[136,128]{1,0:T(8,128)S(1)}) custom-call(s32[2]{0:T(128)S(1)} %pad_add_fusion.ids_ref, s32[8]{0:T(128)S(1)} %copy-done.5, f32[16,1280]{1,0:T(8,128)S(1)} %add_add_fusion.1.own_ref, f32[16,1280]{1,0:T(8,128)S(1)} %collective-permute-done.5.oth_ref, bf16[8,1024,256]{2,1,0:T(8,128)(2,1)S(1)} %bitcast.59), custom_call_target="tpu_custom_call" | custom-call | tf_op jit(solution)/shard_map/attend/pallas_call | solution.py:235
  11.9 0.2 collective-permute-start.6
  12.1 1.1 collective-permute-done.6
  13.3 0.2 collective-permute-start.7
  13.6 1.1 collective-permute-done.7
  14.8 0.2 collective-permute-start.10
  15.0 0.4 collective-permute-start.9
  15.4 0.2 collective-permute-start.8
  15.5 0.6 collective-permute-done.10
  16.1 0.2 collective-permute-done.9
  16.3 0.4 collective-permute-done.8
  16.8 0.2 collective-permute-start.11
  17.0 1.0 output_own.2.term_ref
  18.1 1.0 output.2
  19.1 27.0 %collective-permute-start.13 = (f32[16,1024]{1,0:T(8,128)S(1)}, f32[16,1024]{1,0:T(8,128)S(1)}, u32[]{:S(2)}, u32[]{:S(2)}) collective-permute-start(f32[16,1024]{1,0:T(8,128)S(1)} %output.2), channel_id=1, source_target_pairs={{0,15},{1,14},{2,5},{3,4},{4,3},{5,2},{6,9},{7,8},{8,7},{9,6},{10,... | collective-permute-start | bytes 196616 | tf_op jit(solution)/shard_map/ppermute | solution.py:35
  46.1 2.5 %collective-permute-done.13 = f32[16,1024]{1,0:T(8,128)S(1)} collective-permute-done((f32[16,1024]{1,0:T(8,128)S(1)}, f32[16,1024]{1,0:T(8,128)S(1)}, u32[]{:S(2)}, u32[]{:S(2)}) %collective-permute-start.13) | collective-permute-done | bytes 65568 | tf_op jit(solution)/shard_map/ppermute | solution.py:35
  48.6 1.8 %collective-permute-done.12 = f32[16,1024]{1,0:T(8,128)S(1)} collective-permute-done((f32[16,1024]{1,0:T(8,128)S(1)}, f32[16,1024]{1,0:T(8,128)S(1)}, u32[]{:S(2)}, u32[]{:S(2)}) %collective-permute-start.12) | collective-permute-done | bytes 65568 | tf_op jit(solution)/shard_map/ppermute | solution.py:35
  50.5 0.3 collective-permute-start.15
  50.8 3.1 %collective-permute-start.14 = (f32[16,1024]{1,0:T(8,128)S(1)}, f32[16,1024]{1,0:T(8,128)S(1)}, u32[]{:S(2)}, u32[]{:S(2)}) collective-permute-start(f32[16,1024]{1,0:T(8,128)S(1)} %add.105), channel_id=1, source_target_pairs={{0,16},{1,7},{2,18},{3,13},{4,20},{5,11},{6,22},{7,1},{8,24},{9,15... | collective-permute-start | bytes 196616 | tf_op jit(solution)/shard_map/ppermute | solution.py:35
  53.9 2.9 %collective-permute-done.16 = f32[16,1024]{1,0:T(8,128)S(1)} collective-permute-done((f32[16,1024]{1,0:T(8,128)S(1)}, f32[16,1024]{1,0:T(8,128)S(1)}, u32[]{:S(2)}, u32[]{:S(2)}) %collective-permute-start.16) | collective-permute-done | bytes 65568 | tf_op jit(solution)/shard_map/ppermute | solution.py:35
  56.8 0.8 collective-permute-done.14
  57.7 1.0 project.1
  58.7 1.0 project_own.1
  59.7 0.3 collective-permute-done.17
  60.0 2.5 %collective-permute-start.18 = (f32[16,1280]{1,0:T(8,128)S(1)}, f32[16,1280]{1,0:T(8,128)S(1)}, u32[]{:S(2)}, u32[]{:S(2)}) collective-permute-start(f32[16,1280]{1,0:T(8,128)S(1)} %add.110), channel_id=1, source_target_pairs={{0,16},{1,193},{2,18},{3,195},{4,20},{5,197},{6,22},{7,199},{8,24}... | collective-permute-start | bytes 245768 | tf_op jit(solution)/shard_map/ppermute | solution.py:35
  62.5 3.4 %collective-permute-done.18 = f32[16,1280]{1,0:T(8,128)S(1)} collective-permute-done((f32[16,1280]{1,0:T(8,128)S(1)}, f32[16,1280]{1,0:T(8,128)S(1)}, u32[]{:S(2)}, u32[]{:S(2)}) %collective-permute-start.18) | collective-permute-done | bytes 81952 | tf_op jit(solution)/shard_map/ppermute | solution.py:35
  65.9 1.7 %collective-permute-start.21 = (f32[16,1280]{1,0:T(8,128)S(1)}, f32[16,1280]{1,0:T(8,128)S(1)}, u32[]{:S(2)}, u32[]{:S(2)}) collective-permute-start(f32[16,1280]{1,0:T(8,128)S(1)} %add.111), channel_id=1, source_target_pairs={{0,16},{1,97},{2,18},{3,99},{4,20},{5,101},{6,22},{7,103},{8,24},{... | collective-permute-start | bytes 245768 | tf_op jit(solution)/shard_map/ppermute | solution.py:35
  67.6 1.4 %collective-permute-start.20 = (f32[16,1280]{1,0:T(8,128)S(1)}, f32[16,1280]{1,0:T(8,128)S(1)}, u32[]{:S(2)}, u32[]{:S(2)}) collective-permute-start(f32[16,1280]{1,0:T(8,128)S(1)} %add.111), channel_id=1, source_target_pairs={{0,16},{1,33},{2,18},{3,35},{4,20},{5,37},{6,22},{7,39},{8,24},{9,... | collective-permute-start | bytes 245768 | tf_op jit(solution)/shard_map/ppermute | solution.py:35
  69.0 2.0 %collective-permute-start.19 = (f32[16,1280]{1,0:T(8,128)S(1)}, f32[16,1280]{1,0:T(8,128)S(1)}, u32[]{:S(2)}, u32[]{:S(2)}) collective-permute-start(f32[16,1280]{1,0:T(8,128)S(1)} %add.111), channel_id=1, source_target_pairs={{0,16},{1,65},{2,18},{3,67},{4,20},{5,69},{6,22},{7,71},{8,24},{9,... | collective-permute-start | bytes 245768 | tf_op jit(solution)/shard_map/ppermute | solution.py:35
  71.0 2.5 %collective-permute-done.21 = f32[16,1280]{1,0:T(8,128)S(1)} collective-permute-done((f32[16,1280]{1,0:T(8,128)S(1)}, f32[16,1280]{1,0:T(8,128)S(1)}, u32[]{:S(2)}, u32[]{:S(2)}) %collective-permute-start.21) | collective-permute-done | bytes 81952 | tf_op jit(solution)/shard_map/ppermute | solution.py:35
  73.4 0.5 collective-permute-done.20
  74.1 1.2 %collective-permute-done.22.oth_ref = f32[16,1280]{1,0:T(8,128)S(1)} collective-permute-done((f32[16,1280]{1,0:T(8,128)S(1)}, f32[16,1280]{1,0:T(8,128)S(1)}, u32[]{:S(2)}, u32[]{:S(2)}) %collective-permute-start.22) | collective-permute-done | bytes 81952 | tf_op jit(solution)/shard_map/ppermute | solution.py:35
  75.3 2.2 %attend.3 = (f32[136,128]{1,0:T(8,128)S(1)}, f32[136,128]{1,0:T(8,128)S(1)}) custom-call(s32[2]{0:T(128)S(1)} %pad_add_fusion.ids_ref, s32[8]{0:T(128)S(1)} %copy-done.5, f32[16,1280]{1,0:T(8,128)S(1)} %add_add_fusion.own_ref, f32[16,1280]{1,0:T(8,128)S(1)} %collective-permute-done.22.oth_ref, bf16[8,1024,256]{2,1,0:T(8,128)(2,1)S(1)} %bitcast.60), custom_call_target="tpu_custom_call" | custom-call | tf_op jit(solution)/shard_map/attend/pallas_call | solution.py:235
  77.5 0.5 collective-permute-done.23
  78.1 1.3 %collective-permute-done.24 = f32[136,128]{1,0:T(8,128)S(1)} collective-permute-done((f32[136,128]{1,0:T(8,128)S(1)}, f32[136,128]{1,0:T(8,128)S(1)}, u32[]{:S(2)}, u32[]{:S(2)}) %collective-permute-start.24) | collective-permute-done | bytes 69664 | tf_op jit(solution)/shard_map/ppermute | solution.py:35
  79.4 2.5 %collective-permute-start.25 = (f32[136,128]{1,0:T(8,128)S(1)}, f32[136,128]{1,0:T(8,128)S(1)}, u32[]{:S(2)}, u32[]{:S(2)}) collective-permute-start(f32[136,128]{1,0:T(8,128)S(1)} %add_select_fusion.2), channel_id=1, source_target_pairs={{0,16},{1,193},{2,18},{3,195},{4,20},{5,197},{6,22},{7,199},{8,24}... | collective-permute-start | bytes 208904 | tf_op jit(solution)/shard_map/ppermute | solution.py:35
  81.9 3.1 %collective-permute-done.25 = f32[136,128]{1,0:T(8,128)S(1)} collective-permute-done((f32[136,128]{1,0:T(8,128)S(1)}, f32[136,128]{1,0:T(8,128)S(1)}, u32[]{:S(2)}, u32[]{:S(2)}) %collective-permute-start.25) | collective-permute-done | bytes 69664 | tf_op jit(solution)/shard_map/ppermute | solution.py:35
  85.1 1.9 %collective-permute-start.28 = (f32[136,128]{1,0:T(8,128)S(1)}, f32[136,128]{1,0:T(8,128)S(1)}, u32[]{:S(2)}, u32[]{:S(2)}) collective-permute-start(f32[136,128]{1,0:T(8,128)S(1)} %add_select_fusion.1), channel_id=1, source_target_pairs={{0,16},{1,97},{2,18},{3,99},{4,20},{5,101},{6,22},{7,103},{8,24},{... | collective-permute-start | bytes 208904 | tf_op jit(solution)/shard_map/ppermute | solution.py:35
  87.0 1.5 %collective-permute-start.27 = (f32[136,128]{1,0:T(8,128)S(1)}, f32[136,128]{1,0:T(8,128)S(1)}, u32[]{:S(2)}, u32[]{:S(2)}) collective-permute-start(f32[136,128]{1,0:T(8,128)S(1)} %add_select_fusion.1), channel_id=1, source_target_pairs={{0,16},{1,33},{2,18},{3,35},{4,20},{5,37},{6,22},{7,39},{8,24},{9,... | collective-permute-start | bytes 208904 | tf_op jit(solution)/shard_map/ppermute | solution.py:35
  88.5 1.7 %collective-permute-start.26 = (f32[136,128]{1,0:T(8,128)S(1)}, f32[136,128]{1,0:T(8,128)S(1)}, u32[]{:S(2)}, u32[]{:S(2)}) collective-permute-start(f32[136,128]{1,0:T(8,128)S(1)} %add_select_fusion.1), channel_id=1, source_target_pairs={{0,16},{1,65},{2,18},{3,67},{4,20},{5,69},{6,22},{7,71},{8,24},{9,... | collective-permute-start | bytes 208904 | tf_op jit(solution)/shard_map/ppermute | solution.py:35
  90.2 2.5 %collective-permute-done.28 = f32[136,128]{1,0:T(8,128)S(1)} collective-permute-done((f32[136,128]{1,0:T(8,128)S(1)}, f32[136,128]{1,0:T(8,128)S(1)}, u32[]{:S(2)}, u32[]{:S(2)}) %collective-permute-start.28) | collective-permute-done | bytes 69664 | tf_op jit(solution)/shard_map/ppermute | solution.py:35
  92.7 0.4 collective-permute-done.27
  93.4 1.0 output_own.3.term_ref
  94.3 0.3 collective-permute-done.29.oth_ref
  94.6 1.0 output.3
  95.6 3.6 %collective-permute-start.30 = (f32[16,1024]{1,0:T(8,128)S(1)}, f32[16,1024]{1,0:T(8,128)S(1)}, u32[]{:S(2)}, u32[]{:S(2)}) collective-permute-start(f32[16,1024]{1,0:T(8,128)S(1)} %output.3), channel_id=1, source_target_pairs={{0,16},{1,15},{2,18},{3,5},{4,20},{5,3},{6,22},{7,9},{8,24},{9,7},... | collective-permute-start | bytes 196616 | tf_op jit(solution)/shard_map/ppermute | solution.py:35
  99.2 2.5 %collective-permute-done.30 = f32[16,1024]{1,0:T(8,128)S(1)} collective-permute-done((f32[16,1024]{1,0:T(8,128)S(1)}, f32[16,1024]{1,0:T(8,128)S(1)}, u32[]{:S(2)}, u32[]{:S(2)}) %collective-permute-start.30) | collective-permute-done | bytes 65568 | tf_op jit(solution)/shard_map/ppermute | solution.py:35
  101.7 1.5 %collective-permute-start.33 = (f32[16,1024]{1,0:T(8,128)S(1)}, f32[16,1024]{1,0:T(8,128)S(1)}, u32[]{:S(2)}, u32[]{:S(2)}) collective-permute-start(f32[16,1024]{1,0:T(8,128)S(1)} %add.120), channel_id=1, source_target_pairs={{0,16},{1,5},{2,18},{3,15},{4,20},{5,9},{6,22},{7,3},{8,24},{9,13}... | collective-permute-start | bytes 196616 | tf_op jit(solution)/shard_map/ppermute | solution.py:35
  103.2 3.1 %collective-permute-start.32 = (f32[16,1024]{1,0:T(8,128)S(1)}, f32[16,1024]{1,0:T(8,128)S(1)}, u32[]{:S(2)}, u32[]{:S(2)}) collective-permute-start(f32[16,1024]{1,0:T(8,128)S(1)} %add.120), channel_id=1, source_target_pairs={{0,16},{1,3},{2,18},{3,1},{4,20},{5,7},{6,22},{7,5},{8,24},{9,11},... | collective-permute-start | bytes 196616 | tf_op jit(solution)/shard_map/ppermute | solution.py:35
  106.2 1.9 %collective-permute-start.31 = (f32[16,1024]{1,0:T(8,128)S(1)}, f32[16,1024]{1,0:T(8,128)S(1)}, u32[]{:S(2)}, u32[]{:S(2)}) collective-permute-start(f32[16,1024]{1,0:T(8,128)S(1)} %add.120), channel_id=1, source_target_pairs={{0,16},{1,7},{2,18},{3,13},{4,20},{5,11},{6,22},{7,1},{8,24},{9,15... | collective-permute-start | bytes 196616 | tf_op jit(solution)/shard_map/ppermute | solution.py:35
  108.1 0.2 collective-permute-done.33
  108.3 2.3 %collective-permute-done.32 = f32[16,1024]{1,0:T(8,128)S(1)} collective-permute-done((f32[16,1024]{1,0:T(8,128)S(1)}, f32[16,1024]{1,0:T(8,128)S(1)}, u32[]{:S(2)}, u32[]{:S(2)}) %collective-permute-start.32) | collective-permute-done | bytes 65568 | tf_op jit(solution)/shard_map/ppermute | solution.py:35
  110.6 1.9 %collective-permute-done.31 = f32[16,1024]{1,0:T(8,128)S(1)} collective-permute-done((f32[16,1024]{1,0:T(8,128)S(1)}, f32[16,1024]{1,0:T(8,128)S(1)}, u32[]{:S(2)}, u32[]{:S(2)}) %collective-permute-start.31) | collective-permute-done | bytes 65568 | tf_op jit(solution)/shard_map/ppermute | solution.py:35
  112.5 0.6 fusion.1
  (53 shorter events, 1.8 us)
Async XLA Ops:
  0.0 9.7 %copy-start.5 = (s32[8]{0:T(128)S(1)}, s32[8]{0:T(128)}, u32[]{:S(2)}) copy-start(s32[8]{0:T(128)} %len_ref.3) | copy-start | bytes 100
  0.0 9.7 %copy-start.2 = (bf16[1,1,8,1024,256]{4,3,2,1,0:T(8,128)(2,1)S(1)}, bf16[1,1,8,1024,256]{4,3,2,1,0:T(8,128)(2,1)}, u32[]{:S(2)}) copy-start(bf16[1,1,8,1024,256]{4,3,2,1,0:T(8,128)(2,1)} %param.13) | copy-start | bytes 12582916
  3.6 13.4 %copy-start = (bf16[1,2048,1024]{2,1,0:T(8,128)(2,1)S(1)}, bf16[1,2048,1024]{2,1,0:T(8,128)(2,1)}, u32[]{:S(2)}) copy-start(bf16[1,2048,1024]{2,1,0:T(8,128)(2,1)} %param.12) | copy-start | bytes 12582916
  3.7 1.4 %collective-permute-start = (f32[16,1280]{1,0:T(8,128)S(1)}, f32[16,1280]{1,0:T(8,128)S(1)}, u32[]{:S(2)}, u32[]{:S(2)}) collective-permute-start(f32[16,1280]{1,0:T(8,128)S(1)} %get-tuple-element.18), channel_id=1, source_target_pairs={{0,16},{1,17},{2,18},{3,19},{4,20},{5,21},{6,22},{7,23},{8,24},{9,... | collective-permute-start | bytes 245768 | tf_op jit(solution)/shard_map/ppermute | solution.py:35
  5.0 1.4 %collective-permute-start.1 = (f32[16,1280]{1,0:T(8,128)S(1)}, f32[16,1280]{1,0:T(8,128)S(1)}, u32[]{:S(2)}, u32[]{:S(2)}) collective-permute-start(f32[16,1280]{1,0:T(8,128)S(1)} %add.95), channel_id=1, source_target_pairs={{0,192},{1,17},{2,194},{3,19},{4,196},{5,21},{6,198},{7,23},{8,200... | collective-permute-start | bytes 245768 | tf_op jit(solution)/shard_map/ppermute | solution.py:35
  6.4 1.4 %collective-permute-start.4 = (f32[16,1280]{1,0:T(8,128)S(1)}, f32[16,1280]{1,0:T(8,128)S(1)}, u32[]{:S(2)}, u32[]{:S(2)}) collective-permute-start(f32[16,1280]{1,0:T(8,128)S(1)} %add.96), channel_id=1, source_target_pairs={{0,96},{1,17},{2,98},{3,19},{4,100},{5,21},{6,102},{7,23},{8,104},... | collective-permute-start | bytes 245768 | tf_op jit(solution)/shard_map/ppermute | solution.py:35
  6.7 1.3 %collective-permute-start.3 = (f32[16,1280]{1,0:T(8,128)S(1)}, f32[16,1280]{1,0:T(8,128)S(1)}, u32[]{:S(2)}, u32[]{:S(2)}) collective-permute-start(f32[16,1280]{1,0:T(8,128)S(1)} %add.96), channel_id=1, source_target_pairs={{0,32},{1,17},{2,34},{3,19},{4,36},{5,21},{6,38},{7,23},{8,40},{9,... | collective-permute-start | bytes 245768 | tf_op jit(solution)/shard_map/ppermute | solution.py:35
  7.0 1.3 %collective-permute-start.2 = (f32[16,1280]{1,0:T(8,128)S(1)}, f32[16,1280]{1,0:T(8,128)S(1)}, u32[]{:S(2)}, u32[]{:S(2)}) collective-permute-start(f32[16,1280]{1,0:T(8,128)S(1)} %add.96), channel_id=1, source_target_pairs={{0,64},{1,17},{2,66},{3,19},{4,68},{5,21},{6,70},{7,23},{8,72},{9,... | collective-permute-start | bytes 245768 | tf_op jit(solution)/shard_map/ppermute | solution.py:35
  8.3 1.4 %collective-permute-start.5 = (f32[16,1280]{1,0:T(8,128)S(1)}, f32[16,1280]{1,0:T(8,128)S(1)}, u32[]{:S(2)}, u32[]{:S(2)}) collective-permute-start(f32[16,1280]{1,0:T(8,128)S(1)} %add_add_fusion.1.own_ref), channel_id=1, source_target_pairs={{0,16},{1,17},{2,18},{3,19},{4,20},{5,21},{6,22},{7,23},{8,24},{9,... | collective-permute-start | bytes 245768 | tf_op jit(solution)/shard_map/ppermute | solution.py:35
  11.9 1.3 %collective-permute-start.6 = (f32[136,128]{1,0:T(8,128)S(1)}, f32[136,128]{1,0:T(8,128)S(1)}, u32[]{:S(2)}, u32[]{:S(2)}) collective-permute-start(f32[136,128]{1,0:T(8,128)S(1)} %get-tuple-element.20), channel_id=1, source_target_pairs={{0,16},{1,17},{2,18},{3,19},{4,20},{5,21},{6,22},{7,23},{8,24},{9,... | collective-permute-start | bytes 208904 | tf_op jit(solution)/shard_map/ppermute | solution.py:35
  13.3 1.3 %collective-permute-start.7 = (f32[136,128]{1,0:T(8,128)S(1)}, f32[136,128]{1,0:T(8,128)S(1)}, u32[]{:S(2)}, u32[]{:S(2)}) collective-permute-start(f32[136,128]{1,0:T(8,128)S(1)} %add_select_fusion.5), channel_id=1, source_target_pairs={{0,192},{1,17},{2,194},{3,19},{4,196},{5,21},{6,198},{7,23},{8,200... | collective-permute-start | bytes 208904 | tf_op jit(solution)/shard_map/ppermute | solution.py:35
  14.8 1.3 %collective-permute-start.10 = (f32[136,128]{1,0:T(8,128)S(1)}, f32[136,128]{1,0:T(8,128)S(1)}, u32[]{:S(2)}, u32[]{:S(2)}) collective-permute-start(f32[136,128]{1,0:T(8,128)S(1)} %add_select_fusion.4), channel_id=1, source_target_pairs={{0,96},{1,17},{2,98},{3,19},{4,100},{5,21},{6,102},{7,23},{8,104},... | collective-permute-start | bytes 208904 | tf_op jit(solution)/shard_map/ppermute | solution.py:35
  15.0 1.3 %collective-permute-start.9 = (f32[136,128]{1,0:T(8,128)S(1)}, f32[136,128]{1,0:T(8,128)S(1)}, u32[]{:S(2)}, u32[]{:S(2)}) collective-permute-start(f32[136,128]{1,0:T(8,128)S(1)} %add_select_fusion.4), channel_id=1, source_target_pairs={{0,32},{1,17},{2,34},{3,19},{4,36},{5,21},{6,38},{7,23},{8,40},{9,... | collective-permute-start | bytes 208904 | tf_op jit(solution)/shard_map/ppermute | solution.py:35
  15.4 1.3 %collective-permute-start.8 = (f32[136,128]{1,0:T(8,128)S(1)}, f32[136,128]{1,0:T(8,128)S(1)}, u32[]{:S(2)}, u32[]{:S(2)}) collective-permute-start(f32[136,128]{1,0:T(8,128)S(1)} %add_select_fusion.4), channel_id=1, source_target_pairs={{0,64},{1,17},{2,66},{3,19},{4,68},{5,21},{6,70},{7,23},{8,72},{9,... | collective-permute-start | bytes 208904 | tf_op jit(solution)/shard_map/ppermute | solution.py:35
  16.8 1.3 %collective-permute-start.11 = (f32[136,128]{1,0:T(8,128)S(1)}, f32[136,128]{1,0:T(8,128)S(1)}, u32[]{:S(2)}, u32[]{:S(2)}) collective-permute-start(f32[136,128]{1,0:T(8,128)S(1)} %add_select_fusion.3.own_ref), channel_id=1, source_target_pairs={{0,16},{1,17},{2,18},{3,19},{4,20},{5,21},{6,22},{7,23},{8,24},{9,... | collective-permute-start | bytes 208904 | tf_op jit(solution)/shard_map/ppermute | solution.py:35
  17.0 40.6 %copy-start.6 = (bf16[2,8,1024]{2,1,0:T(8,128)(2,1)S(1)}, bf16[2,8,1024]{2,1,0:T(8,128)(2,1)}, u32[]{:S(2)}) copy-start(bf16[2,8,1024]{2,1,0:T(8,128)(2,1)} %param.7) | copy-start | bytes 98308
  17.0 40.6 %copy-start.1 = (bf16[1,1024,2048]{2,1,0:T(8,128)(2,1)S(1)}, bf16[1,1024,2048]{2,1,0:T(8,128)(2,1)}, u32[]{:S(2)}) copy-start(bf16[1,1024,2048]{2,1,0:T(8,128)(2,1)} %param.10) | copy-start | bytes 12582916
  17.0 40.6 %copy-start.3 = (bf16[1,1024,1,256]{3,1,2,0:T(8,128)(2,1)S(1)}, bf16[1,1024,1,256]{3,1,2,0:T(8,128)(2,1)}, u32[]{:S(2)}) copy-start(bf16[1,1024,1,256]{3,1,2,0:T(8,128)(2,1)} %param.11) | copy-start | bytes 1572868
  17.0 40.6 %copy-start.4 = (bf16[1,1024]{1,0:T(2,128)(2,1)S(1)}, bf16[1,1024]{1,0:T(2,128)(2,1)}, u32[]{:S(2)}) copy-start(bf16[1,1024]{1,0:T(2,128)(2,1)} %gain_ref.1) | copy-start | bytes 6148
  19.1 29.5 %collective-permute-start.13 = (f32[16,1024]{1,0:T(8,128)S(1)}, f32[16,1024]{1,0:T(8,128)S(1)}, u32[]{:S(2)}, u32[]{:S(2)}) collective-permute-start(f32[16,1024]{1,0:T(8,128)S(1)} %output.2), channel_id=1, source_target_pairs={{0,15},{1,14},{2,5},{3,4},{4,3},{5,2},{6,9},{7,8},{8,7},{9,6},{10,... | collective-permute-start | bytes 196616 | tf_op jit(solution)/shard_map/ppermute | solution.py:35
  46.1 4.3 %collective-permute-start.12 = (f32[16,1024]{1,0:T(8,128)S(1)}, f32[16,1024]{1,0:T(8,128)S(1)}, u32[]{:S(2)}, u32[]{:S(2)}) collective-permute-start(f32[16,1024]{1,0:T(8,128)S(1)} %output.2), channel_id=1, source_target_pairs={{0,1},{1,0},{2,3},{3,2},{4,5},{5,4},{6,7},{7,6},{8,9},{9,8},{10,11... | collective-permute-start | bytes 196616 | tf_op jit(solution)/shard_map/ppermute | solution.py:35
  50.4 6.4 %collective-permute-start.16 = (f32[16,1024]{1,0:T(8,128)S(1)}, f32[16,1024]{1,0:T(8,128)S(1)}, u32[]{:S(2)}, u32[]{:S(2)}) collective-permute-start(f32[16,1024]{1,0:T(8,128)S(1)} %add.105), channel_id=1, source_target_pairs={{0,16},{1,5},{2,18},{3,15},{4,20},{5,9},{6,22},{7,3},{8,24},{9,13}... | collective-permute-start | bytes 196616 | tf_op jit(solution)/shard_map/ppermute | solution.py:35
  50.5 6.4 %collective-permute-start.15 = (f32[16,1024]{1,0:T(8,128)S(1)}, f32[16,1024]{1,0:T(8,128)S(1)}, u32[]{:S(2)}, u32[]{:S(2)}) collective-permute-start(f32[16,1024]{1,0:T(8,128)S(1)} %add.105), channel_id=1, source_target_pairs={{0,16},{1,3},{2,18},{3,1},{4,20},{5,7},{6,22},{7,5},{8,24},{9,11},... | collective-permute-start | bytes 196616 | tf_op jit(solution)/shard_map/ppermute | solution.py:35
  50.8 6.8 %collective-permute-start.14 = (f32[16,1024]{1,0:T(8,128)S(1)}, f32[16,1024]{1,0:T(8,128)S(1)}, u32[]{:S(2)}, u32[]{:S(2)}) collective-permute-start(f32[16,1024]{1,0:T(8,128)S(1)} %add.105), channel_id=1, source_target_pairs={{0,16},{1,7},{2,18},{3,13},{4,20},{5,11},{6,22},{7,1},{8,24},{9,15... | collective-permute-start | bytes 196616 | tf_op jit(solution)/shard_map/ppermute | solution.py:35
  58.6 1.4 %collective-permute-start.17 = (f32[16,1280]{1,0:T(8,128)S(1)}, f32[16,1280]{1,0:T(8,128)S(1)}, u32[]{:S(2)}, u32[]{:S(2)}) collective-permute-start(f32[16,1280]{1,0:T(8,128)S(1)} %get-tuple-element.22.first_ref), channel_id=1, source_target_pairs={{0,16},{1,17},{2,18},{3,19},{4,20},{5,21},{6,22},{7,23},{8,24},{9,... | collective-permute-start | bytes 245768 | tf_op jit(solution)/shard_map/ppermute | solution.py:35
  60.0 5.9 %collective-permute-start.18 = (f32[16,1280]{1,0:T(8,128)S(1)}, f32[16,1280]{1,0:T(8,128)S(1)}, u32[]{:S(2)}, u32[]{:S(2)}) collective-permute-start(f32[16,1280]{1,0:T(8,128)S(1)} %add.110), channel_id=1, source_target_pairs={{0,16},{1,193},{2,18},{3,195},{4,20},{5,197},{6,22},{7,199},{8,24}... | collective-permute-start | bytes 245768 | tf_op jit(solution)/shard_map/ppermute | solution.py:35
  65.9 7.6 %collective-permute-start.21 = (f32[16,1280]{1,0:T(8,128)S(1)}, f32[16,1280]{1,0:T(8,128)S(1)}, u32[]{:S(2)}, u32[]{:S(2)}) collective-permute-start(f32[16,1280]{1,0:T(8,128)S(1)} %add.111), channel_id=1, source_target_pairs={{0,16},{1,97},{2,18},{3,99},{4,20},{5,101},{6,22},{7,103},{8,24},{... | collective-permute-start | bytes 245768 | tf_op jit(solution)/shard_map/ppermute | solution.py:35
  67.6 6.3 %collective-permute-start.20 = (f32[16,1280]{1,0:T(8,128)S(1)}, f32[16,1280]{1,0:T(8,128)S(1)}, u32[]{:S(2)}, u32[]{:S(2)}) collective-permute-start(f32[16,1280]{1,0:T(8,128)S(1)} %add.111), channel_id=1, source_target_pairs={{0,16},{1,33},{2,18},{3,35},{4,20},{5,37},{6,22},{7,39},{8,24},{9,... | collective-permute-start | bytes 245768 | tf_op jit(solution)/shard_map/ppermute | solution.py:35
  69.0 4.9 %collective-permute-start.19 = (f32[16,1280]{1,0:T(8,128)S(1)}, f32[16,1280]{1,0:T(8,128)S(1)}, u32[]{:S(2)}, u32[]{:S(2)}) collective-permute-start(f32[16,1280]{1,0:T(8,128)S(1)} %add.111), channel_id=1, source_target_pairs={{0,16},{1,65},{2,18},{3,67},{4,20},{5,69},{6,22},{7,71},{8,24},{9,... | collective-permute-start | bytes 245768 | tf_op jit(solution)/shard_map/ppermute | solution.py:35
  73.9 1.4 %collective-permute-start.22 = (f32[16,1280]{1,0:T(8,128)S(1)}, f32[16,1280]{1,0:T(8,128)S(1)}, u32[]{:S(2)}, u32[]{:S(2)}) collective-permute-start(f32[16,1280]{1,0:T(8,128)S(1)} %add_add_fusion.own_ref), channel_id=1, source_target_pairs={{0,16},{1,17},{2,18},{3,19},{4,20},{5,21},{6,22},{7,23},{8,24},{9,... | collective-permute-start | bytes 245768 | tf_op jit(solution)/shard_map/ppermute | solution.py:35
  74.0 4.0 %collective-permute-start.23 = (bf16[16,1024]{1,0:T(8,128)(2,1)S(1)}, bf16[16,1024]{1,0:T(8,128)(2,1)S(1)}, u32[]{:S(2)}, u32[]{:S(2)}) collective-permute-start(bf16[16,1024]{1,0:T(8,128)(2,1)S(1)} %add_convert_fusion.1.hidden_ref), channel_id=1, source_target_pairs={{0,1},{1,0},{2,3},{3,2},{4,5},{5,4},{6,7},{7,6},{8,9},{9,8},{10,11... | collective-permute-start | bytes 98312 | tf_op jit(solution)/shard_map/ppermute | solution.py:249
  78.0 1.3 %collective-permute-start.24 = (f32[136,128]{1,0:T(8,128)S(1)}, f32[136,128]{1,0:T(8,128)S(1)}, u32[]{:S(2)}, u32[]{:S(2)}) collective-permute-start(f32[136,128]{1,0:T(8,128)S(1)} %get-tuple-element.28), channel_id=1, source_target_pairs={{0,16},{1,17},{2,18},{3,19},{4,20},{5,21},{6,22},{7,23},{8,24},{9,... | collective-permute-start | bytes 208904 | tf_op jit(solution)/shard_map/ppermute | solution.py:35
  79.4 5.6 %collective-permute-start.25 = (f32[136,128]{1,0:T(8,128)S(1)}, f32[136,128]{1,0:T(8,128)S(1)}, u32[]{:S(2)}, u32[]{:S(2)}) collective-permute-start(f32[136,128]{1,0:T(8,128)S(1)} %add_select_fusion.2), channel_id=1, source_target_pairs={{0,16},{1,193},{2,18},{3,195},{4,20},{5,197},{6,22},{7,199},{8,24}... | collective-permute-start | bytes 208904 | tf_op jit(solution)/shard_map/ppermute | solution.py:35
  85.1 7.6 %collective-permute-start.28 = (f32[136,128]{1,0:T(8,128)S(1)}, f32[136,128]{1,0:T(8,128)S(1)}, u32[]{:S(2)}, u32[]{:S(2)}) collective-permute-start(f32[136,128]{1,0:T(8,128)S(1)} %add_select_fusion.1), channel_id=1, source_target_pairs={{0,16},{1,97},{2,18},{3,99},{4,20},{5,101},{6,22},{7,103},{8,24},{... | collective-permute-start | bytes 208904 | tf_op jit(solution)/shard_map/ppermute | solution.py:35
  87.0 6.1 %collective-permute-start.27 = (f32[136,128]{1,0:T(8,128)S(1)}, f32[136,128]{1,0:T(8,128)S(1)}, u32[]{:S(2)}, u32[]{:S(2)}) collective-permute-start(f32[136,128]{1,0:T(8,128)S(1)} %add_select_fusion.1), channel_id=1, source_target_pairs={{0,16},{1,33},{2,18},{3,35},{4,20},{5,37},{6,22},{7,39},{8,24},{9,... | collective-permute-start | bytes 208904 | tf_op jit(solution)/shard_map/ppermute | solution.py:35
  88.5 4.6 %collective-permute-start.26 = (f32[136,128]{1,0:T(8,128)S(1)}, f32[136,128]{1,0:T(8,128)S(1)}, u32[]{:S(2)}, u32[]{:S(2)}) collective-permute-start(f32[136,128]{1,0:T(8,128)S(1)} %add_select_fusion.1), channel_id=1, source_target_pairs={{0,16},{1,65},{2,18},{3,67},{4,20},{5,69},{6,22},{7,71},{8,24},{9,... | collective-permute-start | bytes 208904 | tf_op jit(solution)/shard_map/ppermute | solution.py:35
  93.3 1.3 %collective-permute-start.29 = (f32[136,128]{1,0:T(8,128)S(1)}, f32[136,128]{1,0:T(8,128)S(1)}, u32[]{:S(2)}, u32[]{:S(2)}) collective-permute-start(f32[136,128]{1,0:T(8,128)S(1)} %add_select_fusion.own_ref), channel_id=1, source_target_pairs={{0,16},{1,17},{2,18},{3,19},{4,20},{5,21},{6,22},{7,23},{8,24},{9,... | collective-permute-start | bytes 208904 | tf_op jit(solution)/shard_map/ppermute | solution.py:35
  95.6 6.1 %collective-permute-start.30 = (f32[16,1024]{1,0:T(8,128)S(1)}, f32[16,1024]{1,0:T(8,128)S(1)}, u32[]{:S(2)}, u32[]{:S(2)}) collective-permute-start(f32[16,1024]{1,0:T(8,128)S(1)} %output.3), channel_id=1, source_target_pairs={{0,16},{1,15},{2,18},{3,5},{4,20},{5,3},{6,22},{7,9},{8,24},{9,7},... | collective-permute-start | bytes 196616 | tf_op jit(solution)/shard_map/ppermute | solution.py:35
  101.7 6.6 %collective-permute-start.33 = (f32[16,1024]{1,0:T(8,128)S(1)}, f32[16,1024]{1,0:T(8,128)S(1)}, u32[]{:S(2)}, u32[]{:S(2)}) collective-permute-start(f32[16,1024]{1,0:T(8,128)S(1)} %add.120), channel_id=1, source_target_pairs={{0,16},{1,5},{2,18},{3,15},{4,20},{5,9},{6,22},{7,3},{8,24},{9,13}... | collective-permute-start | bytes 196616 | tf_op jit(solution)/shard_map/ppermute | solution.py:35
  103.2 7.4 %collective-permute-start.32 = (f32[16,1024]{1,0:T(8,128)S(1)}, f32[16,1024]{1,0:T(8,128)S(1)}, u32[]{:S(2)}, u32[]{:S(2)}) collective-permute-start(f32[16,1024]{1,0:T(8,128)S(1)} %add.120), channel_id=1, source_target_pairs={{0,16},{1,3},{2,18},{3,1},{4,20},{5,7},{6,22},{7,5},{8,24},{9,11},... | collective-permute-start | bytes 196616 | tf_op jit(solution)/shard_map/ppermute | solution.py:35
  106.2 6.2 %collective-permute-start.31 = (f32[16,1024]{1,0:T(8,128)S(1)}, f32[16,1024]{1,0:T(8,128)S(1)}, u32[]{:S(2)}, u32[]{:S(2)}) collective-permute-start(f32[16,1024]{1,0:T(8,128)S(1)} %add.120), channel_id=1, source_target_pairs={{0,16},{1,7},{2,18},{3,13},{4,20},{5,11},{6,22},{7,1},{8,24},{9,15... | collective-permute-start | bytes 196616 | tf_op jit(solution)/shard_map/ppermute | solution.py:35

commit v3 on v2

--- a/solution.py
+++ b/solution.py
@@ -19,6 +19,8 @@
 HALF = 1024
 WIDE = HALF + 2 * HEAD_DIM
 ROWS = 16
+FETCHES = 8
+FETCH = 128
 STAT = 8
 
 
@@ -40,11 +42,11 @@
 
 
 def over_chips(value, join, active):
-    value = join(value, permute(value, lambda x, y, c, z, s: (3 - x, y, c, z, s), active))
-    along_x = permute(value, lambda x, y, c, z, s: (x ^ 1, y, c, z, s), active)
-    along_y = permute(value, lambda x, y, c, z, s: (x, 1 - y, c, z, s), active)
-    along_both = permute(value, lambda x, y, c, z, s: (x ^ 1, 1 - y, c, z, s), active)
-    return join(value, along_x, along_y, along_both)
+    value = join(value, permute(value, lambda x, y, c, z, s: (x, 1 - y, c, z, s), active))
+    steps = [
+        permute(value, lambda x, y, c, z, s, k=k: (x ^ k, y, c, z, s), active) for k in (1, 3, 2)
+    ]
+    return join(value, *steps)
 
 
 def over_pairs(pair, active):
@@ -53,7 +55,8 @@
             pair, lambda x, y, c, z, s: (x, y, c, z + (-far if z % 2 else far), s), active
         )
 
-    return add(pair, step(3), step(1), step(2))
+    near, next_near, far = step(1), step(2), step(3)
+    return add(pair, far, near, next_near)
 
 
 def add(left, *others):
@@ -73,37 +76,35 @@
     hidden_ref, gain_ref, query_ref, keyval_ref, sems,
 ):
     core = ids_ref[1]
-    chunk = HALF // 2
     copies = [
         pltpu.make_async_copy(hidden_hbm, hidden_ref, sems.at[0]),
         pltpu.make_async_copy(gain_hbm, gain_ref, sems.at[1]),
-        pltpu.make_async_copy(keyval_hbm, keyval_ref, sems.at[2]),
     ]
-    for part in range(4):
-        half = 1 - core if part < 2 else core
-        start = pl.multiple_of(half * HALF + part % 2 * chunk, chunk)
+    for part in range(FETCHES):
+        rows = pl.ds(part * FETCH, FETCH)
         copies.append(
-            pltpu.make_async_copy(
-                query_hbm.at[:, pl.ds(start, chunk)], query_ref.at[part], sems.at[3 + part]
-            )
-        )
+            pltpu.make_async_copy(query_hbm.at[rows], query_ref.at[rows], sems.at[3 + part])
+        )
+    copies.append(pltpu.make_async_copy(keyval_hbm, keyval_ref, sems.at[2]))
     for copy in copies:
         copy.start()
     copies[0].wait()
     copies[1].wait()
     scaled, squares = scale_rows(hidden_ref[...], gain_ref[...])
-    copies[2].wait()
-    for half, out_ref in ((1 - core, first_out), (core, second_out)):
+    queries = None
+    for part in range(FETCHES):
+        copies[2 + part].wait()
+        rows = slice(part * FETCH, (part + 1) * FETCH)
+        term = jnp.dot(scaled[:, rows], query_ref[rows, :], preferred_element_type=F32)
+        queries = term if queries is None else queries + term
+    copies[-1].wait()
+    keyvals = jnp.dot(scaled, keyval_ref[...], preferred_element_type=F32)
+    for out_ref, low in ((first_out, core == 1), (second_out, core == 0)):
+        out_ref[:, :HALF] = jnp.where(low, queries[:, :HALF], queries[:, HALF:])
+        out_ref[:, HALF : HALF + HEAD_DIM] = jnp.where(
+            low, keyvals[:, :HEAD_DIM], keyvals[:, HEAD_DIM:]
+        )
         out_ref[:, HALF + HEAD_DIM :] = jnp.broadcast_to(squares, (ROWS, HEAD_DIM))
-        columns = pl.ds(pl.multiple_of(half * HEAD_DIM, HEAD_DIM), HEAD_DIM)
-        out_ref[:, HALF : HALF + HEAD_DIM] = jnp.dot(
-            scaled, keyval_ref[:, columns], preferred_element_type=F32
-        )
-    for part in range(4):
-        copies[3 + part].wait()
-        out_ref = first_out if part < 2 else second_out
-        columns = slice(part % 2 * chunk, (part % 2 + 1) * chunk)
-        out_ref[:, columns] = jnp.dot(scaled, query_ref[part], preferred_element_type=F32)
 
 
 def project_half(half, scaled, query_ref, keyval_ref, out_ref):
@@ -259,9 +260,9 @@
                 pltpu.VMEM((256, HEAD_DIM), F32),
             ],
         )
+        own = over_chips(merge(mine, other_core(oth)), merge, active)
         if extra is not None:
-            oth, extra = lax.optimization_barrier((oth, extra))
-        own = over_chips(merge(mine, other_core(oth)), merge, active)
+            own, extra = lax.optimization_barrier((own, extra))
         oth = other_core(own)
         term = call(
             output_own_kernel, "output_own", row_shape, [SMEM] + [VMEM] * 2, ids, own, w_out
@@ -278,9 +279,9 @@
         scratch=[
             pltpu.VMEM((ROWS, width), BF16),
             pltpu.VMEM((1, width), BF16),
-            pltpu.VMEM((4, width, HALF // 2), BF16),
+            pltpu.VMEM((width, 2 * HALF), BF16),
             pltpu.VMEM((width, 2 * HEAD_DIM), BF16),
-            pltpu.SemaphoreType.DMA((7,)),
+            pltpu.SemaphoreType.DMA((3 + FETCHES,)),
         ],
     )
     partial, _ = rest_of_layer(mine, oth, cache, 0)

time: 114 us -> 113 us (level)
  starting transfers between devices: 58.9 us -> 53.5 us
  waiting for transfers between devices: 38.7 us -> 43.9 us
    ppermute x33, waiting for transfers between devices: 38.2 us -> 43.7 us  [permute(): return lax.ppermute(value, ('kvseq', 'kvhead', 'section'), pairs)]
    ppermute x33, starting transfers between devices: 58.8 us -> 53.5 us  [permute(): return lax.ppermute(value, ('kvseq', 'kvhead', 'section'), pairs)]
  transfers between devices with their start and end apart: 34 -> 34, of which waited for: 31 -> 31; matrix products, arithmetic and copies ran while one was open for 0% -> 0% of each run, Pallas kernels for 5% -> 3%
where the time goes in v3:
time: 113 us
  starting transfers between devices  53.5 us (47%)
  waiting for transfers between devices  43.9 us (39%)
  Pallas kernels  13.7 us (12%)
  other arithmetic  1.49 us (1%)
    ppermute x33, starting transfers between devices, permute(): return lax.ppermute(value, ('kvseq', 'kvhead', 'section'), pairs)  53.5 us
    ppermute x33, waiting for transfers between devices, permute(): return lax.ppermute(value, ('kvseq', 'kvhead', 'section'), pairs)  43.7 us
    pallas_call x9, Pallas kernels, call(): pl.pallas_call(kernel, out_shape=out_shape, in_specs=in_specs, out_specs=...  13.7 us
  transfers between devices with their start and end apart: 34, of which 31 were waited for; matrix products, arithmetic and copies ran while one was open for 0% of the time, Pallas kernels for 3%

profile of v3, /device:TPU:24, one launch (start us, length us, event | category | flops | bytes accessed | tf_op | source)
XLA Modules:
  0.0 112.8 jit_solution(15307880111885254692)
XLA Ops:
  0.1 3.5 %project_first.1 = (f32[16,1280]{1,0:T(8,128)S(1)}, f32[16,1280]{1,0:T(8,128)S(1)}) custom-call(s32[2]{0:T(128)S(1)} %pad_add_fusion.ids_ref, bf16[16,1024]{1,0:T(8,128)(2,1)} %bitcast.64, bf16[1,1024]{1,0:T(2,128)(2,1)} %gain_ref.1, bf16[1024,2048]{1,0:T(8,128)(2,1)} %bitcast.56, bf16[1024,256]{1,0:T(8,128)(2,1)} %bitcast.61), custom_call_target="tpu_custom_call" | custom-call | tf_op jit(solution)/shard_map/project_first/pallas_call | solution.py:236
  3.7 1.3 %collective-permute-done = f32[16,1280]{1,0:T(8,128)S(1)} collective-permute-done((f32[16,1280]{1,0:T(8,128)S(1)}, f32[16,1280]{1,0:T(8,128)S(1)}, u32[]{:S(2)}, u32[]{:S(2)}) %collective-permute-start) | collective-permute-done | bytes 81952 | tf_op jit(solution)/shard_map/ppermute | solution.py:37
  5.0 0.2 collective-permute-start.1
  5.2 1.1 collective-permute-done.1
  6.4 0.2 collective-permute-start.4
  6.6 0.4 collective-permute-start.3
  7.1 0.6 collective-permute-done.4
  7.9 0.4 collective-permute-done.2
  8.3 0.2 collective-permute-start.5
  8.5 1.1 collective-permute-done.5.oth_ref
  9.6 2.2 %attend.2 = (f32[136,128]{1,0:T(8,128)S(1)}, f32[136,128]{1,0:T(8,128)S(1)}) custom-call(s32[2]{0:T(128)S(1)} %pad_add_fusion.ids_ref, s32[8]{0:T(128)S(1)} %copy-done.5, f32[16,1280]{1,0:T(8,128)S(1)} %add_add_fusion.1.own_ref, f32[16,1280]{1,0:T(8,128)S(1)} %collective-permute-done.5.oth_ref, bf16[8,1024,256]{2,1,0:T(8,128)(2,1)S(1)} %bitcast.59), custom_call_target="tpu_custom_call" | custom-call | tf_op jit(solution)/shard_map/attend/pallas_call | solution.py:236
  11.8 0.2 collective-permute-start.6
  12.1 1.1 collective-permute-done.6
  13.3 0.2 collective-permute-start.7
  13.5 1.1 collective-permute-done.7
  14.7 0.2 collective-permute-start.10
  15.0 0.4 collective-permute-start.9
  15.3 0.2 collective-permute-start.8
  15.5 0.6 collective-permute-done.10
  16.1 0.2 collective-permute-done.9
  16.2 0.4 collective-permute-done.8
  16.7 0.2 collective-permute-start.11
  17.0 1.0 output_own.2.term_ref
  18.1 1.0 output.2
  19.0 27.6 %collective-permute-start.13 = (f32[16,1024]{1,0:T(8,128)S(1)}, f32[16,1024]{1,0:T(8,128)S(1)}, u32[]{:S(2)}, u32[]{:S(2)}) collective-permute-start(f32[16,1024]{1,0:T(8,128)S(1)} %output.2), channel_id=1, source_target_pairs={{0,15},{1,14},{2,5},{3,4},{4,3},{5,2},{6,9},{7,8},{8,7},{9,6},{10,... | collective-permute-start | bytes 196616 | tf_op jit(solution)/shard_map/ppermute | solution.py:37
  46.6 2.5 %collective-permute-done.13 = f32[16,1024]{1,0:T(8,128)S(1)} collective-permute-done((f32[16,1024]{1,0:T(8,128)S(1)}, f32[16,1024]{1,0:T(8,128)S(1)}, u32[]{:S(2)}, u32[]{:S(2)}) %collective-permute-start.13) | collective-permute-done | bytes 65568 | tf_op jit(solution)/shard_map/ppermute | solution.py:37
  49.1 1.8 %collective-permute-done.12 = f32[16,1024]{1,0:T(8,128)S(1)} collective-permute-done((f32[16,1024]{1,0:T(8,128)S(1)}, f32[16,1024]{1,0:T(8,128)S(1)}, u32[]{:S(2)}, u32[]{:S(2)}) %collective-permute-start.12) | collective-permute-done | bytes 65568 | tf_op jit(solution)/shard_map/ppermute | solution.py:37
  50.9 0.3 collective-permute-start.15
  51.3 3.1 %collective-permute-start.14 = (f32[16,1024]{1,0:T(8,128)S(1)}, f32[16,1024]{1,0:T(8,128)S(1)}, u32[]{:S(2)}, u32[]{:S(2)}) collective-permute-start(f32[16,1024]{1,0:T(8,128)S(1)} %add.105), channel_id=1, source_target_pairs={{0,16},{1,7},{2,18},{3,13},{4,20},{5,11},{6,22},{7,1},{8,24},{9,15... | collective-permute-start | bytes 196616 | tf_op jit(solution)/shard_map/ppermute | solution.py:37
  54.4 2.9 %collective-permute-done.16 = f32[16,1024]{1,0:T(8,128)S(1)} collective-permute-done((f32[16,1024]{1,0:T(8,128)S(1)}, f32[16,1024]{1,0:T(8,128)S(1)}, u32[]{:S(2)}, u32[]{:S(2)}) %collective-permute-start.16) | collective-permute-done | bytes 65568 | tf_op jit(solution)/shard_map/ppermute | solution.py:37
  57.3 0.8 collective-permute-done.14
  58.1 1.0 project.1
  59.2 1.0 project_own.1
  60.2 0.3 collective-permute-done.17
  60.5 1.0 collective-permute-start.18
  61.5 5.1 %collective-permute-done.18 = f32[16,1280]{1,0:T(8,128)S(1)} collective-permute-done((f32[16,1280]{1,0:T(8,128)S(1)}, f32[16,1280]{1,0:T(8,128)S(1)}, u32[]{:S(2)}, u32[]{:S(2)}) %collective-permute-start.18) | collective-permute-done | bytes 81952 | tf_op jit(solution)/shard_map/ppermute | solution.py:37
  66.6 2.2 %collective-permute-start.21 = (f32[16,1280]{1,0:T(8,128)S(1)}, f32[16,1280]{1,0:T(8,128)S(1)}, u32[]{:S(2)}, u32[]{:S(2)}) collective-permute-start(f32[16,1280]{1,0:T(8,128)S(1)} %add.111), channel_id=1, source_target_pairs={{0,16},{1,129},{2,18},{3,131},{4,20},{5,133},{6,22},{7,135},{8,24}... | collective-permute-start | bytes 245768 | tf_op jit(solution)/shard_map/ppermute | solution.py:37
  68.9 1.2 %collective-permute-start.20 = (f32[16,1280]{1,0:T(8,128)S(1)}, f32[16,1280]{1,0:T(8,128)S(1)}, u32[]{:S(2)}, u32[]{:S(2)}) collective-permute-start(f32[16,1280]{1,0:T(8,128)S(1)} %add.111), channel_id=1, source_target_pairs={{0,16},{1,193},{2,18},{3,195},{4,20},{5,197},{6,22},{7,199},{8,24}... | collective-permute-start | bytes 245768 | tf_op jit(solution)/shard_map/ppermute | solution.py:37
  70.2 2.6 %collective-permute-done.21 = f32[16,1280]{1,0:T(8,128)S(1)} collective-permute-done((f32[16,1280]{1,0:T(8,128)S(1)}, f32[16,1280]{1,0:T(8,128)S(1)}, u32[]{:S(2)}, u32[]{:S(2)}) %collective-permute-start.21) | collective-permute-done | bytes 81952 | tf_op jit(solution)/shard_map/ppermute | solution.py:37
  72.8 1.7 %collective-permute-done.20 = f32[16,1280]{1,0:T(8,128)S(1)} collective-permute-done((f32[16,1280]{1,0:T(8,128)S(1)}, f32[16,1280]{1,0:T(8,128)S(1)}, u32[]{:S(2)}, u32[]{:S(2)}) %collective-permute-start.20) | collective-permute-done | bytes 81952 | tf_op jit(solution)/shard_map/ppermute | solution.py:37
  74.7 1.3 %collective-permute-done.22.oth_ref = f32[16,1280]{1,0:T(8,128)S(1)} collective-permute-done((f32[16,1280]{1,0:T(8,128)S(1)}, f32[16,1280]{1,0:T(8,128)S(1)}, u32[]{:S(2)}, u32[]{:S(2)}) %collective-permute-start.22) | collective-permute-done | bytes 81952 | tf_op jit(solution)/shard_map/ppermute | solution.py:37
  75.9 2.2 %attend.3 = (f32[136,128]{1,0:T(8,128)S(1)}, f32[136,128]{1,0:T(8,128)S(1)}) custom-call(s32[2]{0:T(128)S(1)} %pad_add_fusion.ids_ref, s32[8]{0:T(128)S(1)} %copy-done.5, f32[16,1280]{1,0:T(8,128)S(1)} %add_add_fusion.own_ref, f32[16,1280]{1,0:T(8,128)S(1)} %collective-permute-done.22.oth_ref, bf16[8,1024,256]{2,1,0:T(8,128)(2,1)S(1)} %bitcast.60), custom_call_target="tpu_custom_call" | custom-call | tf_op jit(solution)/shard_map/attend/pallas_call | solution.py:236
  78.1 0.2 collective-permute-start.23
  78.4 1.1 collective-permute-done.23
  79.6 1.0 collective-permute-start.24
  80.6 4.9 %collective-permute-done.24 = f32[136,128]{1,0:T(8,128)S(1)} collective-permute-done((f32[136,128]{1,0:T(8,128)S(1)}, f32[136,128]{1,0:T(8,128)S(1)}, u32[]{:S(2)}, u32[]{:S(2)}) %collective-permute-start.24) | collective-permute-done | bytes 69664 | tf_op jit(solution)/shard_map/ppermute | solution.py:37
  85.6 1.5 %collective-permute-start.27 = (f32[136,128]{1,0:T(8,128)S(1)}, f32[136,128]{1,0:T(8,128)S(1)}, u32[]{:S(2)}, u32[]{:S(2)}) collective-permute-start(f32[136,128]{1,0:T(8,128)S(1)} %add_select_fusion.1), channel_id=1, source_target_pairs={{0,16},{1,129},{2,18},{3,131},{4,20},{5,133},{6,22},{7,135},{8,24}... | collective-permute-start | bytes 208904 | tf_op jit(solution)/shard_map/ppermute | solution.py:37
  87.1 1.3 %collective-permute-start.26 = (f32[136,128]{1,0:T(8,128)S(1)}, f32[136,128]{1,0:T(8,128)S(1)}, u32[]{:S(2)}, u32[]{:S(2)}) collective-permute-start(f32[136,128]{1,0:T(8,128)S(1)} %add_select_fusion.1), channel_id=1, source_target_pairs={{0,16},{1,193},{2,18},{3,195},{4,20},{5,197},{6,22},{7,199},{8,24}... | collective-permute-start | bytes 208904 | tf_op jit(solution)/shard_map/ppermute | solution.py:37
  88.5 0.7 collective-permute-start.25
  89.2 3.0 %collective-permute-done.27 = f32[136,128]{1,0:T(8,128)S(1)} collective-permute-done((f32[136,128]{1,0:T(8,128)S(1)}, f32[136,128]{1,0:T(8,128)S(1)}, u32[]{:S(2)}, u32[]{:S(2)}) %collective-permute-start.27) | collective-permute-done | bytes 69664 | tf_op jit(solution)/shard_map/ppermute | solution.py:37
  92.1 0.6 collective-permute-done.26
  92.9 0.2 collective-permute-done.28
  93.1 1.0 output_own.3.term_ref
  94.0 0.3 collective-permute-done.29.oth_ref
  94.3 1.0 output.3
  95.3 3.6 %collective-permute-start.30 = (f32[16,1024]{1,0:T(8,128)S(1)}, f32[16,1024]{1,0:T(8,128)S(1)}, u32[]{:S(2)}, u32[]{:S(2)}) collective-permute-start(f32[16,1024]{1,0:T(8,128)S(1)} %output.3), channel_id=1, source_target_pairs={{0,16},{1,15},{2,18},{3,5},{4,20},{5,3},{6,22},{7,9},{8,24},{9,7},... | collective-permute-start | bytes 196616 | tf_op jit(solution)/shard_map/ppermute | solution.py:37
  98.9 2.5 %collective-permute-done.30 = f32[16,1024]{1,0:T(8,128)S(1)} collective-permute-done((f32[16,1024]{1,0:T(8,128)S(1)}, f32[16,1024]{1,0:T(8,128)S(1)}, u32[]{:S(2)}, u32[]{:S(2)}) %collective-permute-start.30) | collective-permute-done | bytes 65568 | tf_op jit(solution)/shard_map/ppermute | solution.py:37
  101.4 1.5 %collective-permute-start.33 = (f32[16,1024]{1,0:T(8,128)S(1)}, f32[16,1024]{1,0:T(8,128)S(1)}, u32[]{:S(2)}, u32[]{:S(2)}) collective-permute-start(f32[16,1024]{1,0:T(8,128)S(1)} %add.120), channel_id=1, source_target_pairs={{0,16},{1,5},{2,18},{3,15},{4,20},{5,9},{6,22},{7,3},{8,24},{9,13}... | collective-permute-start | bytes 196616 | tf_op jit(solution)/shard_map/ppermute | solution.py:37
  102.9 3.1 %collective-permute-start.32 = (f32[16,1024]{1,0:T(8,128)S(1)}, f32[16,1024]{1,0:T(8,128)S(1)}, u32[]{:S(2)}, u32[]{:S(2)}) collective-permute-start(f32[16,1024]{1,0:T(8,128)S(1)} %add.120), channel_id=1, source_target_pairs={{0,16},{1,3},{2,18},{3,1},{4,20},{5,7},{6,22},{7,5},{8,24},{9,11},... | collective-permute-start | bytes 196616 | tf_op jit(solution)/shard_map/ppermute | solution.py:37
  105.9 1.9 %collective-permute-start.31 = (f32[16,1024]{1,0:T(8,128)S(1)}, f32[16,1024]{1,0:T(8,128)S(1)}, u32[]{:S(2)}, u32[]{:S(2)}) collective-permute-start(f32[16,1024]{1,0:T(8,128)S(1)} %add.120), channel_id=1, source_target_pairs={{0,16},{1,7},{2,18},{3,13},{4,20},{5,11},{6,22},{7,1},{8,24},{9,15... | collective-permute-start | bytes 196616 | tf_op jit(solution)/shard_map/ppermute | solution.py:37
  107.9 0.2 collective-permute-done.33
  108.0 2.3 %collective-permute-done.32 = f32[16,1024]{1,0:T(8,128)S(1)} collective-permute-done((f32[16,1024]{1,0:T(8,128)S(1)}, f32[16,1024]{1,0:T(8,128)S(1)}, u32[]{:S(2)}, u32[]{:S(2)}) %collective-permute-start.32) | collective-permute-done | bytes 65568 | tf_op jit(solution)/shard_map/ppermute | solution.py:37
  110.3 1.9 %collective-permute-done.31 = f32[16,1024]{1,0:T(8,128)S(1)} collective-permute-done((f32[16,1024]{1,0:T(8,128)S(1)}, f32[16,1024]{1,0:T(8,128)S(1)}, u32[]{:S(2)}, u32[]{:S(2)}) %collective-permute-start.31) | collective-permute-done | bytes 65568 | tf_op jit(solution)/shard_map/ppermute | solution.py:37
  112.2 0.6 fusion.1
  (53 shorter events, 1.8 us)
Async XLA Ops:
  0.0 9.6 %copy-start.5 = (s32[8]{0:T(128)S(1)}, s32[8]{0:T(128)}, u32[]{:S(2)}) copy-start(s32[8]{0:T(128)} %len_ref.3) | copy-start | bytes 100
  0.0 9.6 %copy-start.2 = (bf16[1,1,8,1024,256]{4,3,2,1,0:T(8,128)(2,1)S(1)}, bf16[1,1,8,1024,256]{4,3,2,1,0:T(8,128)(2,1)}, u32[]{:S(2)}) copy-start(bf16[1,1,8,1024,256]{4,3,2,1,0:T(8,128)(2,1)} %param.13) | copy-start | bytes 12582916
  3.6 13.4 %copy-start = (bf16[1,2048,1024]{2,1,0:T(8,128)(2,1)S(1)}, bf16[1,2048,1024]{2,1,0:T(8,128)(2,1)}, u32[]{:S(2)}) copy-start(bf16[1,2048,1024]{2,1,0:T(8,128)(2,1)} %param.12) | copy-start | bytes 12582916
  3.6 1.4 %collective-permute-start = (f32[16,1280]{1,0:T(8,128)S(1)}, f32[16,1280]{1,0:T(8,128)S(1)}, u32[]{:S(2)}, u32[]{:S(2)}) collective-permute-start(f32[16,1280]{1,0:T(8,128)S(1)} %get-tuple-element.18), channel_id=1, source_target_pairs={{0,16},{1,17},{2,18},{3,19},{4,20},{5,21},{6,22},{7,23},{8,24},{9,... | collective-permute-start | bytes 245768 | tf_op jit(solution)/shard_map/ppermute | solution.py:37
  5.0 1.4 %collective-permute-start.1 = (f32[16,1280]{1,0:T(8,128)S(1)}, f32[16,1280]{1,0:T(8,128)S(1)}, u32[]{:S(2)}, u32[]{:S(2)}) collective-permute-start(f32[16,1280]{1,0:T(8,128)S(1)} %add.95), channel_id=1, source_target_pairs={{0,32},{1,17},{2,34},{3,19},{4,36},{5,21},{6,38},{7,23},{8,40},{9,... | collective-permute-start | bytes 245768 | tf_op jit(solution)/shard_map/ppermute | solution.py:37
  6.4 1.4 %collective-permute-start.4 = (f32[16,1280]{1,0:T(8,128)S(1)}, f32[16,1280]{1,0:T(8,128)S(1)}, u32[]{:S(2)}, u32[]{:S(2)}) collective-permute-start(f32[16,1280]{1,0:T(8,128)S(1)} %add.96), channel_id=1, source_target_pairs={{0,128},{1,17},{2,130},{3,19},{4,132},{5,21},{6,134},{7,23},{8,136... | collective-permute-start | bytes 245768 | tf_op jit(solution)/shard_map/ppermute | solution.py:37
  6.6 1.3 %collective-permute-start.3 = (f32[16,1280]{1,0:T(8,128)S(1)}, f32[16,1280]{1,0:T(8,128)S(1)}, u32[]{:S(2)}, u32[]{:S(2)}) collective-permute-start(f32[16,1280]{1,0:T(8,128)S(1)} %add.96), channel_id=1, source_target_pairs={{0,192},{1,17},{2,194},{3,19},{4,196},{5,21},{6,198},{7,23},{8,200... | collective-permute-start | bytes 245768 | tf_op jit(solution)/shard_map/ppermute | solution.py:37
  7.0 1.3 %collective-permute-start.2 = (f32[16,1280]{1,0:T(8,128)S(1)}, f32[16,1280]{1,0:T(8,128)S(1)}, u32[]{:S(2)}, u32[]{:S(2)}) collective-permute-start(f32[16,1280]{1,0:T(8,128)S(1)} %add.96), channel_id=1, source_target_pairs={{0,64},{1,17},{2,66},{3,19},{4,68},{5,21},{6,70},{7,23},{8,72},{9,... | collective-permute-start | bytes 245768 | tf_op jit(solution)/shard_map/ppermute | solution.py:37
  8.3 1.4 %collective-permute-start.5 = (f32[16,1280]{1,0:T(8,128)S(1)}, f32[16,1280]{1,0:T(8,128)S(1)}, u32[]{:S(2)}, u32[]{:S(2)}) collective-permute-start(f32[16,1280]{1,0:T(8,128)S(1)} %add_add_fusion.1.own_ref), channel_id=1, source_target_pairs={{0,16},{1,17},{2,18},{3,19},{4,20},{5,21},{6,22},{7,23},{8,24},{9,... | collective-permute-start | bytes 245768 | tf_op jit(solution)/shard_map/ppermute | solution.py:37
  11.8 1.3 %collective-permute-start.6 = (f32[136,128]{1,0:T(8,128)S(1)}, f32[136,128]{1,0:T(8,128)S(1)}, u32[]{:S(2)}, u32[]{:S(2)}) collective-permute-start(f32[136,128]{1,0:T(8,128)S(1)} %get-tuple-element.20), channel_id=1, source_target_pairs={{0,16},{1,17},{2,18},{3,19},{4,20},{5,21},{6,22},{7,23},{8,24},{9,... | collective-permute-start | bytes 208904 | tf_op jit(solution)/shard_map/ppermute | solution.py:37
  13.3 1.3 %collective-permute-start.7 = (f32[136,128]{1,0:T(8,128)S(1)}, f32[136,128]{1,0:T(8,128)S(1)}, u32[]{:S(2)}, u32[]{:S(2)}) collective-permute-start(f32[136,128]{1,0:T(8,128)S(1)} %add_select_fusion.5), channel_id=1, source_target_pairs={{0,32},{1,17},{2,34},{3,19},{4,36},{5,21},{6,38},{7,23},{8,40},{9,... | collective-permute-start | bytes 208904 | tf_op jit(solution)/shard_map/ppermute | solution.py:37
  14.7 1.3 %collective-permute-start.10 = (f32[136,128]{1,0:T(8,128)S(1)}, f32[136,128]{1,0:T(8,128)S(1)}, u32[]{:S(2)}, u32[]{:S(2)}) collective-permute-start(f32[136,128]{1,0:T(8,128)S(1)} %add_select_fusion.4), channel_id=1, source_target_pairs={{0,128},{1,17},{2,130},{3,19},{4,132},{5,21},{6,134},{7,23},{8,136... | collective-permute-start | bytes 208904 | tf_op jit(solution)/shard_map/ppermute | solution.py:37
  15.0 1.3 %collective-permute-start.9 = (f32[136,128]{1,0:T(8,128)S(1)}, f32[136,128]{1,0:T(8,128)S(1)}, u32[]{:S(2)}, u32[]{:S(2)}) collective-permute-start(f32[136,128]{1,0:T(8,128)S(1)} %add_select_fusion.4), channel_id=1, source_target_pairs={{0,192},{1,17},{2,194},{3,19},{4,196},{5,21},{6,198},{7,23},{8,200... | collective-permute-start | bytes 208904 | tf_op jit(solution)/shard_map/ppermute | solution.py:37
  15.3 1.3 %collective-permute-start.8 = (f32[136,128]{1,0:T(8,128)S(1)}, f32[136,128]{1,0:T(8,128)S(1)}, u32[]{:S(2)}, u32[]{:S(2)}) collective-permute-start(f32[136,128]{1,0:T(8,128)S(1)} %add_select_fusion.4), channel_id=1, source_target_pairs={{0,64},{1,17},{2,66},{3,19},{4,68},{5,21},{6,70},{7,23},{8,72},{9,... | collective-permute-start | bytes 208904 | tf_op jit(solution)/shard_map/ppermute | solution.py:37
  16.7 1.3 %collective-permute-start.11 = (f32[136,128]{1,0:T(8,128)S(1)}, f32[136,128]{1,0:T(8,128)S(1)}, u32[]{:S(2)}, u32[]{:S(2)}) collective-permute-start(f32[136,128]{1,0:T(8,128)S(1)} %add_select_fusion.3.own_ref), channel_id=1, source_target_pairs={{0,16},{1,17},{2,18},{3,19},{4,20},{5,21},{6,22},{7,23},{8,24},{9,... | collective-permute-start | bytes 208904 | tf_op jit(solution)/shard_map/ppermute | solution.py:37
  17.0 41.1 %copy-start.6 = (bf16[2,8,1024]{2,1,0:T(8,128)(2,1)S(1)}, bf16[2,8,1024]{2,1,0:T(8,128)(2,1)}, u32[]{:S(2)}) copy-start(bf16[2,8,1024]{2,1,0:T(8,128)(2,1)} %param.7) | copy-start | bytes 98308
  17.0 41.2 %copy-start.1 = (bf16[1,1024,2048]{2,1,0:T(8,128)(2,1)S(1)}, bf16[1,1024,2048]{2,1,0:T(8,128)(2,1)}, u32[]{:S(2)}) copy-start(bf16[1,1024,2048]{2,1,0:T(8,128)(2,1)} %param.10) | copy-start | bytes 12582916
  17.0 41.2 %copy-start.3 = (bf16[1,1024,1,256]{3,1,2,0:T(8,128)(2,1)S(1)}, bf16[1,1024,1,256]{3,1,2,0:T(8,128)(2,1)}, u32[]{:S(2)}) copy-start(bf16[1,1024,1,256]{3,1,2,0:T(8,128)(2,1)} %param.11) | copy-start | bytes 1572868
  17.0 41.2 %copy-start.4 = (bf16[1,1024]{1,0:T(2,128)(2,1)S(1)}, bf16[1,1024]{1,0:T(2,128)(2,1)}, u32[]{:S(2)}) copy-start(bf16[1,1024]{1,0:T(2,128)(2,1)} %gain_ref.1) | copy-start | bytes 6148
  19.0 30.1 %collective-permute-start.13 = (f32[16,1024]{1,0:T(8,128)S(1)}, f32[16,1024]{1,0:T(8,128)S(1)}, u32[]{:S(2)}, u32[]{:S(2)}) collective-permute-start(f32[16,1024]{1,0:T(8,128)S(1)} %output.2), channel_id=1, source_target_pairs={{0,15},{1,14},{2,5},{3,4},{4,3},{5,2},{6,9},{7,8},{8,7},{9,6},{10,... | collective-permute-start | bytes 196616 | tf_op jit(solution)/shard_map/ppermute | solution.py:37
  46.6 4.3 %collective-permute-start.12 = (f32[16,1024]{1,0:T(8,128)S(1)}, f32[16,1024]{1,0:T(8,128)S(1)}, u32[]{:S(2)}, u32[]{:S(2)}) collective-permute-start(f32[16,1024]{1,0:T(8,128)S(1)} %output.2), channel_id=1, source_target_pairs={{0,1},{1,0},{2,3},{3,2},{4,5},{5,4},{6,7},{7,6},{8,9},{9,8},{10,11... | collective-permute-start | bytes 196616 | tf_op jit(solution)/shard_map/ppermute | solution.py:37
  50.9 6.4 %collective-permute-start.16 = (f32[16,1024]{1,0:T(8,128)S(1)}, f32[16,1024]{1,0:T(8,128)S(1)}, u32[]{:S(2)}, u32[]{:S(2)}) collective-permute-start(f32[16,1024]{1,0:T(8,128)S(1)} %add.105), channel_id=1, source_target_pairs={{0,16},{1,5},{2,18},{3,15},{4,20},{5,9},{6,22},{7,3},{8,24},{9,13}... | collective-permute-start | bytes 196616 | tf_op jit(solution)/shard_map/ppermute | solution.py:37
  50.9 6.4 %collective-permute-start.15 = (f32[16,1024]{1,0:T(8,128)S(1)}, f32[16,1024]{1,0:T(8,128)S(1)}, u32[]{:S(2)}, u32[]{:S(2)}) collective-permute-start(f32[16,1024]{1,0:T(8,128)S(1)} %add.105), channel_id=1, source_target_pairs={{0,16},{1,3},{2,18},{3,1},{4,20},{5,7},{6,22},{7,5},{8,24},{9,11},... | collective-permute-start | bytes 196616 | tf_op jit(solution)/shard_map/ppermute | solution.py:37
  51.3 6.8 %collective-permute-start.14 = (f32[16,1024]{1,0:T(8,128)S(1)}, f32[16,1024]{1,0:T(8,128)S(1)}, u32[]{:S(2)}, u32[]{:S(2)}) collective-permute-start(f32[16,1024]{1,0:T(8,128)S(1)} %add.105), channel_id=1, source_target_pairs={{0,16},{1,7},{2,18},{3,13},{4,20},{5,11},{6,22},{7,1},{8,24},{9,15... | collective-permute-start | bytes 196616 | tf_op jit(solution)/shard_map/ppermute | solution.py:37
  59.1 1.4 %collective-permute-start.17 = (f32[16,1280]{1,0:T(8,128)S(1)}, f32[16,1280]{1,0:T(8,128)S(1)}, u32[]{:S(2)}, u32[]{:S(2)}) collective-permute-start(f32[16,1280]{1,0:T(8,128)S(1)} %get-tuple-element.22.first_ref), channel_id=1, source_target_pairs={{0,16},{1,17},{2,18},{3,19},{4,20},{5,21},{6,22},{7,23},{8,24},{9,... | collective-permute-start | bytes 245768 | tf_op jit(solution)/shard_map/ppermute | solution.py:37
  60.5 6.1 %collective-permute-start.18 = (f32[16,1280]{1,0:T(8,128)S(1)}, f32[16,1280]{1,0:T(8,128)S(1)}, u32[]{:S(2)}, u32[]{:S(2)}) collective-permute-start(f32[16,1280]{1,0:T(8,128)S(1)} %add.110), channel_id=1, source_target_pairs={{0,16},{1,33},{2,18},{3,35},{4,20},{5,37},{6,22},{7,39},{8,24},{9,... | collective-permute-start | bytes 245768 | tf_op jit(solution)/shard_map/ppermute | solution.py:37
  66.6 6.1 %collective-permute-start.21 = (f32[16,1280]{1,0:T(8,128)S(1)}, f32[16,1280]{1,0:T(8,128)S(1)}, u32[]{:S(2)}, u32[]{:S(2)}) collective-permute-start(f32[16,1280]{1,0:T(8,128)S(1)} %add.111), channel_id=1, source_target_pairs={{0,16},{1,129},{2,18},{3,131},{4,20},{5,133},{6,22},{7,135},{8,24}... | collective-permute-start | bytes 245768 | tf_op jit(solution)/shard_map/ppermute | solution.py:37
  68.9 5.7 %collective-permute-start.20 = (f32[16,1280]{1,0:T(8,128)S(1)}, f32[16,1280]{1,0:T(8,128)S(1)}, u32[]{:S(2)}, u32[]{:S(2)}) collective-permute-start(f32[16,1280]{1,0:T(8,128)S(1)} %add.111), channel_id=1, source_target_pairs={{0,16},{1,193},{2,18},{3,195},{4,20},{5,197},{6,22},{7,199},{8,24}... | collective-permute-start | bytes 245768 | tf_op jit(solution)/shard_map/ppermute | solution.py:37
  70.1 4.4 %collective-permute-start.19 = (f32[16,1280]{1,0:T(8,128)S(1)}, f32[16,1280]{1,0:T(8,128)S(1)}, u32[]{:S(2)}, u32[]{:S(2)}) collective-permute-start(f32[16,1280]{1,0:T(8,128)S(1)} %add.111), channel_id=1, source_target_pairs={{0,16},{1,65},{2,18},{3,67},{4,20},{5,69},{6,22},{7,71},{8,24},{9,... | collective-permute-start | bytes 245768 | tf_op jit(solution)/shard_map/ppermute | solution.py:37
  74.6 1.4 %collective-permute-start.22 = (f32[16,1280]{1,0:T(8,128)S(1)}, f32[16,1280]{1,0:T(8,128)S(1)}, u32[]{:S(2)}, u32[]{:S(2)}) collective-permute-start(f32[16,1280]{1,0:T(8,128)S(1)} %add_add_fusion.own_ref), channel_id=1, source_target_pairs={{0,16},{1,17},{2,18},{3,19},{4,20},{5,21},{6,22},{7,23},{8,24},{9,... | collective-permute-start | bytes 245768 | tf_op jit(solution)/shard_map/ppermute | solution.py:37
  78.1 1.3 %collective-permute-start.23 = (f32[136,128]{1,0:T(8,128)S(1)}, f32[136,128]{1,0:T(8,128)S(1)}, u32[]{:S(2)}, u32[]{:S(2)}) collective-permute-start(f32[136,128]{1,0:T(8,128)S(1)} %get-tuple-element.25), channel_id=1, source_target_pairs={{0,16},{1,17},{2,18},{3,19},{4,20},{5,21},{6,22},{7,23},{8,24},{9,... | collective-permute-start | bytes 208904 | tf_op jit(solution)/shard_map/ppermute | solution.py:37
  79.6 5.9 %collective-permute-start.24 = (f32[136,128]{1,0:T(8,128)S(1)}, f32[136,128]{1,0:T(8,128)S(1)}, u32[]{:S(2)}, u32[]{:S(2)}) collective-permute-start(f32[136,128]{1,0:T(8,128)S(1)} %add_select_fusion.2), channel_id=1, source_target_pairs={{0,16},{1,33},{2,18},{3,35},{4,20},{5,37},{6,22},{7,39},{8,24},{9,... | collective-permute-start | bytes 208904 | tf_op jit(solution)/shard_map/ppermute | solution.py:37
  85.6 6.5 %collective-permute-start.27 = (f32[136,128]{1,0:T(8,128)S(1)}, f32[136,128]{1,0:T(8,128)S(1)}, u32[]{:S(2)}, u32[]{:S(2)}) collective-permute-start(f32[136,128]{1,0:T(8,128)S(1)} %add_select_fusion.1), channel_id=1, source_target_pairs={{0,16},{1,129},{2,18},{3,131},{4,20},{5,133},{6,22},{7,135},{8,24}... | collective-permute-start | bytes 208904 | tf_op jit(solution)/shard_map/ppermute | solution.py:37
  87.1 5.6 %collective-permute-start.26 = (f32[136,128]{1,0:T(8,128)S(1)}, f32[136,128]{1,0:T(8,128)S(1)}, u32[]{:S(2)}, u32[]{:S(2)}) collective-permute-start(f32[136,128]{1,0:T(8,128)S(1)} %add_select_fusion.1), channel_id=1, source_target_pairs={{0,16},{1,193},{2,18},{3,195},{4,20},{5,197},{6,22},{7,199},{8,24}... | collective-permute-start | bytes 208904 | tf_op jit(solution)/shard_map/ppermute | solution.py:37
  88.5 4.3 %collective-permute-start.25 = (f32[136,128]{1,0:T(8,128)S(1)}, f32[136,128]{1,0:T(8,128)S(1)}, u32[]{:S(2)}, u32[]{:S(2)}) collective-permute-start(f32[136,128]{1,0:T(8,128)S(1)} %add_select_fusion.1), channel_id=1, source_target_pairs={{0,16},{1,65},{2,18},{3,67},{4,20},{5,69},{6,22},{7,71},{8,24},{9,... | collective-permute-start | bytes 208904 | tf_op jit(solution)/shard_map/ppermute | solution.py:37
  89.2 3.9 %collective-permute-start.28 = (bf16[16,1024]{1,0:T(8,128)(2,1)S(1)}, bf16[16,1024]{1,0:T(8,128)(2,1)S(1)}, u32[]{:S(2)}, u32[]{:S(2)}) collective-permute-start(bf16[16,1024]{1,0:T(8,128)(2,1)S(1)} %add_convert_fusion.1.hidden_ref), channel_id=1, source_target_pairs={{0,1},{1,0},{2,3},{3,2},{4,5},{5,4},{6,7},{7,6},{8,9},{9,8},{10,11... | collective-permute-start | bytes 98312 | tf_op jit(solution)/shard_map/ppermute | solution.py:250
  93.1 1.3 %collective-permute-start.29 = (f32[136,128]{1,0:T(8,128)S(1)}, f32[136,128]{1,0:T(8,128)S(1)}, u32[]{:S(2)}, u32[]{:S(2)}) collective-permute-start(f32[136,128]{1,0:T(8,128)S(1)} %add_select_fusion.own_ref), channel_id=1, source_target_pairs={{0,16},{1,17},{2,18},{3,19},{4,20},{5,21},{6,22},{7,23},{8,24},{9,... | collective-permute-start | bytes 208904 | tf_op jit(solution)/shard_map/ppermute | solution.py:37
  95.3 6.1 %collective-permute-start.30 = (f32[16,1024]{1,0:T(8,128)S(1)}, f32[16,1024]{1,0:T(8,128)S(1)}, u32[]{:S(2)}, u32[]{:S(2)}) collective-permute-start(f32[16,1024]{1,0:T(8,128)S(1)} %output.3), channel_id=1, source_target_pairs={{0,16},{1,15},{2,18},{3,5},{4,20},{5,3},{6,22},{7,9},{8,24},{9,7},... | collective-permute-start | bytes 196616 | tf_op jit(solution)/shard_map/ppermute | solution.py:37
  101.4 6.6 %collective-permute-start.33 = (f32[16,1024]{1,0:T(8,128)S(1)}, f32[16,1024]{1,0:T(8,128)S(1)}, u32[]{:S(2)}, u32[]{:S(2)}) collective-permute-start(f32[16,1024]{1,0:T(8,128)S(1)} %add.120), channel_id=1, source_target_pairs={{0,16},{1,5},{2,18},{3,15},{4,20},{5,9},{6,22},{7,3},{8,24},{9,13}... | collective-permute-start | bytes 196616 | tf_op jit(solution)/shard_map/ppermute | solution.py:37
  102.9 7.4 %collective-permute-start.32 = (f32[16,1024]{1,0:T(8,128)S(1)}, f32[16,1024]{1,0:T(8,128)S(1)}, u32[]{:S(2)}, u32[]{:S(2)}) collective-permute-start(f32[16,1024]{1,0:T(8,128)S(1)} %add.120), channel_id=1, source_target_pairs={{0,16},{1,3},{2,18},{3,1},{4,20},{5,7},{6,22},{7,5},{8,24},{9,11},... | collective-permute-start | bytes 196616 | tf_op jit(solution)/shard_map/ppermute | solution.py:37
  105.9 6.2 %collective-permute-start.31 = (f32[16,1024]{1,0:T(8,128)S(1)}, f32[16,1024]{1,0:T(8,128)S(1)}, u32[]{:S(2)}, u32[]{:S(2)}) collective-permute-start(f32[16,1024]{1,0:T(8,128)S(1)} %add.120), channel_id=1, source_target_pairs={{0,16},{1,7},{2,18},{3,13},{4,20},{5,11},{6,22},{7,1},{8,24},{9,15... | collective-permute-start | bytes 196616 | tf_op jit(solution)/shard_map/ppermute | solution.py:37

commit v4 on v3

--- a/solution.py
+++ b/solution.py
@@ -202,6 +202,10 @@
     out_ref[...] = term_ref[...] + output_half(1 - ids_ref[1], oth_ref, w_ref)
 
 
+def add_kernel(left_ref, right_ref, out_ref):
+    out_ref[...] = left_ref[...] + right_ref[...]
+
+
 def merge(*parts):
     tops = [part[HEAD_DIM : HEAD_DIM + 1] for part in parts]
     top = functools.reduce(jnp.maximum, tops)
@@ -232,7 +236,7 @@
     row_shape = jax.ShapeDtypeStruct((ROWS, width), F32)
     scaled_shape = jax.ShapeDtypeStruct((ROWS, width), BF16)
 
-    def call(kernel, name, out_shape, in_specs, *args, scratch=()):
+    def call(kernel, name, out_shape, in_specs, *args, scratch=(), cost=None):
         return pl.pallas_call(
             kernel,
             out_shape=out_shape,
@@ -240,11 +244,12 @@
             out_specs=jax.tree.map(lambda _: VMEM, out_shape),
             scratch_shapes=scratch,
             compiler_params=pltpu.CompilerParams(vmem_limit_bytes=24 * 2**20),
+            cost_estimate=cost,
             name=name,
         )(*args)
 
-    def rest_of_layer(mine, oth, cache, active, extra=None):
-        own = over_chips(mine + other_core(oth), add, active)
+    def rest_of_layer(own, cache, active, extra=None):
+        own = over_chips(own, add, active)
         if extra is not None:
             own, extra = lax.optimization_barrier((own, extra))
             extra = lax.ppermute(extra, "section", [(0, 1), (1, 0)])
@@ -284,7 +289,11 @@
             pltpu.SemaphoreType.DMA((3 + FETCHES,)),
         ],
     )
-    partial, _ = rest_of_layer(mine, oth, cache, 0)
+    own = call(
+        add_kernel, "add_first", payload, [VMEM, VMEM], mine, other_core(oth),
+        cost=pl.CostEstimate(flops=2 * 10**10, bytes_accessed=10**8, transcendentals=0),
+    )
+    partial, _ = rest_of_layer(own, cache, 0)
     pair = permute(partial, lambda x, y, c, z, s: (x, y, c, z, 1 - s))
     pair = pair + permute(partial, lambda x, y, c, z, s: (x, y, c, z + (1 if z % 2 else -1), 1 - s))
     hidden = (hidden.astype(F32) + over_pairs(pair, 1)).astype(BF16)
@@ -296,7 +305,7 @@
         project_own_kernel, "project_own", payload, [SMEM] + [VMEM] * 4,
         ids, scaled, oth, w_query, w_keyval,
     )
-    partial, first = rest_of_layer(mine, oth, cache, 1, hidden)
+    partial, first = rest_of_layer(mine + other_core(oth), cache, 1, hidden)
     pair = partial + permute(partial, lambda x, y, c, z, s: (x, y, c, z + (1 if z % 2 else -1), s), 1)
     second = (hidden.astype(F32) + over_pairs(pair, 1)).astype(BF16)
     result = jnp.where(section_id == 0, first, second)

time: 113 us -> 113 us (level)
    pallas_call x9 -> x10, Pallas kernels: 13.7 us -> 13.4 us  [call(): pl.pallas_call(kernel, out_shape=out_shape, in_specs=in_specs, out_specs=...]
where the time goes in v4:
time: 113 us; the launch traced here: 112 us
  starting transfers between devices  53.5 us (47%)
  waiting for transfers between devices  43.8 us (39%)
  Pallas kernels  13.4 us (12%)
  other arithmetic  1.47 us (1%)
    ppermute x33, starting transfers between devices, permute(): return lax.ppermute(value, ('kvseq', 'kvhead', 'section'), pairs)  53.5 us
    ppermute x33, waiting for transfers between devices, permute(): return lax.ppermute(value, ('kvseq', 'kvhead', 'section'), pairs)  43.7 us
    pallas_call x10, Pallas kernels, call(): pl.pallas_call(kernel, out_shape=out_shape, in_specs=in_specs, out_specs=...  13.4 us
  transfers between devices with their start and end apart: 34, of which 31 were waited for; matrix products, arithmetic and copies ran while one was open for 0% of the time, Pallas kernels for 3%

profile of v4, /device:TPU:24, one launch (start us, length us, event | category | flops | bytes accessed | tf_op | source)
XLA Modules:
  0.0 112.5 jit_solution(14736333986683404057)
XLA Ops:
  0.1 3.2 %project_first.1 = (f32[16,1280]{1,0:T(8,128)S(1)}, f32[16,1280]{1,0:T(8,128)S(1)}) custom-call(s32[2]{0:T(128)S(1)} %pad_add_fusion.ids_ref, bf16[16,1024]{1,0:T(8,128)(2,1)} %bitcast.64, bf16[1,1024]{1,0:T(2,128)(2,1)} %gain_ref.1, bf16[1024,2048]{1,0:T(8,128)(2,1)} %bitcast.56, bf16[1024,256]{1,0:T(8,128)(2,1)} %bitcast.61), custom_call_target="tpu_custom_call" | custom-call | tf_op jit(solution)/shard_map/project_first/pallas_call | solution.py:240
  3.4 1.3 %collective-permute-done.right_ref = f32[16,1280]{1,0:T(8,128)S(1)} collective-permute-done((f32[16,1280]{1,0:T(8,128)S(1)}, f32[16,1280]{1,0:T(8,128)S(1)}, u32[]{:S(2)}, u32[]{:S(2)}) %collective-permute-start) | collective-permute-done | bytes 81952 | tf_op jit(solution)/shard_map/ppermute | solution.py:37
  4.7 0.2 collective-permute-start.1
  4.9 1.1 collective-permute-done.1
  6.0 0.2 collective-permute-start.4
  6.3 0.4 collective-permute-start.3
  6.8 0.6 collective-permute-done.4
  7.6 0.4 collective-permute-done.2
  7.9 0.2 collective-permute-start.5
  8.2 1.1 collective-permute-done.5.oth_ref
  9.3 2.2 %attend.2 = (f32[136,128]{1,0:T(8,128)S(1)}, f32[136,128]{1,0:T(8,128)S(1)}) custom-call(s32[2]{0:T(128)S(1)} %pad_add_fusion.ids_ref, s32[8]{0:T(128)S(1)} %copy-done.5, f32[16,1280]{1,0:T(8,128)S(1)} %add_add_fusion.1.own_ref, f32[16,1280]{1,0:T(8,128)S(1)} %collective-permute-done.5.oth_ref, bf16[8,1024,256]{2,1,0:T(8,128)(2,1)S(1)} %bitcast.59), custom_call_target="tpu_custom_call" | custom-call | tf_op jit(solution)/shard_map/attend/pallas_call | solution.py:240
  11.5 0.2 collective-permute-start.6
  11.7 1.1 collective-permute-done.6
  12.9 0.2 collective-permute-start.7
  13.2 1.1 collective-permute-done.7
  14.4 0.2 collective-permute-start.10
  14.7 0.4 collective-permute-start.9
  15.0 0.2 collective-permute-start.8
  15.2 0.6 collective-permute-done.10
  15.8 0.2 collective-permute-done.9
  15.9 0.4 collective-permute-done.8
  16.4 0.2 collective-permute-start.11
  16.7 1.0 output_own.2.term_ref
  17.7 1.0 output.2
  18.7 27.5 %collective-permute-start.13 = (f32[16,1024]{1,0:T(8,128)S(1)}, f32[16,1024]{1,0:T(8,128)S(1)}, u32[]{:S(2)}, u32[]{:S(2)}) collective-permute-start(f32[16,1024]{1,0:T(8,128)S(1)} %output.2), channel_id=1, source_target_pairs={{0,15},{1,14},{2,5},{3,4},{4,3},{5,2},{6,9},{7,8},{8,7},{9,6},{10,... | collective-permute-start | bytes 196616 | tf_op jit(solution)/shard_map/ppermute | solution.py:37
  46.3 2.5 %collective-permute-done.13 = f32[16,1024]{1,0:T(8,128)S(1)} collective-permute-done((f32[16,1024]{1,0:T(8,128)S(1)}, f32[16,1024]{1,0:T(8,128)S(1)}, u32[]{:S(2)}, u32[]{:S(2)}) %collective-permute-start.13) | collective-permute-done | bytes 65568 | tf_op jit(solution)/shard_map/ppermute | solution.py:37
  48.8 1.8 %collective-permute-done.12 = f32[16,1024]{1,0:T(8,128)S(1)} collective-permute-done((f32[16,1024]{1,0:T(8,128)S(1)}, f32[16,1024]{1,0:T(8,128)S(1)}, u32[]{:S(2)}, u32[]{:S(2)}) %collective-permute-start.12) | collective-permute-done | bytes 65568 | tf_op jit(solution)/shard_map/ppermute | solution.py:37
  50.6 0.3 collective-permute-start.15
  51.0 3.1 %collective-permute-start.14 = (f32[16,1024]{1,0:T(8,128)S(1)}, f32[16,1024]{1,0:T(8,128)S(1)}, u32[]{:S(2)}, u32[]{:S(2)}) collective-permute-start(f32[16,1024]{1,0:T(8,128)S(1)} %add.101), channel_id=1, source_target_pairs={{0,16},{1,7},{2,18},{3,13},{4,20},{5,11},{6,22},{7,1},{8,24},{9,15... | collective-permute-start | bytes 196616 | tf_op jit(solution)/shard_map/ppermute | solution.py:37
  54.1 2.9 %collective-permute-done.16 = f32[16,1024]{1,0:T(8,128)S(1)} collective-permute-done((f32[16,1024]{1,0:T(8,128)S(1)}, f32[16,1024]{1,0:T(8,128)S(1)}, u32[]{:S(2)}, u32[]{:S(2)}) %collective-permute-start.16) | collective-permute-done | bytes 65568 | tf_op jit(solution)/shard_map/ppermute | solution.py:37
  57.0 0.8 collective-permute-done.14
  57.8 1.0 project.1
  58.9 1.0 project_own.1
  59.8 0.3 collective-permute-done.17
  60.1 1.0 collective-permute-start.18
  61.2 5.1 %collective-permute-done.18 = f32[16,1280]{1,0:T(8,128)S(1)} collective-permute-done((f32[16,1280]{1,0:T(8,128)S(1)}, f32[16,1280]{1,0:T(8,128)S(1)}, u32[]{:S(2)}, u32[]{:S(2)}) %collective-permute-start.18) | collective-permute-done | bytes 81952 | tf_op jit(solution)/shard_map/ppermute | solution.py:37
  66.3 2.2 %collective-permute-start.21 = (f32[16,1280]{1,0:T(8,128)S(1)}, f32[16,1280]{1,0:T(8,128)S(1)}, u32[]{:S(2)}, u32[]{:S(2)}) collective-permute-start(f32[16,1280]{1,0:T(8,128)S(1)} %add.107), channel_id=1, source_target_pairs={{0,16},{1,129},{2,18},{3,131},{4,20},{5,133},{6,22},{7,135},{8,24}... | collective-permute-start | bytes 245768 | tf_op jit(solution)/shard_map/ppermute | solution.py:37
  68.6 1.2 %collective-permute-start.20 = (f32[16,1280]{1,0:T(8,128)S(1)}, f32[16,1280]{1,0:T(8,128)S(1)}, u32[]{:S(2)}, u32[]{:S(2)}) collective-permute-start(f32[16,1280]{1,0:T(8,128)S(1)} %add.107), channel_id=1, source_target_pairs={{0,16},{1,193},{2,18},{3,195},{4,20},{5,197},{6,22},{7,199},{8,24}... | collective-permute-start | bytes 245768 | tf_op jit(solution)/shard_map/ppermute | solution.py:37
  69.9 2.6 %collective-permute-done.21 = f32[16,1280]{1,0:T(8,128)S(1)} collective-permute-done((f32[16,1280]{1,0:T(8,128)S(1)}, f32[16,1280]{1,0:T(8,128)S(1)}, u32[]{:S(2)}, u32[]{:S(2)}) %collective-permute-start.21) | collective-permute-done | bytes 81952 | tf_op jit(solution)/shard_map/ppermute | solution.py:37
  72.4 1.8 %collective-permute-done.20 = f32[16,1280]{1,0:T(8,128)S(1)} collective-permute-done((f32[16,1280]{1,0:T(8,128)S(1)}, f32[16,1280]{1,0:T(8,128)S(1)}, u32[]{:S(2)}, u32[]{:S(2)}) %collective-permute-start.20) | collective-permute-done | bytes 81952 | tf_op jit(solution)/shard_map/ppermute | solution.py:37
  74.3 1.3 %collective-permute-done.22.oth_ref = f32[16,1280]{1,0:T(8,128)S(1)} collective-permute-done((f32[16,1280]{1,0:T(8,128)S(1)}, f32[16,1280]{1,0:T(8,128)S(1)}, u32[]{:S(2)}, u32[]{:S(2)}) %collective-permute-start.22) | collective-permute-done | bytes 81952 | tf_op jit(solution)/shard_map/ppermute | solution.py:37
  75.6 2.2 %attend.3 = (f32[136,128]{1,0:T(8,128)S(1)}, f32[136,128]{1,0:T(8,128)S(1)}) custom-call(s32[2]{0:T(128)S(1)} %pad_add_fusion.ids_ref, s32[8]{0:T(128)S(1)} %copy-done.5, f32[16,1280]{1,0:T(8,128)S(1)} %add_add_fusion.own_ref, f32[16,1280]{1,0:T(8,128)S(1)} %collective-permute-done.22.oth_ref, bf16[8,1024,256]{2,1,0:T(8,128)(2,1)S(1)} %bitcast.60), custom_call_target="tpu_custom_call" | custom-call | tf_op jit(solution)/shard_map/attend/pallas_call | solution.py:240
  77.8 0.2 collective-permute-start.23
  78.0 1.1 collective-permute-done.23
  79.2 1.0 collective-permute-start.24
  80.3 4.9 %collective-permute-done.24 = f32[136,128]{1,0:T(8,128)S(1)} collective-permute-done((f32[136,128]{1,0:T(8,128)S(1)}, f32[136,128]{1,0:T(8,128)S(1)}, u32[]{:S(2)}, u32[]{:S(2)}) %collective-permute-start.24) | collective-permute-done | bytes 69664 | tf_op jit(solution)/shard_map/ppermute | solution.py:37
  85.2 1.5 %collective-permute-start.27 = (f32[136,128]{1,0:T(8,128)S(1)}, f32[136,128]{1,0:T(8,128)S(1)}, u32[]{:S(2)}, u32[]{:S(2)}) collective-permute-start(f32[136,128]{1,0:T(8,128)S(1)} %add_select_fusion.1), channel_id=1, source_target_pairs={{0,16},{1,129},{2,18},{3,131},{4,20},{5,133},{6,22},{7,135},{8,24}... | collective-permute-start | bytes 208904 | tf_op jit(solution)/shard_map/ppermute | solution.py:37
  86.8 1.3 %collective-permute-start.26 = (f32[136,128]{1,0:T(8,128)S(1)}, f32[136,128]{1,0:T(8,128)S(1)}, u32[]{:S(2)}, u32[]{:S(2)}) collective-permute-start(f32[136,128]{1,0:T(8,128)S(1)} %add_select_fusion.1), channel_id=1, source_target_pairs={{0,16},{1,193},{2,18},{3,195},{4,20},{5,197},{6,22},{7,199},{8,24}... | collective-permute-start | bytes 208904 | tf_op jit(solution)/shard_map/ppermute | solution.py:37
  88.1 0.7 collective-permute-start.25
  88.8 3.0 %collective-permute-done.27 = f32[136,128]{1,0:T(8,128)S(1)} collective-permute-done((f32[136,128]{1,0:T(8,128)S(1)}, f32[136,128]{1,0:T(8,128)S(1)}, u32[]{:S(2)}, u32[]{:S(2)}) %collective-permute-start.27) | collective-permute-done | bytes 69664 | tf_op jit(solution)/shard_map/ppermute | solution.py:37
  91.8 0.6 collective-permute-done.26
  92.6 0.2 collective-permute-done.28
  92.7 1.0 output_own.3.term_ref
  93.7 0.3 collective-permute-done.29.oth_ref
  94.0 1.0 output.3
  95.0 3.6 %collective-permute-start.30 = (f32[16,1024]{1,0:T(8,128)S(1)}, f32[16,1024]{1,0:T(8,128)S(1)}, u32[]{:S(2)}, u32[]{:S(2)}) collective-permute-start(f32[16,1024]{1,0:T(8,128)S(1)} %output.3), channel_id=1, source_target_pairs={{0,16},{1,15},{2,18},{3,5},{4,20},{5,3},{6,22},{7,9},{8,24},{9,7},... | collective-permute-start | bytes 196616 | tf_op jit(solution)/shard_map/ppermute | solution.py:37
  98.6 2.5 %collective-permute-done.30 = f32[16,1024]{1,0:T(8,128)S(1)} collective-permute-done((f32[16,1024]{1,0:T(8,128)S(1)}, f32[16,1024]{1,0:T(8,128)S(1)}, u32[]{:S(2)}, u32[]{:S(2)}) %collective-permute-start.30) | collective-permute-done | bytes 65568 | tf_op jit(solution)/shard_map/ppermute | solution.py:37
  101.1 1.5 %collective-permute-start.33 = (f32[16,1024]{1,0:T(8,128)S(1)}, f32[16,1024]{1,0:T(8,128)S(1)}, u32[]{:S(2)}, u32[]{:S(2)}) collective-permute-start(f32[16,1024]{1,0:T(8,128)S(1)} %add.116), channel_id=1, source_target_pairs={{0,16},{1,5},{2,18},{3,15},{4,20},{5,9},{6,22},{7,3},{8,24},{9,13}... | collective-permute-start | bytes 196616 | tf_op jit(solution)/shard_map/ppermute | solution.py:37
  102.6 3.0 %collective-permute-start.32 = (f32[16,1024]{1,0:T(8,128)S(1)}, f32[16,1024]{1,0:T(8,128)S(1)}, u32[]{:S(2)}, u32[]{:S(2)}) collective-permute-start(f32[16,1024]{1,0:T(8,128)S(1)} %add.116), channel_id=1, source_target_pairs={{0,16},{1,3},{2,18},{3,1},{4,20},{5,7},{6,22},{7,5},{8,24},{9,11},... | collective-permute-start | bytes 196616 | tf_op jit(solution)/shard_map/ppermute | solution.py:37
  105.6 1.9 %collective-permute-start.31 = (f32[16,1024]{1,0:T(8,128)S(1)}, f32[16,1024]{1,0:T(8,128)S(1)}, u32[]{:S(2)}, u32[]{:S(2)}) collective-permute-start(f32[16,1024]{1,0:T(8,128)S(1)} %add.116), channel_id=1, source_target_pairs={{0,16},{1,7},{2,18},{3,13},{4,20},{5,11},{6,22},{7,1},{8,24},{9,15... | collective-permute-start | bytes 196616 | tf_op jit(solution)/shard_map/ppermute | solution.py:37
  107.5 0.2 collective-permute-done.33
  107.7 2.3 %collective-permute-done.32 = f32[16,1024]{1,0:T(8,128)S(1)} collective-permute-done((f32[16,1024]{1,0:T(8,128)S(1)}, f32[16,1024]{1,0:T(8,128)S(1)}, u32[]{:S(2)}, u32[]{:S(2)}) %collective-permute-start.32) | collective-permute-done | bytes 65568 | tf_op jit(solution)/shard_map/ppermute | solution.py:37
  110.0 1.9 %collective-permute-done.31 = f32[16,1024]{1,0:T(8,128)S(1)} collective-permute-done((f32[16,1024]{1,0:T(8,128)S(1)}, f32[16,1024]{1,0:T(8,128)S(1)}, u32[]{:S(2)}, u32[]{:S(2)}) %collective-permute-start.31) | collective-permute-done | bytes 65568 | tf_op jit(solution)/shard_map/ppermute | solution.py:37
  111.9 0.6 fusion.1
  (53 shorter events, 1.8 us)
Async XLA Ops:
  3.3 1.4 %collective-permute-start = (f32[16,1280]{1,0:T(8,128)S(1)}, f32[16,1280]{1,0:T(8,128)S(1)}, u32[]{:S(2)}, u32[]{:S(2)}) collective-permute-start(f32[16,1280]{1,0:T(8,128)S(1)} %get-tuple-element.18), channel_id=1, source_target_pairs={{0,16},{1,17},{2,18},{3,19},{4,20},{5,21},{6,22},{7,23},{8,24},{9,... | collective-permute-start | bytes 245768 | tf_op jit(solution)/shard_map/ppermute | solution.py:37
  4.6 4.7 %copy-start.2 = (bf16[1,1,8,1024,256]{4,3,2,1,0:T(8,128)(2,1)S(1)}, bf16[1,1,8,1024,256]{4,3,2,1,0:T(8,128)(2,1)}, u32[]{:S(2)}) copy-start(bf16[1,1,8,1024,256]{4,3,2,1,0:T(8,128)(2,1)} %param.13) | copy-start | bytes 12582916
  4.6 4.7 %copy-start.5 = (s32[8]{0:T(128)S(1)}, s32[8]{0:T(128)}, u32[]{:S(2)}) copy-start(s32[8]{0:T(128)} %len_ref.3) | copy-start | bytes 100
  4.7 12.0 %copy-start = (bf16[1,2048,1024]{2,1,0:T(8,128)(2,1)S(1)}, bf16[1,2048,1024]{2,1,0:T(8,128)(2,1)}, u32[]{:S(2)}) copy-start(bf16[1,2048,1024]{2,1,0:T(8,128)(2,1)} %param.12) | copy-start | bytes 12582916
  4.7 1.4 %collective-permute-start.1 = (f32[16,1280]{1,0:T(8,128)S(1)}, f32[16,1280]{1,0:T(8,128)S(1)}, u32[]{:S(2)}, u32[]{:S(2)}) collective-permute-start(f32[16,1280]{1,0:T(8,128)S(1)} %add_first.1), channel_id=1, source_target_pairs={{0,32},{1,17},{2,34},{3,19},{4,36},{5,21},{6,38},{7,23},{8,40},{9,... | collective-permute-start | bytes 245768 | tf_op jit(solution)/shard_map/ppermute | solution.py:37
  6.0 1.4 %collective-permute-start.4 = (f32[16,1280]{1,0:T(8,128)S(1)}, f32[16,1280]{1,0:T(8,128)S(1)}, u32[]{:S(2)}, u32[]{:S(2)}) collective-permute-start(f32[16,1280]{1,0:T(8,128)S(1)} %add.92), channel_id=1, source_target_pairs={{0,128},{1,17},{2,130},{3,19},{4,132},{5,21},{6,134},{7,23},{8,136... | collective-permute-start | bytes 245768 | tf_op jit(solution)/shard_map/ppermute | solution.py:37
  6.3 1.3 %collective-permute-start.3 = (f32[16,1280]{1,0:T(8,128)S(1)}, f32[16,1280]{1,0:T(8,128)S(1)}, u32[]{:S(2)}, u32[]{:S(2)}) collective-permute-start(f32[16,1280]{1,0:T(8,128)S(1)} %add.92), channel_id=1, source_target_pairs={{0,192},{1,17},{2,194},{3,19},{4,196},{5,21},{6,198},{7,23},{8,200... | collective-permute-start | bytes 245768 | tf_op jit(solution)/shard_map/ppermute | solution.py:37
  6.6 1.3 %collective-permute-start.2 = (f32[16,1280]{1,0:T(8,128)S(1)}, f32[16,1280]{1,0:T(8,128)S(1)}, u32[]{:S(2)}, u32[]{:S(2)}) collective-permute-start(f32[16,1280]{1,0:T(8,128)S(1)} %add.92), channel_id=1, source_target_pairs={{0,64},{1,17},{2,66},{3,19},{4,68},{5,21},{6,70},{7,23},{8,72},{9,... | collective-permute-start | bytes 245768 | tf_op jit(solution)/shard_map/ppermute | solution.py:37
  7.9 1.4 %collective-permute-start.5 = (f32[16,1280]{1,0:T(8,128)S(1)}, f32[16,1280]{1,0:T(8,128)S(1)}, u32[]{:S(2)}, u32[]{:S(2)}) collective-permute-start(f32[16,1280]{1,0:T(8,128)S(1)} %add_add_fusion.1.own_ref), channel_id=1, source_target_pairs={{0,16},{1,17},{2,18},{3,19},{4,20},{5,21},{6,22},{7,23},{8,24},{9,... | collective-permute-start | bytes 245768 | tf_op jit(solution)/shard_map/ppermute | solution.py:37
  11.5 1.3 %collective-permute-start.6 = (f32[136,128]{1,0:T(8,128)S(1)}, f32[136,128]{1,0:T(8,128)S(1)}, u32[]{:S(2)}, u32[]{:S(2)}) collective-permute-start(f32[136,128]{1,0:T(8,128)S(1)} %get-tuple-element.20), channel_id=1, source_target_pairs={{0,16},{1,17},{2,18},{3,19},{4,20},{5,21},{6,22},{7,23},{8,24},{9,... | collective-permute-start | bytes 208904 | tf_op jit(solution)/shard_map/ppermute | solution.py:37
  12.9 1.3 %collective-permute-start.7 = (f32[136,128]{1,0:T(8,128)S(1)}, f32[136,128]{1,0:T(8,128)S(1)}, u32[]{:S(2)}, u32[]{:S(2)}) collective-permute-start(f32[136,128]{1,0:T(8,128)S(1)} %add_select_fusion.5), channel_id=1, source_target_pairs={{0,32},{1,17},{2,34},{3,19},{4,36},{5,21},{6,38},{7,23},{8,40},{9,... | collective-permute-start | bytes 208904 | tf_op jit(solution)/shard_map/ppermute | solution.py:37
  14.4 1.3 %collective-permute-start.10 = (f32[136,128]{1,0:T(8,128)S(1)}, f32[136,128]{1,0:T(8,128)S(1)}, u32[]{:S(2)}, u32[]{:S(2)}) collective-permute-start(f32[136,128]{1,0:T(8,128)S(1)} %add_select_fusion.4), channel_id=1, source_target_pairs={{0,128},{1,17},{2,130},{3,19},{4,132},{5,21},{6,134},{7,23},{8,136... | collective-permute-start | bytes 208904 | tf_op jit(solution)/shard_map/ppermute | solution.py:37
  14.7 1.3 %collective-permute-start.9 = (f32[136,128]{1,0:T(8,128)S(1)}, f32[136,128]{1,0:T(8,128)S(1)}, u32[]{:S(2)}, u32[]{:S(2)}) collective-permute-start(f32[136,128]{1,0:T(8,128)S(1)} %add_select_fusion.4), channel_id=1, source_target_pairs={{0,192},{1,17},{2,194},{3,19},{4,196},{5,21},{6,198},{7,23},{8,200... | collective-permute-start | bytes 208904 | tf_op jit(solution)/shard_map/ppermute | solution.py:37
  15.0 1.3 %collective-permute-start.8 = (f32[136,128]{1,0:T(8,128)S(1)}, f32[136,128]{1,0:T(8,128)S(1)}, u32[]{:S(2)}, u32[]{:S(2)}) collective-permute-start(f32[136,128]{1,0:T(8,128)S(1)} %add_select_fusion.4), channel_id=1, source_target_pairs={{0,64},{1,17},{2,66},{3,19},{4,68},{5,21},{6,70},{7,23},{8,72},{9,... | collective-permute-start | bytes 208904 | tf_op jit(solution)/shard_map/ppermute | solution.py:37
  16.4 1.3 %collective-permute-start.11 = (f32[136,128]{1,0:T(8,128)S(1)}, f32[136,128]{1,0:T(8,128)S(1)}, u32[]{:S(2)}, u32[]{:S(2)}) collective-permute-start(f32[136,128]{1,0:T(8,128)S(1)} %add_select_fusion.3.own_ref), channel_id=1, source_target_pairs={{0,16},{1,17},{2,18},{3,19},{4,20},{5,21},{6,22},{7,23},{8,24},{9,... | collective-permute-start | bytes 208904 | tf_op jit(solution)/shard_map/ppermute | solution.py:37
  16.6 41.1 %copy-start.6 = (bf16[2,8,1024]{2,1,0:T(8,128)(2,1)S(1)}, bf16[2,8,1024]{2,1,0:T(8,128)(2,1)}, u32[]{:S(2)}) copy-start(bf16[2,8,1024]{2,1,0:T(8,128)(2,1)} %param.7) | copy-start | bytes 98308
  16.6 41.1 %copy-start.1 = (bf16[1,1024,2048]{2,1,0:T(8,128)(2,1)S(1)}, bf16[1,1024,2048]{2,1,0:T(8,128)(2,1)}, u32[]{:S(2)}) copy-start(bf16[1,1024,2048]{2,1,0:T(8,128)(2,1)} %param.10) | copy-start | bytes 12582916
  16.6 41.2 %copy-start.3 = (bf16[1,1024,1,256]{3,1,2,0:T(8,128)(2,1)S(1)}, bf16[1,1024,1,256]{3,1,2,0:T(8,128)(2,1)}, u32[]{:S(2)}) copy-start(bf16[1,1024,1,256]{3,1,2,0:T(8,128)(2,1)} %param.11) | copy-start | bytes 1572868
  16.6 41.2 %copy-start.4 = (bf16[1,1024]{1,0:T(2,128)(2,1)S(1)}, bf16[1,1024]{1,0:T(2,128)(2,1)}, u32[]{:S(2)}) copy-start(bf16[1,1024]{1,0:T(2,128)(2,1)} %gain_ref.1) | copy-start | bytes 6148
  18.7 30.1 %collective-permute-start.13 = (f32[16,1024]{1,0:T(8,128)S(1)}, f32[16,1024]{1,0:T(8,128)S(1)}, u32[]{:S(2)}, u32[]{:S(2)}) collective-permute-start(f32[16,1024]{1,0:T(8,128)S(1)} %output.2), channel_id=1, source_target_pairs={{0,15},{1,14},{2,5},{3,4},{4,3},{5,2},{6,9},{7,8},{8,7},{9,6},{10,... | collective-permute-start | bytes 196616 | tf_op jit(solution)/shard_map/ppermute | solution.py:37
  46.3 4.3 %collective-permute-start.12 = (f32[16,1024]{1,0:T(8,128)S(1)}, f32[16,1024]{1,0:T(8,128)S(1)}, u32[]{:S(2)}, u32[]{:S(2)}) collective-permute-start(f32[16,1024]{1,0:T(8,128)S(1)} %output.2), channel_id=1, source_target_pairs={{0,1},{1,0},{2,3},{3,2},{4,5},{5,4},{6,7},{7,6},{8,9},{9,8},{10,11... | collective-permute-start | bytes 196616 | tf_op jit(solution)/shard_map/ppermute | solution.py:37
  50.5 6.4 %collective-permute-start.16 = (f32[16,1024]{1,0:T(8,128)S(1)}, f32[16,1024]{1,0:T(8,128)S(1)}, u32[]{:S(2)}, u32[]{:S(2)}) collective-permute-start(f32[16,1024]{1,0:T(8,128)S(1)} %add.101), channel_id=1, source_target_pairs={{0,16},{1,5},{2,18},{3,15},{4,20},{5,9},{6,22},{7,3},{8,24},{9,13}... | collective-permute-start | bytes 196616 | tf_op jit(solution)/shard_map/ppermute | solution.py:37
  50.6 6.4 %collective-permute-start.15 = (f32[16,1024]{1,0:T(8,128)S(1)}, f32[16,1024]{1,0:T(8,128)S(1)}, u32[]{:S(2)}, u32[]{:S(2)}) collective-permute-start(f32[16,1024]{1,0:T(8,128)S(1)} %add.101), channel_id=1, source_target_pairs={{0,16},{1,3},{2,18},{3,1},{4,20},{5,7},{6,22},{7,5},{8,24},{9,11},... | collective-permute-start | bytes 196616 | tf_op jit(solution)/shard_map/ppermute | solution.py:37
  51.0 6.8 %collective-permute-start.14 = (f32[16,1024]{1,0:T(8,128)S(1)}, f32[16,1024]{1,0:T(8,128)S(1)}, u32[]{:S(2)}, u32[]{:S(2)}) collective-permute-start(f32[16,1024]{1,0:T(8,128)S(1)} %add.101), channel_id=1, source_target_pairs={{0,16},{1,7},{2,18},{3,13},{4,20},{5,11},{6,22},{7,1},{8,24},{9,15... | collective-permute-start | bytes 196616 | tf_op jit(solution)/shard_map/ppermute | solution.py:37
  58.8 1.4 %collective-permute-start.17 = (f32[16,1280]{1,0:T(8,128)S(1)}, f32[16,1280]{1,0:T(8,128)S(1)}, u32[]{:S(2)}, u32[]{:S(2)}) collective-permute-start(f32[16,1280]{1,0:T(8,128)S(1)} %get-tuple-element.22.first_ref), channel_id=1, source_target_pairs={{0,16},{1,17},{2,18},{3,19},{4,20},{5,21},{6,22},{7,23},{8,24},{9,... | collective-permute-start | bytes 245768 | tf_op jit(solution)/shard_map/ppermute | solution.py:37
  60.1 6.1 %collective-permute-start.18 = (f32[16,1280]{1,0:T(8,128)S(1)}, f32[16,1280]{1,0:T(8,128)S(1)}, u32[]{:S(2)}, u32[]{:S(2)}) collective-permute-start(f32[16,1280]{1,0:T(8,128)S(1)} %add.106), channel_id=1, source_target_pairs={{0,16},{1,33},{2,18},{3,35},{4,20},{5,37},{6,22},{7,39},{8,24},{9,... | collective-permute-start | bytes 245768 | tf_op jit(solution)/shard_map/ppermute | solution.py:37
  66.3 6.1 %collective-permute-start.21 = (f32[16,1280]{1,0:T(8,128)S(1)}, f32[16,1280]{1,0:T(8,128)S(1)}, u32[]{:S(2)}, u32[]{:S(2)}) collective-permute-start(f32[16,1280]{1,0:T(8,128)S(1)} %add.107), channel_id=1, source_target_pairs={{0,16},{1,129},{2,18},{3,131},{4,20},{5,133},{6,22},{7,135},{8,24}... | collective-permute-start | bytes 245768 | tf_op jit(solution)/shard_map/ppermute | solution.py:37
  68.6 5.7 %collective-permute-start.20 = (f32[16,1280]{1,0:T(8,128)S(1)}, f32[16,1280]{1,0:T(8,128)S(1)}, u32[]{:S(2)}, u32[]{:S(2)}) collective-permute-start(f32[16,1280]{1,0:T(8,128)S(1)} %add.107), channel_id=1, source_target_pairs={{0,16},{1,193},{2,18},{3,195},{4,20},{5,197},{6,22},{7,199},{8,24}... | collective-permute-start | bytes 245768 | tf_op jit(solution)/shard_map/ppermute | solution.py:37
  69.8 4.4 %collective-permute-start.19 = (f32[16,1280]{1,0:T(8,128)S(1)}, f32[16,1280]{1,0:T(8,128)S(1)}, u32[]{:S(2)}, u32[]{:S(2)}) collective-permute-start(f32[16,1280]{1,0:T(8,128)S(1)} %add.107), channel_id=1, source_target_pairs={{0,16},{1,65},{2,18},{3,67},{4,20},{5,69},{6,22},{7,71},{8,24},{9,... | collective-permute-start | bytes 245768 | tf_op jit(solution)/shard_map/ppermute | solution.py:37
  74.2 1.4 %collective-permute-start.22 = (f32[16,1280]{1,0:T(8,128)S(1)}, f32[16,1280]{1,0:T(8,128)S(1)}, u32[]{:S(2)}, u32[]{:S(2)}) collective-permute-start(f32[16,1280]{1,0:T(8,128)S(1)} %add_add_fusion.own_ref), channel_id=1, source_target_pairs={{0,16},{1,17},{2,18},{3,19},{4,20},{5,21},{6,22},{7,23},{8,24},{9,... | collective-permute-start | bytes 245768 | tf_op jit(solution)/shard_map/ppermute | solution.py:37
  77.8 1.3 %collective-permute-start.23 = (f32[136,128]{1,0:T(8,128)S(1)}, f32[136,128]{1,0:T(8,128)S(1)}, u32[]{:S(2)}, u32[]{:S(2)}) collective-permute-start(f32[136,128]{1,0:T(8,128)S(1)} %get-tuple-element.25), channel_id=1, source_target_pairs={{0,16},{1,17},{2,18},{3,19},{4,20},{5,21},{6,22},{7,23},{8,24},{9,... | collective-permute-start | bytes 208904 | tf_op jit(solution)/shard_map/ppermute | solution.py:37
  79.2 5.9 %collective-permute-start.24 = (f32[136,128]{1,0:T(8,128)S(1)}, f32[136,128]{1,0:T(8,128)S(1)}, u32[]{:S(2)}, u32[]{:S(2)}) collective-permute-start(f32[136,128]{1,0:T(8,128)S(1)} %add_select_fusion.2), channel_id=1, source_target_pairs={{0,16},{1,33},{2,18},{3,35},{4,20},{5,37},{6,22},{7,39},{8,24},{9,... | collective-permute-start | bytes 208904 | tf_op jit(solution)/shard_map/ppermute | solution.py:37
  85.2 6.5 %collective-permute-start.27 = (f32[136,128]{1,0:T(8,128)S(1)}, f32[136,128]{1,0:T(8,128)S(1)}, u32[]{:S(2)}, u32[]{:S(2)}) collective-permute-start(f32[136,128]{1,0:T(8,128)S(1)} %add_select_fusion.1), channel_id=1, source_target_pairs={{0,16},{1,129},{2,18},{3,131},{4,20},{5,133},{6,22},{7,135},{8,24}... | collective-permute-start | bytes 208904 | tf_op jit(solution)/shard_map/ppermute | solution.py:37
  86.8 5.6 %collective-permute-start.26 = (f32[136,128]{1,0:T(8,128)S(1)}, f32[136,128]{1,0:T(8,128)S(1)}, u32[]{:S(2)}, u32[]{:S(2)}) collective-permute-start(f32[136,128]{1,0:T(8,128)S(1)} %add_select_fusion.1), channel_id=1, source_target_pairs={{0,16},{1,193},{2,18},{3,195},{4,20},{5,197},{6,22},{7,199},{8,24}... | collective-permute-start | bytes 208904 | tf_op jit(solution)/shard_map/ppermute | solution.py:37
  88.1 4.3 %collective-permute-start.25 = (f32[136,128]{1,0:T(8,128)S(1)}, f32[136,128]{1,0:T(8,128)S(1)}, u32[]{:S(2)}, u32[]{:S(2)}) collective-permute-start(f32[136,128]{1,0:T(8,128)S(1)} %add_select_fusion.1), channel_id=1, source_target_pairs={{0,16},{1,65},{2,18},{3,67},{4,20},{5,69},{6,22},{7,71},{8,24},{9,... | collective-permute-start | bytes 208904 | tf_op jit(solution)/shard_map/ppermute | solution.py:37
  88.8 3.9 %collective-permute-start.28 = (bf16[16,1024]{1,0:T(8,128)(2,1)S(1)}, bf16[16,1024]{1,0:T(8,128)(2,1)S(1)}, u32[]{:S(2)}, u32[]{:S(2)}) collective-permute-start(bf16[16,1024]{1,0:T(8,128)(2,1)S(1)} %add_convert_fusion.1.hidden_ref), channel_id=1, source_target_pairs={{0,1},{1,0},{2,3},{3,2},{4,5},{5,4},{6,7},{7,6},{8,9},{9,8},{10,11... | collective-permute-start | bytes 98312 | tf_op jit(solution)/shard_map/ppermute | solution.py:255
  92.7 1.3 %collective-permute-start.29 = (f32[136,128]{1,0:T(8,128)S(1)}, f32[136,128]{1,0:T(8,128)S(1)}, u32[]{:S(2)}, u32[]{:S(2)}) collective-permute-start(f32[136,128]{1,0:T(8,128)S(1)} %add_select_fusion.own_ref), channel_id=1, source_target_pairs={{0,16},{1,17},{2,18},{3,19},{4,20},{5,21},{6,22},{7,23},{8,24},{9,... | collective-permute-start | bytes 208904 | tf_op jit(solution)/shard_map/ppermute | solution.py:37
  95.0 6.1 %collective-permute-start.30 = (f32[16,1024]{1,0:T(8,128)S(1)}, f32[16,1024]{1,0:T(8,128)S(1)}, u32[]{:S(2)}, u32[]{:S(2)}) collective-permute-start(f32[16,1024]{1,0:T(8,128)S(1)} %output.3), channel_id=1, source_target_pairs={{0,16},{1,15},{2,18},{3,5},{4,20},{5,3},{6,22},{7,9},{8,24},{9,7},... | collective-permute-start | bytes 196616 | tf_op jit(solution)/shard_map/ppermute | solution.py:37
  101.1 6.6 %collective-permute-start.33 = (f32[16,1024]{1,0:T(8,128)S(1)}, f32[16,1024]{1,0:T(8,128)S(1)}, u32[]{:S(2)}, u32[]{:S(2)}) collective-permute-start(f32[16,1024]{1,0:T(8,128)S(1)} %add.116), channel_id=1, source_target_pairs={{0,16},{1,5},{2,18},{3,15},{4,20},{5,9},{6,22},{7,3},{8,24},{9,13}... | collective-permute-start | bytes 196616 | tf_op jit(solution)/shard_map/ppermute | solution.py:37
  102.6 7.4 %collective-permute-start.32 = (f32[16,1024]{1,0:T(8,128)S(1)}, f32[16,1024]{1,0:T(8,128)S(1)}, u32[]{:S(2)}, u32[]{:S(2)}) collective-permute-start(f32[16,1024]{1,0:T(8,128)S(1)} %add.116), channel_id=1, source_target_pairs={{0,16},{1,3},{2,18},{3,1},{4,20},{5,7},{6,22},{7,5},{8,24},{9,11},... | collective-permute-start | bytes 196616 | tf_op jit(solution)/shard_map/ppermute | solution.py:37
  105.6 6.2 %collective-permute-start.31 = (f32[16,1024]{1,0:T(8,128)S(1)}, f32[16,1024]{1,0:T(8,128)S(1)}, u32[]{:S(2)}, u32[]{:S(2)}) collective-permute-start(f32[16,1024]{1,0:T(8,128)S(1)} %add.116), channel_id=1, source_target_pairs={{0,16},{1,7},{2,18},{3,13},{4,20},{5,11},{6,22},{7,1},{8,24},{9,15... | collective-permute-start | bytes 196616 | tf_op jit(solution)/shard_map/ppermute | solution.py:37

commit v5 on v4

--- a/solution.py
+++ b/solution.py
@@ -257,12 +257,12 @@
             attend_kernel, "attend", (part_shape, part_shape), [SMEM, SMEM] + [VMEM] * 3,
             ids, lengths, own, other_core(own), cache,
             scratch=[
-                pltpu.VMEM((256, HEAD_DIM), F32),
+                pltpu.VMEM((264, HEAD_DIM), F32),
                 pltpu.VMEM((2, ROWS, HEAD_DIM), F32),
                 pltpu.VMEM((8, 32, 1024), F32),
                 pltpu.VMEM((8, 32, 1024), BF16),
-                pltpu.VMEM((256, HEAD_DIM), F32),
-                pltpu.VMEM((256, HEAD_DIM), F32),
+                pltpu.VMEM((264, HEAD_DIM), F32),
+                pltpu.VMEM((264, HEAD_DIM), F32),
             ],
         )
         own = over_chips(merge(mine, other_core(oth)), merge, active)

time: 113 us -> 113 us (level)
  no operation moved by 1% of the time
where the time goes in v5:
time: 113 us; the launch traced here: 112 us
  starting transfers between devices  53.5 us (47%)
  waiting for transfers between devices  43.9 us (39%)
  Pallas kernels  13.4 us (12%)
  other arithmetic  1.47 us (1%)
    ppermute x33, starting transfers between devices, permute(): return lax.ppermute(value, ('kvseq', 'kvhead', 'section'), pairs)  53.5 us
    ppermute x33, waiting for transfers between devices, permute(): return lax.ppermute(value, ('kvseq', 'kvhead', 'section'), pairs)  43.7 us
    pallas_call x10, Pallas kernels, call(): pl.pallas_call(kernel, out_shape=out_shape, in_specs=in_specs, out_specs=...  13.4 us
  transfers between devices with their start and end apart: 34, of which 31 were waited for; matrix products, arithmetic and copies ran while one was open for 0% of the time, Pallas kernels for 3%

profile of v5, /device:TPU:24, one launch (start us, length us, event | category | flops | bytes accessed | tf_op | source)
XLA Modules:
  0.0 112.5 jit_solution(4462451766090798280)
XLA Ops:
  0.1 3.2 %project_first.1 = (f32[16,1280]{1,0:T(8,128)S(1)}, f32[16,1280]{1,0:T(8,128)S(1)}) custom-call(s32[2]{0:T(128)S(1)} %pad_add_fusion.ids_ref, bf16[16,1024]{1,0:T(8,128)(2,1)} %bitcast.64, bf16[1,1024]{1,0:T(2,128)(2,1)} %gain_ref.1, bf16[1024,2048]{1,0:T(8,128)(2,1)} %bitcast.56, bf16[1024,256]{1,0:T(8,128)(2,1)} %bitcast.61), custom_call_target="tpu_custom_call" | custom-call | tf_op jit(solution)/shard_map/project_first/pallas_call | solution.py:240
  3.4 1.3 %collective-permute-done.right_ref = f32[16,1280]{1,0:T(8,128)S(1)} collective-permute-done((f32[16,1280]{1,0:T(8,128)S(1)}, f32[16,1280]{1,0:T(8,128)S(1)}, u32[]{:S(2)}, u32[]{:S(2)}) %collective-permute-start) | collective-permute-done | bytes 81952 | tf_op jit(solution)/shard_map/ppermute | solution.py:37
  4.7 0.2 collective-permute-start.1
  4.9 1.1 collective-permute-done.1
  6.0 0.2 collective-permute-start.4
  6.3 0.4 collective-permute-start.3
  6.8 0.6 collective-permute-done.4
  7.6 0.4 collective-permute-done.2
  7.9 0.2 collective-permute-start.5
  8.2 1.1 collective-permute-done.5.oth_ref
  9.3 2.2 %attend.2 = (f32[136,128]{1,0:T(8,128)S(1)}, f32[136,128]{1,0:T(8,128)S(1)}) custom-call(s32[2]{0:T(128)S(1)} %pad_add_fusion.ids_ref, s32[8]{0:T(128)S(1)} %copy-done.5, f32[16,1280]{1,0:T(8,128)S(1)} %add_add_fusion.1.own_ref, f32[16,1280]{1,0:T(8,128)S(1)} %collective-permute-done.5.oth_ref, bf16[8,1024,256]{2,1,0:T(8,128)(2,1)S(1)} %bitcast.59), custom_call_target="tpu_custom_call" | custom-call | tf_op jit(solution)/shard_map/attend/pallas_call | solution.py:240
  11.5 0.2 collective-permute-start.6
  11.7 1.1 collective-permute-done.6
  12.9 0.2 collective-permute-start.7
  13.2 1.1 collective-permute-done.7
  14.4 0.2 collective-permute-start.10
  14.6 0.4 collective-permute-start.9
  15.0 0.2 collective-permute-start.8
  15.2 0.6 collective-permute-done.10
  15.8 0.2 collective-permute-done.9
  15.9 0.4 collective-permute-done.8
  16.4 0.2 collective-permute-start.11
  16.7 1.0 output_own.2.term_ref
  17.7 1.0 output.2
  18.7 27.5 %collective-permute-start.13 = (f32[16,1024]{1,0:T(8,128)S(1)}, f32[16,1024]{1,0:T(8,128)S(1)}, u32[]{:S(2)}, u32[]{:S(2)}) collective-permute-start(f32[16,1024]{1,0:T(8,128)S(1)} %output.2), channel_id=1, source_target_pairs={{0,15},{1,14},{2,5},{3,4},{4,3},{5,2},{6,9},{7,8},{8,7},{9,6},{10,... | collective-permute-start | bytes 196616 | tf_op jit(solution)/shard_map/ppermute | solution.py:37
  46.3 2.5 %collective-permute-done.13 = f32[16,1024]{1,0:T(8,128)S(1)} collective-permute-done((f32[16,1024]{1,0:T(8,128)S(1)}, f32[16,1024]{1,0:T(8,128)S(1)}, u32[]{:S(2)}, u32[]{:S(2)}) %collective-permute-start.13) | collective-permute-done | bytes 65568 | tf_op jit(solution)/shard_map/ppermute | solution.py:37
  48.8 1.8 %collective-permute-done.12 = f32[16,1024]{1,0:T(8,128)S(1)} collective-permute-done((f32[16,1024]{1,0:T(8,128)S(1)}, f32[16,1024]{1,0:T(8,128)S(1)}, u32[]{:S(2)}, u32[]{:S(2)}) %collective-permute-start.12) | collective-permute-done | bytes 65568 | tf_op jit(solution)/shard_map/ppermute | solution.py:37
  50.6 0.3 collective-permute-start.15
  51.0 3.1 %collective-permute-start.14 = (f32[16,1024]{1,0:T(8,128)S(1)}, f32[16,1024]{1,0:T(8,128)S(1)}, u32[]{:S(2)}, u32[]{:S(2)}) collective-permute-start(f32[16,1024]{1,0:T(8,128)S(1)} %add.101), channel_id=1, source_target_pairs={{0,16},{1,7},{2,18},{3,13},{4,20},{5,11},{6,22},{7,1},{8,24},{9,15... | collective-permute-start | bytes 196616 | tf_op jit(solution)/shard_map/ppermute | solution.py:37
  54.1 2.9 %collective-permute-done.16 = f32[16,1024]{1,0:T(8,128)S(1)} collective-permute-done((f32[16,1024]{1,0:T(8,128)S(1)}, f32[16,1024]{1,0:T(8,128)S(1)}, u32[]{:S(2)}, u32[]{:S(2)}) %collective-permute-start.16) | collective-permute-done | bytes 65568 | tf_op jit(solution)/shard_map/ppermute | solution.py:37
  57.0 0.8 collective-permute-done.14
  57.8 1.0 project.1
  58.9 1.0 project_own.1
  59.8 0.3 collective-permute-done.17
  60.1 1.0 collective-permute-start.18
  61.2 5.1 %collective-permute-done.18 = f32[16,1280]{1,0:T(8,128)S(1)} collective-permute-done((f32[16,1280]{1,0:T(8,128)S(1)}, f32[16,1280]{1,0:T(8,128)S(1)}, u32[]{:S(2)}, u32[]{:S(2)}) %collective-permute-start.18) | collective-permute-done | bytes 81952 | tf_op jit(solution)/shard_map/ppermute | solution.py:37
  66.3 2.2 %collective-permute-start.21 = (f32[16,1280]{1,0:T(8,128)S(1)}, f32[16,1280]{1,0:T(8,128)S(1)}, u32[]{:S(2)}, u32[]{:S(2)}) collective-permute-start(f32[16,1280]{1,0:T(8,128)S(1)} %add.107), channel_id=1, source_target_pairs={{0,16},{1,129},{2,18},{3,131},{4,20},{5,133},{6,22},{7,135},{8,24}... | collective-permute-start | bytes 245768 | tf_op jit(solution)/shard_map/ppermute | solution.py:37
  68.5 1.2 %collective-permute-start.20 = (f32[16,1280]{1,0:T(8,128)S(1)}, f32[16,1280]{1,0:T(8,128)S(1)}, u32[]{:S(2)}, u32[]{:S(2)}) collective-permute-start(f32[16,1280]{1,0:T(8,128)S(1)} %add.107), channel_id=1, source_target_pairs={{0,16},{1,193},{2,18},{3,195},{4,20},{5,197},{6,22},{7,199},{8,24}... | collective-permute-start | bytes 245768 | tf_op jit(solution)/shard_map/ppermute | solution.py:37
  69.9 2.6 %collective-permute-done.21 = f32[16,1280]{1,0:T(8,128)S(1)} collective-permute-done((f32[16,1280]{1,0:T(8,128)S(1)}, f32[16,1280]{1,0:T(8,128)S(1)}, u32[]{:S(2)}, u32[]{:S(2)}) %collective-permute-start.21) | collective-permute-done | bytes 81952 | tf_op jit(solution)/shard_map/ppermute | solution.py:37
  72.4 1.7 %collective-permute-done.20 = f32[16,1280]{1,0:T(8,128)S(1)} collective-permute-done((f32[16,1280]{1,0:T(8,128)S(1)}, f32[16,1280]{1,0:T(8,128)S(1)}, u32[]{:S(2)}, u32[]{:S(2)}) %collective-permute-start.20) | collective-permute-done | bytes 81952 | tf_op jit(solution)/shard_map/ppermute | solution.py:37
  74.3 1.3 %collective-permute-done.22.oth_ref = f32[16,1280]{1,0:T(8,128)S(1)} collective-permute-done((f32[16,1280]{1,0:T(8,128)S(1)}, f32[16,1280]{1,0:T(8,128)S(1)}, u32[]{:S(2)}, u32[]{:S(2)}) %collective-permute-start.22) | collective-permute-done | bytes 81952 | tf_op jit(solution)/shard_map/ppermute | solution.py:37
  75.6 2.2 %attend.3 = (f32[136,128]{1,0:T(8,128)S(1)}, f32[136,128]{1,0:T(8,128)S(1)}) custom-call(s32[2]{0:T(128)S(1)} %pad_add_fusion.ids_ref, s32[8]{0:T(128)S(1)} %copy-done.5, f32[16,1280]{1,0:T(8,128)S(1)} %add_add_fusion.own_ref, f32[16,1280]{1,0:T(8,128)S(1)} %collective-permute-done.22.oth_ref, bf16[8,1024,256]{2,1,0:T(8,128)(2,1)S(1)} %bitcast.60), custom_call_target="tpu_custom_call" | custom-call | tf_op jit(solution)/shard_map/attend/pallas_call | solution.py:240
  77.8 0.2 collective-permute-start.23
  78.0 1.1 collective-permute-done.23
  79.2 1.0 collective-permute-start.24
  80.2 4.9 %collective-permute-done.24 = f32[136,128]{1,0:T(8,128)S(1)} collective-permute-done((f32[136,128]{1,0:T(8,128)S(1)}, f32[136,128]{1,0:T(8,128)S(1)}, u32[]{:S(2)}, u32[]{:S(2)}) %collective-permute-start.24) | collective-permute-done | bytes 69664 | tf_op jit(solution)/shard_map/ppermute | solution.py:37
  85.2 1.5 %collective-permute-start.27 = (f32[136,128]{1,0:T(8,128)S(1)}, f32[136,128]{1,0:T(8,128)S(1)}, u32[]{:S(2)}, u32[]{:S(2)}) collective-permute-start(f32[136,128]{1,0:T(8,128)S(1)} %add_select_fusion.1), channel_id=1, source_target_pairs={{0,16},{1,129},{2,18},{3,131},{4,20},{5,133},{6,22},{7,135},{8,24}... | collective-permute-start | bytes 208904 | tf_op jit(solution)/shard_map/ppermute | solution.py:37
  86.8 1.3 %collective-permute-start.26 = (f32[136,128]{1,0:T(8,128)S(1)}, f32[136,128]{1,0:T(8,128)S(1)}, u32[]{:S(2)}, u32[]{:S(2)}) collective-permute-start(f32[136,128]{1,0:T(8,128)S(1)} %add_select_fusion.1), channel_id=1, source_target_pairs={{0,16},{1,193},{2,18},{3,195},{4,20},{5,197},{6,22},{7,199},{8,24}... | collective-permute-start | bytes 208904 | tf_op jit(solution)/shard_map/ppermute | solution.py:37
  88.1 0.7 collective-permute-start.25
  88.8 3.0 %collective-permute-done.27 = f32[136,128]{1,0:T(8,128)S(1)} collective-permute-done((f32[136,128]{1,0:T(8,128)S(1)}, f32[136,128]{1,0:T(8,128)S(1)}, u32[]{:S(2)}, u32[]{:S(2)}) %collective-permute-start.27) | collective-permute-done | bytes 69664 | tf_op jit(solution)/shard_map/ppermute | solution.py:37
  91.8 0.6 collective-permute-done.26
  92.5 0.2 collective-permute-done.28
  92.7 1.0 output_own.3.term_ref
  93.7 0.3 collective-permute-done.29.oth_ref
  94.0 1.0 output.3
  95.0 3.6 %collective-permute-start.30 = (f32[16,1024]{1,0:T(8,128)S(1)}, f32[16,1024]{1,0:T(8,128)S(1)}, u32[]{:S(2)}, u32[]{:S(2)}) collective-permute-start(f32[16,1024]{1,0:T(8,128)S(1)} %output.3), channel_id=1, source_target_pairs={{0,16},{1,15},{2,18},{3,5},{4,20},{5,3},{6,22},{7,9},{8,24},{9,7},... | collective-permute-start | bytes 196616 | tf_op jit(solution)/shard_map/ppermute | solution.py:37
  98.6 2.5 %collective-permute-done.30 = f32[16,1024]{1,0:T(8,128)S(1)} collective-permute-done((f32[16,1024]{1,0:T(8,128)S(1)}, f32[16,1024]{1,0:T(8,128)S(1)}, u32[]{:S(2)}, u32[]{:S(2)}) %collective-permute-start.30) | collective-permute-done | bytes 65568 | tf_op jit(solution)/shard_map/ppermute | solution.py:37
  101.1 1.5 %collective-permute-start.33 = (f32[16,1024]{1,0:T(8,128)S(1)}, f32[16,1024]{1,0:T(8,128)S(1)}, u32[]{:S(2)}, u32[]{:S(2)}) collective-permute-start(f32[16,1024]{1,0:T(8,128)S(1)} %add.116), channel_id=1, source_target_pairs={{0,16},{1,5},{2,18},{3,15},{4,20},{5,9},{6,22},{7,3},{8,24},{9,13}... | collective-permute-start | bytes 196616 | tf_op jit(solution)/shard_map/ppermute | solution.py:37
  102.5 3.1 %collective-permute-start.32 = (f32[16,1024]{1,0:T(8,128)S(1)}, f32[16,1024]{1,0:T(8,128)S(1)}, u32[]{:S(2)}, u32[]{:S(2)}) collective-permute-start(f32[16,1024]{1,0:T(8,128)S(1)} %add.116), channel_id=1, source_target_pairs={{0,16},{1,3},{2,18},{3,1},{4,20},{5,7},{6,22},{7,5},{8,24},{9,11},... | collective-permute-start | bytes 196616 | tf_op jit(solution)/shard_map/ppermute | solution.py:37
  105.6 1.9 %collective-permute-start.31 = (f32[16,1024]{1,0:T(8,128)S(1)}, f32[16,1024]{1,0:T(8,128)S(1)}, u32[]{:S(2)}, u32[]{:S(2)}) collective-permute-start(f32[16,1024]{1,0:T(8,128)S(1)} %add.116), channel_id=1, source_target_pairs={{0,16},{1,7},{2,18},{3,13},{4,20},{5,11},{6,22},{7,1},{8,24},{9,15... | collective-permute-start | bytes 196616 | tf_op jit(solution)/shard_map/ppermute | solution.py:37
  107.5 0.2 collective-permute-done.33
  107.7 2.3 %collective-permute-done.32 = f32[16,1024]{1,0:T(8,128)S(1)} collective-permute-done((f32[16,1024]{1,0:T(8,128)S(1)}, f32[16,1024]{1,0:T(8,128)S(1)}, u32[]{:S(2)}, u32[]{:S(2)}) %collective-permute-start.32) | collective-permute-done | bytes 65568 | tf_op jit(solution)/shard_map/ppermute | solution.py:37
  109.9 1.9 %collective-permute-done.31 = f32[16,1024]{1,0:T(8,128)S(1)} collective-permute-done((f32[16,1024]{1,0:T(8,128)S(1)}, f32[16,1024]{1,0:T(8,128)S(1)}, u32[]{:S(2)}, u32[]{:S(2)}) %collective-permute-start.31) | collective-permute-done | bytes 65568 | tf_op jit(solution)/shard_map/ppermute | solution.py:37
  111.8 0.6 fusion.1
  (53 shorter events, 1.8 us)
Async XLA Ops:
  3.3 1.4 %collective-permute-start = (f32[16,1280]{1,0:T(8,128)S(1)}, f32[16,1280]{1,0:T(8,128)S(1)}, u32[]{:S(2)}, u32[]{:S(2)}) collective-permute-start(f32[16,1280]{1,0:T(8,128)S(1)} %get-tuple-element.18), channel_id=1, source_target_pairs={{0,16},{1,17},{2,18},{3,19},{4,20},{5,21},{6,22},{7,23},{8,24},{9,... | collective-permute-start | bytes 245768 | tf_op jit(solution)/shard_map/ppermute | solution.py:37
  4.6 4.7 %copy-start.2 = (bf16[1,1,8,1024,256]{4,3,2,1,0:T(8,128)(2,1)S(1)}, bf16[1,1,8,1024,256]{4,3,2,1,0:T(8,128)(2,1)}, u32[]{:S(2)}) copy-start(bf16[1,1,8,1024,256]{4,3,2,1,0:T(8,128)(2,1)} %param.13) | copy-start | bytes 12582916
  4.6 4.7 %copy-start.5 = (s32[8]{0:T(128)S(1)}, s32[8]{0:T(128)}, u32[]{:S(2)}) copy-start(s32[8]{0:T(128)} %len_ref.3) | copy-start | bytes 100
  4.7 12.0 %copy-start = (bf16[1,2048,1024]{2,1,0:T(8,128)(2,1)S(1)}, bf16[1,2048,1024]{2,1,0:T(8,128)(2,1)}, u32[]{:S(2)}) copy-start(bf16[1,2048,1024]{2,1,0:T(8,128)(2,1)} %param.12) | copy-start | bytes 12582916
  4.7 1.4 %collective-permute-start.1 = (f32[16,1280]{1,0:T(8,128)S(1)}, f32[16,1280]{1,0:T(8,128)S(1)}, u32[]{:S(2)}, u32[]{:S(2)}) collective-permute-start(f32[16,1280]{1,0:T(8,128)S(1)} %add_first.1), channel_id=1, source_target_pairs={{0,32},{1,17},{2,34},{3,19},{4,36},{5,21},{6,38},{7,23},{8,40},{9,... | collective-permute-start | bytes 245768 | tf_op jit(solution)/shard_map/ppermute | solution.py:37
  6.0 1.4 %collective-permute-start.4 = (f32[16,1280]{1,0:T(8,128)S(1)}, f32[16,1280]{1,0:T(8,128)S(1)}, u32[]{:S(2)}, u32[]{:S(2)}) collective-permute-start(f32[16,1280]{1,0:T(8,128)S(1)} %add.92), channel_id=1, source_target_pairs={{0,128},{1,17},{2,130},{3,19},{4,132},{5,21},{6,134},{7,23},{8,136... | collective-permute-start | bytes 245768 | tf_op jit(solution)/shard_map/ppermute | solution.py:37
  6.3 1.3 %collective-permute-start.3 = (f32[16,1280]{1,0:T(8,128)S(1)}, f32[16,1280]{1,0:T(8,128)S(1)}, u32[]{:S(2)}, u32[]{:S(2)}) collective-permute-start(f32[16,1280]{1,0:T(8,128)S(1)} %add.92), channel_id=1, source_target_pairs={{0,192},{1,17},{2,194},{3,19},{4,196},{5,21},{6,198},{7,23},{8,200... | collective-permute-start | bytes 245768 | tf_op jit(solution)/shard_map/ppermute | solution.py:37
  6.6 1.3 %collective-permute-start.2 = (f32[16,1280]{1,0:T(8,128)S(1)}, f32[16,1280]{1,0:T(8,128)S(1)}, u32[]{:S(2)}, u32[]{:S(2)}) collective-permute-start(f32[16,1280]{1,0:T(8,128)S(1)} %add.92), channel_id=1, source_target_pairs={{0,64},{1,17},{2,66},{3,19},{4,68},{5,21},{6,70},{7,23},{8,72},{9,... | collective-permute-start | bytes 245768 | tf_op jit(solution)/shard_map/ppermute | solution.py:37
  7.9 1.4 %collective-permute-start.5 = (f32[16,1280]{1,0:T(8,128)S(1)}, f32[16,1280]{1,0:T(8,128)S(1)}, u32[]{:S(2)}, u32[]{:S(2)}) collective-permute-start(f32[16,1280]{1,0:T(8,128)S(1)} %add_add_fusion.1.own_ref), channel_id=1, source_target_pairs={{0,16},{1,17},{2,18},{3,19},{4,20},{5,21},{6,22},{7,23},{8,24},{9,... | collective-permute-start | bytes 245768 | tf_op jit(solution)/shard_map/ppermute | solution.py:37
  11.5 1.3 %collective-permute-start.6 = (f32[136,128]{1,0:T(8,128)S(1)}, f32[136,128]{1,0:T(8,128)S(1)}, u32[]{:S(2)}, u32[]{:S(2)}) collective-permute-start(f32[136,128]{1,0:T(8,128)S(1)} %get-tuple-element.20), channel_id=1, source_target_pairs={{0,16},{1,17},{2,18},{3,19},{4,20},{5,21},{6,22},{7,23},{8,24},{9,... | collective-permute-start | bytes 208904 | tf_op jit(solution)/shard_map/ppermute | solution.py:37
  12.9 1.3 %collective-permute-start.7 = (f32[136,128]{1,0:T(8,128)S(1)}, f32[136,128]{1,0:T(8,128)S(1)}, u32[]{:S(2)}, u32[]{:S(2)}) collective-permute-start(f32[136,128]{1,0:T(8,128)S(1)} %add_select_fusion.5), channel_id=1, source_target_pairs={{0,32},{1,17},{2,34},{3,19},{4,36},{5,21},{6,38},{7,23},{8,40},{9,... | collective-permute-start | bytes 208904 | tf_op jit(solution)/shard_map/ppermute | solution.py:37
  14.4 1.3 %collective-permute-start.10 = (f32[136,128]{1,0:T(8,128)S(1)}, f32[136,128]{1,0:T(8,128)S(1)}, u32[]{:S(2)}, u32[]{:S(2)}) collective-permute-start(f32[136,128]{1,0:T(8,128)S(1)} %add_select_fusion.4), channel_id=1, source_target_pairs={{0,128},{1,17},{2,130},{3,19},{4,132},{5,21},{6,134},{7,23},{8,136... | collective-permute-start | bytes 208904 | tf_op jit(solution)/shard_map/ppermute | solution.py:37
  14.6 1.3 %collective-permute-start.9 = (f32[136,128]{1,0:T(8,128)S(1)}, f32[136,128]{1,0:T(8,128)S(1)}, u32[]{:S(2)}, u32[]{:S(2)}) collective-permute-start(f32[136,128]{1,0:T(8,128)S(1)} %add_select_fusion.4), channel_id=1, source_target_pairs={{0,192},{1,17},{2,194},{3,19},{4,196},{5,21},{6,198},{7,23},{8,200... | collective-permute-start | bytes 208904 | tf_op jit(solution)/shard_map/ppermute | solution.py:37
  15.0 1.3 %collective-permute-start.8 = (f32[136,128]{1,0:T(8,128)S(1)}, f32[136,128]{1,0:T(8,128)S(1)}, u32[]{:S(2)}, u32[]{:S(2)}) collective-permute-start(f32[136,128]{1,0:T(8,128)S(1)} %add_select_fusion.4), channel_id=1, source_target_pairs={{0,64},{1,17},{2,66},{3,19},{4,68},{5,21},{6,70},{7,23},{8,72},{9,... | collective-permute-start | bytes 208904 | tf_op jit(solution)/shard_map/ppermute | solution.py:37
  16.4 1.3 %collective-permute-start.11 = (f32[136,128]{1,0:T(8,128)S(1)}, f32[136,128]{1,0:T(8,128)S(1)}, u32[]{:S(2)}, u32[]{:S(2)}) collective-permute-start(f32[136,128]{1,0:T(8,128)S(1)} %add_select_fusion.3.own_ref), channel_id=1, source_target_pairs={{0,16},{1,17},{2,18},{3,19},{4,20},{5,21},{6,22},{7,23},{8,24},{9,... | collective-permute-start | bytes 208904 | tf_op jit(solution)/shard_map/ppermute | solution.py:37
  16.6 41.1 %copy-start.6 = (bf16[2,8,1024]{2,1,0:T(8,128)(2,1)S(1)}, bf16[2,8,1024]{2,1,0:T(8,128)(2,1)}, u32[]{:S(2)}) copy-start(bf16[2,8,1024]{2,1,0:T(8,128)(2,1)} %param.7) | copy-start | bytes 98308
  16.6 41.1 %copy-start.1 = (bf16[1,1024,2048]{2,1,0:T(8,128)(2,1)S(1)}, bf16[1,1024,2048]{2,1,0:T(8,128)(2,1)}, u32[]{:S(2)}) copy-start(bf16[1,1024,2048]{2,1,0:T(8,128)(2,1)} %param.10) | copy-start | bytes 12582916
  16.6 41.2 %copy-start.3 = (bf16[1,1024,1,256]{3,1,2,0:T(8,128)(2,1)S(1)}, bf16[1,1024,1,256]{3,1,2,0:T(8,128)(2,1)}, u32[]{:S(2)}) copy-start(bf16[1,1024,1,256]{3,1,2,0:T(8,128)(2,1)} %param.11) | copy-start | bytes 1572868
  16.6 41.2 %copy-start.4 = (bf16[1,1024]{1,0:T(2,128)(2,1)S(1)}, bf16[1,1024]{1,0:T(2,128)(2,1)}, u32[]{:S(2)}) copy-start(bf16[1,1024]{1,0:T(2,128)(2,1)} %gain_ref.1) | copy-start | bytes 6148
  18.7 30.1 %collective-permute-start.13 = (f32[16,1024]{1,0:T(8,128)S(1)}, f32[16,1024]{1,0:T(8,128)S(1)}, u32[]{:S(2)}, u32[]{:S(2)}) collective-permute-start(f32[16,1024]{1,0:T(8,128)S(1)} %output.2), channel_id=1, source_target_pairs={{0,15},{1,14},{2,5},{3,4},{4,3},{5,2},{6,9},{7,8},{8,7},{9,6},{10,... | collective-permute-start | bytes 196616 | tf_op jit(solution)/shard_map/ppermute | solution.py:37
  46.2 4.3 %collective-permute-start.12 = (f32[16,1024]{1,0:T(8,128)S(1)}, f32[16,1024]{1,0:T(8,128)S(1)}, u32[]{:S(2)}, u32[]{:S(2)}) collective-permute-start(f32[16,1024]{1,0:T(8,128)S(1)} %output.2), channel_id=1, source_target_pairs={{0,1},{1,0},{2,3},{3,2},{4,5},{5,4},{6,7},{7,6},{8,9},{9,8},{10,11... | collective-permute-start | bytes 196616 | tf_op jit(solution)/shard_map/ppermute | solution.py:37
  50.5 6.4 %collective-permute-start.16 = (f32[16,1024]{1,0:T(8,128)S(1)}, f32[16,1024]{1,0:T(8,128)S(1)}, u32[]{:S(2)}, u32[]{:S(2)}) collective-permute-start(f32[16,1024]{1,0:T(8,128)S(1)} %add.101), channel_id=1, source_target_pairs={{0,16},{1,5},{2,18},{3,15},{4,20},{5,9},{6,22},{7,3},{8,24},{9,13}... | collective-permute-start | bytes 196616 | tf_op jit(solution)/shard_map/ppermute | solution.py:37
  50.6 6.4 %collective-permute-start.15 = (f32[16,1024]{1,0:T(8,128)S(1)}, f32[16,1024]{1,0:T(8,128)S(1)}, u32[]{:S(2)}, u32[]{:S(2)}) collective-permute-start(f32[16,1024]{1,0:T(8,128)S(1)} %add.101), channel_id=1, source_target_pairs={{0,16},{1,3},{2,18},{3,1},{4,20},{5,7},{6,22},{7,5},{8,24},{9,11},... | collective-permute-start | bytes 196616 | tf_op jit(solution)/shard_map/ppermute | solution.py:37
  51.0 6.8 %collective-permute-start.14 = (f32[16,1024]{1,0:T(8,128)S(1)}, f32[16,1024]{1,0:T(8,128)S(1)}, u32[]{:S(2)}, u32[]{:S(2)}) collective-permute-start(f32[16,1024]{1,0:T(8,128)S(1)} %add.101), channel_id=1, source_target_pairs={{0,16},{1,7},{2,18},{3,13},{4,20},{5,11},{6,22},{7,1},{8,24},{9,15... | collective-permute-start | bytes 196616 | tf_op jit(solution)/shard_map/ppermute | solution.py:37
  58.8 1.4 %collective-permute-start.17 = (f32[16,1280]{1,0:T(8,128)S(1)}, f32[16,1280]{1,0:T(8,128)S(1)}, u32[]{:S(2)}, u32[]{:S(2)}) collective-permute-start(f32[16,1280]{1,0:T(8,128)S(1)} %get-tuple-element.22.first_ref), channel_id=1, source_target_pairs={{0,16},{1,17},{2,18},{3,19},{4,20},{5,21},{6,22},{7,23},{8,24},{9,... | collective-permute-start | bytes 245768 | tf_op jit(solution)/shard_map/ppermute | solution.py:37
  60.1 6.1 %collective-permute-start.18 = (f32[16,1280]{1,0:T(8,128)S(1)}, f32[16,1280]{1,0:T(8,128)S(1)}, u32[]{:S(2)}, u32[]{:S(2)}) collective-permute-start(f32[16,1280]{1,0:T(8,128)S(1)} %add.106), channel_id=1, source_target_pairs={{0,16},{1,33},{2,18},{3,35},{4,20},{5,37},{6,22},{7,39},{8,24},{9,... | collective-permute-start | bytes 245768 | tf_op jit(solution)/shard_map/ppermute | solution.py:37
  66.3 6.1 %collective-permute-start.21 = (f32[16,1280]{1,0:T(8,128)S(1)}, f32[16,1280]{1,0:T(8,128)S(1)}, u32[]{:S(2)}, u32[]{:S(2)}) collective-permute-start(f32[16,1280]{1,0:T(8,128)S(1)} %add.107), channel_id=1, source_target_pairs={{0,16},{1,129},{2,18},{3,131},{4,20},{5,133},{6,22},{7,135},{8,24}... | collective-permute-start | bytes 245768 | tf_op jit(solution)/shard_map/ppermute | solution.py:37
  68.5 5.7 %collective-permute-start.20 = (f32[16,1280]{1,0:T(8,128)S(1)}, f32[16,1280]{1,0:T(8,128)S(1)}, u32[]{:S(2)}, u32[]{:S(2)}) collective-permute-start(f32[16,1280]{1,0:T(8,128)S(1)} %add.107), channel_id=1, source_target_pairs={{0,16},{1,193},{2,18},{3,195},{4,20},{5,197},{6,22},{7,199},{8,24}... | collective-permute-start | bytes 245768 | tf_op jit(solution)/shard_map/ppermute | solution.py:37
  69.8 4.4 %collective-permute-start.19 = (f32[16,1280]{1,0:T(8,128)S(1)}, f32[16,1280]{1,0:T(8,128)S(1)}, u32[]{:S(2)}, u32[]{:S(2)}) collective-permute-start(f32[16,1280]{1,0:T(8,128)S(1)} %add.107), channel_id=1, source_target_pairs={{0,16},{1,65},{2,18},{3,67},{4,20},{5,69},{6,22},{7,71},{8,24},{9,... | collective-permute-start | bytes 245768 | tf_op jit(solution)/shard_map/ppermute | solution.py:37
  74.2 1.4 %collective-permute-start.22 = (f32[16,1280]{1,0:T(8,128)S(1)}, f32[16,1280]{1,0:T(8,128)S(1)}, u32[]{:S(2)}, u32[]{:S(2)}) collective-permute-start(f32[16,1280]{1,0:T(8,128)S(1)} %add_add_fusion.own_ref), channel_id=1, source_target_pairs={{0,16},{1,17},{2,18},{3,19},{4,20},{5,21},{6,22},{7,23},{8,24},{9,... | collective-permute-start | bytes 245768 | tf_op jit(solution)/shard_map/ppermute | solution.py:37
  77.8 1.3 %collective-permute-start.23 = (f32[136,128]{1,0:T(8,128)S(1)}, f32[136,128]{1,0:T(8,128)S(1)}, u32[]{:S(2)}, u32[]{:S(2)}) collective-permute-start(f32[136,128]{1,0:T(8,128)S(1)} %get-tuple-element.25), channel_id=1, source_target_pairs={{0,16},{1,17},{2,18},{3,19},{4,20},{5,21},{6,22},{7,23},{8,24},{9,... | collective-permute-start | bytes 208904 | tf_op jit(solution)/shard_map/ppermute | solution.py:37
  79.2 5.9 %collective-permute-start.24 = (f32[136,128]{1,0:T(8,128)S(1)}, f32[136,128]{1,0:T(8,128)S(1)}, u32[]{:S(2)}, u32[]{:S(2)}) collective-permute-start(f32[136,128]{1,0:T(8,128)S(1)} %add_select_fusion.2), channel_id=1, source_target_pairs={{0,16},{1,33},{2,18},{3,35},{4,20},{5,37},{6,22},{7,39},{8,24},{9,... | collective-permute-start | bytes 208904 | tf_op jit(solution)/shard_map/ppermute | solution.py:37
  85.2 6.5 %collective-permute-start.27 = (f32[136,128]{1,0:T(8,128)S(1)}, f32[136,128]{1,0:T(8,128)S(1)}, u32[]{:S(2)}, u32[]{:S(2)}) collective-permute-start(f32[136,128]{1,0:T(8,128)S(1)} %add_select_fusion.1), channel_id=1, source_target_pairs={{0,16},{1,129},{2,18},{3,131},{4,20},{5,133},{6,22},{7,135},{8,24}... | collective-permute-start | bytes 208904 | tf_op jit(solution)/shard_map/ppermute | solution.py:37
  86.8 5.6 %collective-permute-start.26 = (f32[136,128]{1,0:T(8,128)S(1)}, f32[136,128]{1,0:T(8,128)S(1)}, u32[]{:S(2)}, u32[]{:S(2)}) collective-permute-start(f32[136,128]{1,0:T(8,128)S(1)} %add_select_fusion.1), channel_id=1, source_target_pairs={{0,16},{1,193},{2,18},{3,195},{4,20},{5,197},{6,22},{7,199},{8,24}... | collective-permute-start | bytes 208904 | tf_op jit(solution)/shard_map/ppermute | solution.py:37
  88.1 4.3 %collective-permute-start.25 = (f32[136,128]{1,0:T(8,128)S(1)}, f32[136,128]{1,0:T(8,128)S(1)}, u32[]{:S(2)}, u32[]{:S(2)}) collective-permute-start(f32[136,128]{1,0:T(8,128)S(1)} %add_select_fusion.1), channel_id=1, source_target_pairs={{0,16},{1,65},{2,18},{3,67},{4,20},{5,69},{6,22},{7,71},{8,24},{9,... | collective-permute-start | bytes 208904 | tf_op jit(solution)/shard_map/ppermute | solution.py:37
  88.8 3.9 %collective-permute-start.28 = (bf16[16,1024]{1,0:T(8,128)(2,1)S(1)}, bf16[16,1024]{1,0:T(8,128)(2,1)S(1)}, u32[]{:S(2)}, u32[]{:S(2)}) collective-permute-start(bf16[16,1024]{1,0:T(8,128)(2,1)S(1)} %add_convert_fusion.1.hidden_ref), channel_id=1, source_target_pairs={{0,1},{1,0},{2,3},{3,2},{4,5},{5,4},{6,7},{7,6},{8,9},{9,8},{10,11... | collective-permute-start | bytes 98312 | tf_op jit(solution)/shard_map/ppermute | solution.py:255
  92.7 1.3 %collective-permute-start.29 = (f32[136,128]{1,0:T(8,128)S(1)}, f32[136,128]{1,0:T(8,128)S(1)}, u32[]{:S(2)}, u32[]{:S(2)}) collective-permute-start(f32[136,128]{1,0:T(8,128)S(1)} %add_select_fusion.own_ref), channel_id=1, source_target_pairs={{0,16},{1,17},{2,18},{3,19},{4,20},{5,21},{6,22},{7,23},{8,24},{9,... | collective-permute-start | bytes 208904 | tf_op jit(solution)/shard_map/ppermute | solution.py:37
  95.0 6.1 %collective-permute-start.30 = (f32[16,1024]{1,0:T(8,128)S(1)}, f32[16,1024]{1,0:T(8,128)S(1)}, u32[]{:S(2)}, u32[]{:S(2)}) collective-permute-start(f32[16,1024]{1,0:T(8,128)S(1)} %output.3), channel_id=1, source_target_pairs={{0,16},{1,15},{2,18},{3,5},{4,20},{5,3},{6,22},{7,9},{8,24},{9,7},... | collective-permute-start | bytes 196616 | tf_op jit(solution)/shard_map/ppermute | solution.py:37
  101.1 6.6 %collective-permute-start.33 = (f32[16,1024]{1,0:T(8,128)S(1)}, f32[16,1024]{1,0:T(8,128)S(1)}, u32[]{:S(2)}, u32[]{:S(2)}) collective-permute-start(f32[16,1024]{1,0:T(8,128)S(1)} %add.116), channel_id=1, source_target_pairs={{0,16},{1,5},{2,18},{3,15},{4,20},{5,9},{6,22},{7,3},{8,24},{9,13}... | collective-permute-start | bytes 196616 | tf_op jit(solution)/shard_map/ppermute | solution.py:37
  102.5 7.4 %collective-permute-start.32 = (f32[16,1024]{1,0:T(8,128)S(1)}, f32[16,1024]{1,0:T(8,128)S(1)}, u32[]{:S(2)}, u32[]{:S(2)}) collective-permute-start(f32[16,1024]{1,0:T(8,128)S(1)} %add.116), channel_id=1, source_target_pairs={{0,16},{1,3},{2,18},{3,1},{4,20},{5,7},{6,22},{7,5},{8,24},{9,11},... | collective-permute-start | bytes 196616 | tf_op jit(solution)/shard_map/ppermute | solution.py:37
  105.6 6.2 %collective-permute-start.31 = (f32[16,1024]{1,0:T(8,128)S(1)}, f32[16,1024]{1,0:T(8,128)S(1)}, u32[]{:S(2)}, u32[]{:S(2)}) collective-permute-start(f32[16,1024]{1,0:T(8,128)S(1)} %add.116), channel_id=1, source_target_pairs={{0,16},{1,7},{2,18},{3,13},{4,20},{5,11},{6,22},{7,1},{8,24},{9,15... | collective-permute-start | bytes 196616 | tf_op jit(solution)/shard_map/ppermute | solution.py:37

commit v6 on v5

--- a/solution.py
+++ b/solution.py
@@ -17,7 +17,8 @@
 SMEM = pl.BlockSpec(memory_space=pltpu.SMEM)
 HBM = pl.BlockSpec(memory_space=pltpu.HBM)
 HALF = 1024
-WIDE = HALF + 2 * HEAD_DIM
+WIDE = HALF + 3 * HEAD_DIM
+SQUARES = HALF + 2 * HEAD_DIM
 ROWS = 16
 FETCHES = 8
 FETCH = 128
@@ -101,55 +102,56 @@
     keyvals = jnp.dot(scaled, keyval_ref[...], preferred_element_type=F32)
     for out_ref, low in ((first_out, core == 1), (second_out, core == 0)):
         out_ref[:, :HALF] = jnp.where(low, queries[:, :HALF], queries[:, HALF:])
-        out_ref[:, HALF : HALF + HEAD_DIM] = jnp.where(
-            low, keyvals[:, :HEAD_DIM], keyvals[:, HEAD_DIM:]
-        )
-        out_ref[:, HALF + HEAD_DIM :] = jnp.broadcast_to(squares, (ROWS, HEAD_DIM))
+        out_ref[:, HALF:SQUARES] = keyvals
+        out_ref[:, SQUARES:] = jnp.broadcast_to(squares, (ROWS, HEAD_DIM))
 
 
 def project_half(half, scaled, query_ref, keyval_ref, out_ref):
     columns = pl.ds(pl.multiple_of(half * HALF, HALF), HALF)
     out_ref[:, :HALF] = jnp.dot(scaled, query_ref[:, columns], preferred_element_type=F32)
-    columns = pl.ds(pl.multiple_of(half * HEAD_DIM, HEAD_DIM), HEAD_DIM)
-    out_ref[:, HALF : HALF + HEAD_DIM] = jnp.dot(
-        scaled, keyval_ref[:, columns], preferred_element_type=F32
-    )
+    out_ref[:, HALF:SQUARES] = jnp.dot(scaled, keyval_ref[...], preferred_element_type=F32)
 
 
 def project_kernel(ids_ref, hidden_ref, gain_ref, query_ref, keyval_ref, out_ref, scaled_ref):
     scaled, squares = scale_rows(hidden_ref[...], gain_ref[...])
     scaled_ref[...] = scaled
-    out_ref[:, HALF + HEAD_DIM :] = jnp.broadcast_to(squares, (ROWS, HEAD_DIM))
+    out_ref[:, SQUARES:] = jnp.broadcast_to(squares, (ROWS, HEAD_DIM))
     project_half(1 - ids_ref[1], scaled, query_ref, keyval_ref, out_ref)
 
 
 def project_own_kernel(ids_ref, scaled_ref, first_ref, query_ref, keyval_ref, out_ref):
-    out_ref[:, HALF + HEAD_DIM :] = first_ref[:, HALF + HEAD_DIM :]
+    out_ref[:, SQUARES:] = first_ref[:, SQUARES:]
     project_half(ids_ref[1], scaled_ref[...], query_ref, keyval_ref, out_ref)
 
 
 def attend_kernel(
-    ids_ref, len_ref, own_ref, oth_ref, cache_ref, first_out, second_out,
+    ids_ref, len_ref, own_ref, cache_ref, sibling_ref, out_ref,
     q_s, kv_s, score_s, weight_s, acc_s, stat_s,
 ):
-    seq_id, core = ids_ref[0], ids_ref[1]
-    for part, ref in enumerate((own_ref, oth_ref)):
-        inv_rms = lax.rsqrt(ref[:, HALF + HEAD_DIM : HALF + HEAD_DIM + 1] / D + EPSILON)
-        queries = (ref[:, :HALF] * inv_rms * HEAD_DIM ** (-0.5)).astype(BF16).astype(F32)
-        for g in range(8):
-            q_s[pl.ds((part * 8 + g) * ROWS, ROWS), :] = queries[:, g * HEAD_DIM : (g + 1) * HEAD_DIM]
-        fresh = (ref[:, HALF : HALF + HEAD_DIM] * inv_rms).astype(BF16).astype(F32)
-        kv_s[core if part == 0 else 1 - core] = fresh
+    seq_id = ids_ref[0]
+    inv_rms = lax.rsqrt(own_ref[:, SQUARES : SQUARES + 1] / D + EPSILON)
+    queries = (own_ref[:, :HALF] * inv_rms * HEAD_DIM ** (-0.5)).astype(BF16).astype(F32)
+    for g in range(8):
+        q_s[pl.ds(g * ROWS, ROWS), :] = queries[:, g * HEAD_DIM : (g + 1) * HEAD_DIM]
+    for part in range(2):
+        start = HALF + part * HEAD_DIM
+        fresh = own_ref[:, start : start + HEAD_DIM] * inv_rms
+        kv_s[part] = fresh.astype(BF16).astype(F32)
+    blocks = (cache_ref, sibling_ref)
     for r in range(8):
-        queries = q_s[pl.ds(r, 32, stride=8), :].astype(BF16)
-        score_s[r] = lax.dot_general(
-            queries,
-            cache_ref[r, :, :HEAD_DIM],
-            (((1,), (1,)), ((), ())),
-            preferred_element_type=F32,
-        )
+        queries = q_s[pl.ds(r, 16, stride=8), :].astype(BF16)
+        for part, block in enumerate(blocks):
+            score_s[r, part * 16 : part * 16 + 16] = lax.dot_general(
+                queries,
+                block[r, :, :HEAD_DIM],
+                (((1,), (1,)), ((), ())),
+                preferred_element_type=F32,
+            )
     lane = lax.broadcasted_iota(jnp.int32, (32, HEAD_DIM), 1)
-    position = seq_id * 1024 + lax.broadcasted_iota(jnp.int32, (32, 1024), 1)
+    sibling_id = seq_id + 1 - 2 * ids_ref[1]
+    in_own = lax.broadcasted_iota(jnp.int32, (32, 1024), 0) < 16
+    position = lax.broadcasted_iota(jnp.int32, (32, 1024), 1)
+    position = position + 1024 * jnp.where(in_own, seq_id, sibling_id)
     for r in range(8):
         scores = score_s[r]
         valid = position < len_ref[r]
@@ -157,34 +159,39 @@
         weights = jnp.where(valid, jnp.exp(scores - top), 0.0)
         weight_s[r] = weights.astype(BF16)
         total = jnp.sum(weights, axis=-1, keepdims=True)
-        stat_s[pl.ds(r, 32, stride=8), :] = jnp.where(lane == 0, top, total)
+        stats = jnp.where(lane == 0, top, total)
+        for part in range(2):
+            stat_s[part, pl.ds(r, 16, stride=8), :] = stats[part * 16 : part * 16 + 16]
     for r in range(8):
-        acc_s[pl.ds(r, 32, stride=8), :] = jnp.dot(
-            weight_s[r], cache_ref[r, :, HEAD_DIM:], preferred_element_type=F32
-        )
+        for part, block in enumerate(blocks):
+            acc_s[part, pl.ds(r, 16, stride=8), :] = jnp.dot(
+                weight_s[r, part * 16 : part * 16 + 16],
+                block[r, :, HEAD_DIM:],
+                preferred_element_type=F32,
+            )
+    rows = slice(0, HEAD_DIM)
     row = lax.broadcasted_iota(jnp.int32, (HEAD_DIM, 1), 0)
     late = (row // 8) % 2 == 1
-    holder = seq_id == 0
+    holder = seq_id < 2
     lane = lax.broadcasted_iota(jnp.int32, (HEAD_DIM, HEAD_DIM), 1)
-    for part, out_ref in enumerate((first_out, second_out)):
-        rows = pl.ds(part * HEAD_DIM, HEAD_DIM)
-        queries = q_s[rows, :]
-        top, total, acc = stat_s[rows, 0:1], stat_s[rows, 1:2], acc_s[rows, :]
-        new_top, fresh = top, []
-        for t in range(2):
-            key = jnp.concatenate([kv_s[0, pl.ds(t * 8, 8), :]] * 16, axis=0)
-            score = jnp.sum(queries * key, axis=-1, keepdims=True)
-            seen = (late & holder) if t else (row >= 0) & holder
-            fresh.append((seen, score))
-            new_top = jnp.maximum(new_top, jnp.where(seen, score, NEG_FLOOR))
-        scale = jnp.exp(top - new_top)
-        acc, total = acc * scale, total * scale
-        for t, (seen, score) in enumerate(fresh):
-            weight = jnp.where(seen, jnp.exp(score - new_top), 0.0)
-            acc = acc + weight * jnp.concatenate([kv_s[1, pl.ds(t * 8, 8), :]] * 16, axis=0)
-            total = total + weight
-        out_ref[:HEAD_DIM, :] = acc.T
-        out_ref[HEAD_DIM:, :] = jnp.where(lane == 0, new_top, total).T[:STAT]
+    queries = q_s[rows, :]
+    tops = [stat_s[part, rows, 0:1] for part in range(2)]
+    new_top, found = jnp.maximum(tops[0], tops[1]), []
+    for t in range(2):
+        key = jnp.concatenate([kv_s[0, pl.ds(t * 8, 8), :]] * 16, axis=0)
+        score = jnp.sum(queries * key, axis=-1, keepdims=True)
+        seen = (late & holder) if t else (row >= 0) & holder
+        found.append((seen, score))
+        new_top = jnp.maximum(new_top, jnp.where(seen, score, NEG_FLOOR))
+    scales = [jnp.exp(top - new_top) for top in tops]
+    acc = acc_s[0, rows, :] * scales[0] + acc_s[1, rows, :] * scales[1]
+    total = stat_s[0, rows, 1:2] * scales[0] + stat_s[1, rows, 1:2] * scales[1]
+    for t, (seen, score) in enumerate(found):
+        weight = jnp.where(seen, jnp.exp(score - new_top), 0.0)
+        acc = acc + weight * jnp.concatenate([kv_s[1, pl.ds(t * 8, 8), :]] * 16, axis=0)
+        total = total + weight
+    out_ref[:HEAD_DIM, :] = acc.T
+    out_ref[HEAD_DIM:, :] = jnp.where(lane == 0, new_top, total).T[:STAT]
 
 
 def output_half(half, ref, w_ref):
@@ -248,24 +255,24 @@
             name=name,
         )(*args)
 
-    def rest_of_layer(own, cache, active, extra=None):
+    def rest_of_layer(own, sibling, active, extra=None):
         own = over_chips(own, add, active)
         if extra is not None:
             own, extra = lax.optimization_barrier((own, extra))
             extra = lax.ppermute(extra, "section", [(0, 1), (1, 0)])
-        mine, oth = call(
-            attend_kernel, "attend", (part_shape, part_shape), [SMEM, SMEM] + [VMEM] * 3,
-            ids, lengths, own, other_core(own), cache,
+        part = call(
+            attend_kernel, "attend", part_shape, [SMEM, SMEM] + [VMEM] * 3,
+            ids, lengths, own, cache, sibling,
             scratch=[
-                pltpu.VMEM((264, HEAD_DIM), F32),
+                pltpu.VMEM((136, HEAD_DIM), F32),
                 pltpu.VMEM((2, ROWS, HEAD_DIM), F32),
                 pltpu.VMEM((8, 32, 1024), F32),
                 pltpu.VMEM((8, 32, 1024), BF16),
-                pltpu.VMEM((264, HEAD_DIM), F32),
-                pltpu.VMEM((264, HEAD_DIM), F32),
+                pltpu.VMEM((2, 136, HEAD_DIM), F32),
+                pltpu.VMEM((2, 136, HEAD_DIM), F32),
             ],
         )
-        own = over_chips(merge(mine, other_core(oth)), merge, active)
+        own = over_chips(part, merge, active)
         if extra is not None:
             own, extra = lax.optimization_barrier((own, extra))
         oth = other_core(own)
@@ -293,7 +300,9 @@
         add_kernel, "add_first", payload, [VMEM, VMEM], mine, other_core(oth),
         cost=pl.CostEstimate(flops=2 * 10**10, bytes_accessed=10**8, transcendentals=0),
     )
-    partial, _ = rest_of_layer(own, cache, 0)
+    raw_cache, own = lax.optimization_barrier((kv_cache[0, 0], own))
+    sibling = in_vmem(other_core(raw_cache))
+    partial, _ = rest_of_layer(own, sibling, 0)
     pair = permute(partial, lambda x, y, c, z, s: (x, y, c, z, 1 - s))
     pair = pair + permute(partial, lambda x, y, c, z, s: (x, y, c, z + (1 if z % 2 else -1), 1 - s))
     hidden = (hidden.astype(F32) + over_pairs(pair, 1)).astype(BF16)
@@ -305,7 +314,7 @@
         project_own_kernel, "project_own", payload, [SMEM] + [VMEM] * 4,
         ids, scaled, oth, w_query, w_keyval,
     )
-    partial, first = rest_of_layer(mine + other_core(oth), cache, 1, hidden)
+    partial, first = rest_of_layer(mine + other_core(oth), sibling, 1, hidden)
     pair = partial + permute(partial, lambda x, y, c, z, s: (x, y, c, z + (1 if z % 2 else -1), s), 1)
     second = (hidden.astype(F32) + over_pairs(pair, 1)).astype(BF16)
     result = jnp.where(section_id == 0, first, second)

time: 113 us -> 111 us (0.982)
  starting transfers between devices: 53.5 us -> 47.7 us
  local copies, waits for them, and re-layouts: 0.03 us -> 2.2 us
  waiting for transfers between devices: 43.9 us -> 45.1 us
    ppermute x33 -> x30, starting transfers between devices: 53.5 us -> 47.7 us  [permute(): return lax.ppermute(value, ('kvseq', 'kvhead', 'section'), pairs)]
    unnamed x14, local copies, waits for them, and re-layouts: 0.03 us -> 2.2 us
    ppermute x33 -> x30, waiting for transfers between devices: 43.7 us -> 45 us  [permute(): return lax.ppermute(value, ('kvseq', 'kvhead', 'section'), pairs)]
  transfers between devices with their start and end apart: 34 -> 31, of which waited for: 31 -> 28; matrix products, arithmetic and copies ran while one was open for 0% -> 0% of each run, Pallas kernels for 3% -> 3%
where the time goes in v6:
time: 111 us
  starting transfers between devices  47.7 us (43%)
  waiting for transfers between devices  45.1 us (41%)
  Pallas kernels  14.2 us (13%)
  local copies, waits for them, and re-layouts  2.2 us (2%)
  other arithmetic  1.27 us (1%)
    ppermute x30, starting transfers between devices, permute(): return lax.ppermute(value, ('kvseq', 'kvhead', 'section'), pairs)  47.7 us
    ppermute x30, waiting for transfers between devices, permute(): return lax.ppermute(value, ('kvseq', 'kvhead', 'section'), pairs)  45 us
    pallas_call x10, Pallas kernels, call(): pl.pallas_call(kernel, out_shape=out_shape, in_specs=in_specs, out_specs=...  14.2 us
  transfers between devices with their start and end apart: 31, of which 28 were waited for; matrix products, arithmetic and copies ran while one was open for 0% of the time, Pallas kernels for 3%

profile of v6, /device:TPU:24, one launch (start us, length us, event | category | flops | bytes accessed | tf_op | source)
XLA Modules:
  0.0 110.7 jit_solution(12930651093028841446)
XLA Ops:
  0.1 3.2 %project_first.1 = (f32[16,1408]{1,0:T(8,128)S(1)}, f32[16,1408]{1,0:T(8,128)S(1)}) custom-call(s32[2]{0:T(128)S(1)} %pad_add_fusion.ids_ref, bf16[16,1024]{1,0:T(8,128)(2,1)} %bitcast.53, bf16[1,1024]{1,0:T(2,128)(2,1)} %gain_ref.1, bf16[1024,2048]{1,0:T(8,128)(2,1)} %bitcast.44, bf16[1024,256]{1,0:T(8,128)(2,1)} %bitcast.50), custom_call_target="tpu_custom_call" | custom-call | tf_op jit(solution)/shard_map/project_first/pallas_call | solution.py:247
  3.4 1.3 %collective-permute-done.right_ref = f32[16,1408]{1,0:T(8,128)S(1)} collective-permute-done((f32[16,1408]{1,0:T(8,128)S(1)}, f32[16,1408]{1,0:T(8,128)S(1)}, u32[]{:S(2)}, u32[]{:S(2)}) %collective-permute-start) | collective-permute-done | bytes 90144 | tf_op jit(solution)/shard_map/ppermute | solution.py:38
  4.7 2.2 %copy-done.2 = bf16[1,1,8,1024,256]{4,3,2,1,0:T(8,128)(2,1)S(1)} copy-done((bf16[1,1,8,1024,256]{4,3,2,1,0:T(8,128)(2,1)S(1)}, bf16[1,1,8,1024,256]{4,3,2,1,0:T(8,128)(2,1)}, u32[]{:S(2)}) %copy-start.2) | copy-done | bytes 4194328
  6.8 0.2 collective-permute-start.5
  7.0 0.4 collective-permute-start.1
  7.3 6.8 %collective-permute-done.1 = f32[16,1408]{1,0:T(8,128)S(1)} collective-permute-done((f32[16,1408]{1,0:T(8,128)S(1)}, f32[16,1408]{1,0:T(8,128)S(1)}, u32[]{:S(2)}, u32[]{:S(2)}) %collective-permute-start.1) | collective-permute-done | bytes 90144 | tf_op jit(solution)/shard_map/ppermute | solution.py:38
  14.1 0.2 collective-permute-start.4
  14.4 0.4 collective-permute-start.3
  14.7 0.2 collective-permute-start.2
  14.9 0.6 collective-permute-done.4
  15.5 0.2 collective-permute-done.3
  15.7 0.4 collective-permute-done.2
  16.1 2.5 %attend.2 = f32[136,128]{1,0:T(8,128)S(1)} custom-call(s32[2]{0:T(128)S(1)} %pad_add_fusion.ids_ref, s32[8]{0:T(128)S(1)} %copy-done.5, f32[16,1408]{1,0:T(8,128)S(1)} %add_add_fusion.1.own_ref, bf16[8,1024,256]{2,1,0:T(8,128)(2,1)S(1)} %bitcast.48, bf16[8,1024,256]{2,1,0:T(8,128)(2,1)S(1)} %collective-permute-done.5.sibling_ref), custom_call_target="tpu_custom_call" | custom-call | tf_op jit(solution)/shard_map/attend/pallas_call | solution.py:247
  18.6 0.2 collective-permute-start.6
  18.9 1.1 collective-permute-done.6
  20.1 0.2 collective-permute-start.9
  20.3 0.4 collective-permute-start.8
  20.7 0.2 collective-permute-start.7
  20.9 0.6 collective-permute-done.9
  21.4 0.2 collective-permute-done.8
  21.6 0.4 collective-permute-done.7
  22.1 0.2 collective-permute-start.10
  22.4 1.0 output_own.2.term_ref
  23.3 0.1 collective-permute-done.10.oth_ref
  23.4 1.0 output.2
  24.4 22.3 %collective-permute-start.12 = (f32[16,1024]{1,0:T(8,128)S(1)}, f32[16,1024]{1,0:T(8,128)S(1)}, u32[]{:S(2)}, u32[]{:S(2)}) collective-permute-start(f32[16,1024]{1,0:T(8,128)S(1)} %output.2), channel_id=1, source_target_pairs={{0,15},{1,14},{2,5},{3,4},{4,3},{5,2},{6,9},{7,8},{8,7},{9,6},{10,... | collective-permute-start | bytes 196616 | tf_op jit(solution)/shard_map/ppermute | solution.py:38
  46.7 2.5 %collective-permute-done.12 = f32[16,1024]{1,0:T(8,128)S(1)} collective-permute-done((f32[16,1024]{1,0:T(8,128)S(1)}, f32[16,1024]{1,0:T(8,128)S(1)}, u32[]{:S(2)}, u32[]{:S(2)}) %collective-permute-start.12) | collective-permute-done | bytes 65568 | tf_op jit(solution)/shard_map/ppermute | solution.py:38
  49.2 1.8 %collective-permute-done.11 = f32[16,1024]{1,0:T(8,128)S(1)} collective-permute-done((f32[16,1024]{1,0:T(8,128)S(1)}, f32[16,1024]{1,0:T(8,128)S(1)}, u32[]{:S(2)}, u32[]{:S(2)}) %collective-permute-start.11) | collective-permute-done | bytes 65568 | tf_op jit(solution)/shard_map/ppermute | solution.py:38
  51.1 0.3 collective-permute-start.14
  51.4 3.1 %collective-permute-start.13 = (f32[16,1024]{1,0:T(8,128)S(1)}, f32[16,1024]{1,0:T(8,128)S(1)}, u32[]{:S(2)}, u32[]{:S(2)}) collective-permute-start(f32[16,1024]{1,0:T(8,128)S(1)} %add.94), channel_id=1, source_target_pairs={{0,16},{1,7},{2,18},{3,13},{4,20},{5,11},{6,22},{7,1},{8,24},{9,15... | collective-permute-start | bytes 196616 | tf_op jit(solution)/shard_map/ppermute | solution.py:38
  54.5 2.9 %collective-permute-done.15 = f32[16,1024]{1,0:T(8,128)S(1)} collective-permute-done((f32[16,1024]{1,0:T(8,128)S(1)}, f32[16,1024]{1,0:T(8,128)S(1)}, u32[]{:S(2)}, u32[]{:S(2)}) %collective-permute-start.15) | collective-permute-done | bytes 65568 | tf_op jit(solution)/shard_map/ppermute | solution.py:38
  57.4 0.8 collective-permute-done.13
  58.3 1.0 project.1
  59.3 1.0 project_own.1
  60.3 0.3 collective-permute-done.16
  60.6 1.0 collective-permute-start.17
  61.6 5.3 %collective-permute-done.17 = f32[16,1408]{1,0:T(8,128)S(1)} collective-permute-done((f32[16,1408]{1,0:T(8,128)S(1)}, f32[16,1408]{1,0:T(8,128)S(1)}, u32[]{:S(2)}, u32[]{:S(2)}) %collective-permute-start.17) | collective-permute-done | bytes 90144 | tf_op jit(solution)/shard_map/ppermute | solution.py:38
  66.9 2.1 %collective-permute-start.20 = (f32[16,1408]{1,0:T(8,128)S(1)}, f32[16,1408]{1,0:T(8,128)S(1)}, u32[]{:S(2)}, u32[]{:S(2)}) collective-permute-start(f32[16,1408]{1,0:T(8,128)S(1)} %add.100), channel_id=1, source_target_pairs={{0,16},{1,129},{2,18},{3,131},{4,20},{5,133},{6,22},{7,135},{8,24}... | collective-permute-start | bytes 270344 | tf_op jit(solution)/shard_map/ppermute | solution.py:38
  69.0 1.2 %collective-permute-start.19 = (f32[16,1408]{1,0:T(8,128)S(1)}, f32[16,1408]{1,0:T(8,128)S(1)}, u32[]{:S(2)}, u32[]{:S(2)}) collective-permute-start(f32[16,1408]{1,0:T(8,128)S(1)} %add.100), channel_id=1, source_target_pairs={{0,16},{1,193},{2,18},{3,195},{4,20},{5,197},{6,22},{7,199},{8,24}... | collective-permute-start | bytes 270344 | tf_op jit(solution)/shard_map/ppermute | solution.py:38
  70.2 0.3 collective-permute-start.18
  70.5 2.7 %collective-permute-done.20 = f32[16,1408]{1,0:T(8,128)S(1)} collective-permute-done((f32[16,1408]{1,0:T(8,128)S(1)}, f32[16,1408]{1,0:T(8,128)S(1)}, u32[]{:S(2)}, u32[]{:S(2)}) %collective-permute-start.20) | collective-permute-done | bytes 90144 | tf_op jit(solution)/shard_map/ppermute | solution.py:38
  73.2 1.7 %collective-permute-done.19 = f32[16,1408]{1,0:T(8,128)S(1)} collective-permute-done((f32[16,1408]{1,0:T(8,128)S(1)}, f32[16,1408]{1,0:T(8,128)S(1)}, u32[]{:S(2)}, u32[]{:S(2)}) %collective-permute-start.19) | collective-permute-done | bytes 90144 | tf_op jit(solution)/shard_map/ppermute | solution.py:38
  74.9 2.5 %attend.3 = f32[136,128]{1,0:T(8,128)S(1)} custom-call(s32[2]{0:T(128)S(1)} %pad_add_fusion.ids_ref, s32[8]{0:T(128)S(1)} %copy-done.5, f32[16,1408]{1,0:T(8,128)S(1)} %add_add_fusion.own_ref, bf16[8,1024,256]{2,1,0:T(8,128)(2,1)S(1)} %bitcast.49, bf16[8,1024,256]{2,1,0:T(8,128)(2,1)S(1)} %collective-permute-done.5.sibling_ref), custom_call_target="tpu_custom_call" | custom-call | tf_op jit(solution)/shard_map/attend/pallas_call | solution.py:247
  77.4 1.0 collective-permute-start.21
  78.5 4.9 %collective-permute-done.21 = f32[136,128]{1,0:T(8,128)S(1)} collective-permute-done((f32[136,128]{1,0:T(8,128)S(1)}, f32[136,128]{1,0:T(8,128)S(1)}, u32[]{:S(2)}, u32[]{:S(2)}) %collective-permute-start.21) | collective-permute-done | bytes 69664 | tf_op jit(solution)/shard_map/ppermute | solution.py:38
  83.4 1.5 %collective-permute-start.24 = (f32[136,128]{1,0:T(8,128)S(1)}, f32[136,128]{1,0:T(8,128)S(1)}, u32[]{:S(2)}, u32[]{:S(2)}) collective-permute-start(f32[136,128]{1,0:T(8,128)S(1)} %add_select_fusion.1), channel_id=1, source_target_pairs={{0,16},{1,129},{2,18},{3,131},{4,20},{5,133},{6,22},{7,135},{8,24}... | collective-permute-start | bytes 208904 | tf_op jit(solution)/shard_map/ppermute | solution.py:38
  84.9 1.5 %collective-permute-start.23 = (f32[136,128]{1,0:T(8,128)S(1)}, f32[136,128]{1,0:T(8,128)S(1)}, u32[]{:S(2)}, u32[]{:S(2)}) collective-permute-start(f32[136,128]{1,0:T(8,128)S(1)} %add_select_fusion.1), channel_id=1, source_target_pairs={{0,16},{1,193},{2,18},{3,195},{4,20},{5,197},{6,22},{7,199},{8,24}... | collective-permute-start | bytes 208904 | tf_op jit(solution)/shard_map/ppermute | solution.py:38
  86.4 0.6 collective-permute-start.22
  87.0 2.3 %collective-permute-done.24 = f32[136,128]{1,0:T(8,128)S(1)} collective-permute-done((f32[136,128]{1,0:T(8,128)S(1)}, f32[136,128]{1,0:T(8,128)S(1)}, u32[]{:S(2)}, u32[]{:S(2)}) %collective-permute-start.24) | collective-permute-done | bytes 69664 | tf_op jit(solution)/shard_map/ppermute | solution.py:38
  89.3 1.1 collective-permute-done.23
  90.4 0.3 collective-permute-done.22
  90.8 0.1 collective-permute-done.25
  90.9 1.0 output_own.3.term_ref
  91.9 0.3 collective-permute-done.26.oth_ref
  92.2 1.0 output.3
  93.2 3.6 %collective-permute-start.27 = (f32[16,1024]{1,0:T(8,128)S(1)}, f32[16,1024]{1,0:T(8,128)S(1)}, u32[]{:S(2)}, u32[]{:S(2)}) collective-permute-start(f32[16,1024]{1,0:T(8,128)S(1)} %output.3), channel_id=1, source_target_pairs={{0,16},{1,15},{2,18},{3,5},{4,20},{5,3},{6,22},{7,9},{8,24},{9,7},... | collective-permute-start | bytes 196616 | tf_op jit(solution)/shard_map/ppermute | solution.py:38
  96.8 2.5 %collective-permute-done.27 = f32[16,1024]{1,0:T(8,128)S(1)} collective-permute-done((f32[16,1024]{1,0:T(8,128)S(1)}, f32[16,1024]{1,0:T(8,128)S(1)}, u32[]{:S(2)}, u32[]{:S(2)}) %collective-permute-start.27) | collective-permute-done | bytes 65568 | tf_op jit(solution)/shard_map/ppermute | solution.py:38
  99.3 1.5 %collective-permute-start.30 = (f32[16,1024]{1,0:T(8,128)S(1)}, f32[16,1024]{1,0:T(8,128)S(1)}, u32[]{:S(2)}, u32[]{:S(2)}) collective-permute-start(f32[16,1024]{1,0:T(8,128)S(1)} %add.108), channel_id=1, source_target_pairs={{0,16},{1,5},{2,18},{3,15},{4,20},{5,9},{6,22},{7,3},{8,24},{9,13}... | collective-permute-start | bytes 196616 | tf_op jit(solution)/shard_map/ppermute | solution.py:38
  100.8 3.1 %collective-permute-start.29 = (f32[16,1024]{1,0:T(8,128)S(1)}, f32[16,1024]{1,0:T(8,128)S(1)}, u32[]{:S(2)}, u32[]{:S(2)}) collective-permute-start(f32[16,1024]{1,0:T(8,128)S(1)} %add.108), channel_id=1, source_target_pairs={{0,16},{1,3},{2,18},{3,1},{4,20},{5,7},{6,22},{7,5},{8,24},{9,11},... | collective-permute-start | bytes 196616 | tf_op jit(solution)/shard_map/ppermute | solution.py:38
  103.8 1.9 %collective-permute-start.28 = (f32[16,1024]{1,0:T(8,128)S(1)}, f32[16,1024]{1,0:T(8,128)S(1)}, u32[]{:S(2)}, u32[]{:S(2)}) collective-permute-start(f32[16,1024]{1,0:T(8,128)S(1)} %add.108), channel_id=1, source_target_pairs={{0,16},{1,7},{2,18},{3,13},{4,20},{5,11},{6,22},{7,1},{8,24},{9,15... | collective-permute-start | bytes 196616 | tf_op jit(solution)/shard_map/ppermute | solution.py:38
  105.7 0.2 collective-permute-done.30
  105.9 2.3 %collective-permute-done.29 = f32[16,1024]{1,0:T(8,128)S(1)} collective-permute-done((f32[16,1024]{1,0:T(8,128)S(1)}, f32[16,1024]{1,0:T(8,128)S(1)}, u32[]{:S(2)}, u32[]{:S(2)}) %collective-permute-start.29) | collective-permute-done | bytes 65568 | tf_op jit(solution)/shard_map/ppermute | solution.py:38
  108.2 1.9 %collective-permute-done.28 = f32[16,1024]{1,0:T(8,128)S(1)} collective-permute-done((f32[16,1024]{1,0:T(8,128)S(1)}, f32[16,1024]{1,0:T(8,128)S(1)}, u32[]{:S(2)}, u32[]{:S(2)}) %collective-permute-start.28) | collective-permute-done | bytes 65568 | tf_op jit(solution)/shard_map/ppermute | solution.py:38
  110.1 0.6 fusion.1
  (43 shorter events, 0.9 us)
Async XLA Ops:
  3.3 1.4 %collective-permute-start = (f32[16,1408]{1,0:T(8,128)S(1)}, f32[16,1408]{1,0:T(8,128)S(1)}, u32[]{:S(2)}, u32[]{:S(2)}) collective-permute-start(f32[16,1408]{1,0:T(8,128)S(1)} %get-tuple-element.16), channel_id=1, source_target_pairs={{0,16},{1,17},{2,18},{3,19},{4,20},{5,21},{6,22},{7,23},{8,24},{9,... | collective-permute-start | bytes 270344 | tf_op jit(solution)/shard_map/ppermute | solution.py:38
  4.6 2.2 %copy-start.2 = (bf16[1,1,8,1024,256]{4,3,2,1,0:T(8,128)(2,1)S(1)}, bf16[1,1,8,1024,256]{4,3,2,1,0:T(8,128)(2,1)}, u32[]{:S(2)}) copy-start(bf16[1,1,8,1024,256]{4,3,2,1,0:T(8,128)(2,1)} %param.13) | copy-start | bytes 12582916
  4.7 11.4 %copy-start.5 = (s32[8]{0:T(128)S(1)}, s32[8]{0:T(128)}, u32[]{:S(2)}) copy-start(s32[8]{0:T(128)} %len_ref.3) | copy-start | bytes 100
  6.8 9.2 %collective-permute-start.5 = (bf16[8,1024,256]{2,1,0:T(8,128)(2,1)S(1)}, bf16[8,1024,256]{2,1,0:T(8,128)(2,1)S(1)}, u32[]{:S(2)}, u32[]{:S(2)}) collective-permute-start(bf16[8,1024,256]{2,1,0:T(8,128)(2,1)S(1)} %bitcast.47), channel_id=1, source_target_pairs={{0,16},{1,17},{2,18},{3,19},{4,20},{5,21},{6,22},{7,23},{8,24},{9,... | collective-permute-start | bytes 12582920 | tf_op jit(solution)/shard_map/ppermute | solution.py:38
  7.0 7.1 %collective-permute-start.1 = (f32[16,1408]{1,0:T(8,128)S(1)}, f32[16,1408]{1,0:T(8,128)S(1)}, u32[]{:S(2)}, u32[]{:S(2)}) collective-permute-start(f32[16,1408]{1,0:T(8,128)S(1)} %add_first.1), channel_id=1, source_target_pairs={{0,32},{1,17},{2,34},{3,19},{4,36},{5,21},{6,38},{7,23},{8,40},{9,... | collective-permute-start | bytes 270344 | tf_op jit(solution)/shard_map/ppermute | solution.py:38
  14.1 1.4 %collective-permute-start.4 = (f32[16,1408]{1,0:T(8,128)S(1)}, f32[16,1408]{1,0:T(8,128)S(1)}, u32[]{:S(2)}, u32[]{:S(2)}) collective-permute-start(f32[16,1408]{1,0:T(8,128)S(1)} %add.86), channel_id=1, source_target_pairs={{0,128},{1,17},{2,130},{3,19},{4,132},{5,21},{6,134},{7,23},{8,136... | collective-permute-start | bytes 270344 | tf_op jit(solution)/shard_map/ppermute | solution.py:38
  14.4 1.3 %collective-permute-start.3 = (f32[16,1408]{1,0:T(8,128)S(1)}, f32[16,1408]{1,0:T(8,128)S(1)}, u32[]{:S(2)}, u32[]{:S(2)}) collective-permute-start(f32[16,1408]{1,0:T(8,128)S(1)} %add.86), channel_id=1, source_target_pairs={{0,192},{1,17},{2,194},{3,19},{4,196},{5,21},{6,198},{7,23},{8,200... | collective-permute-start | bytes 270344 | tf_op jit(solution)/shard_map/ppermute | solution.py:38
  14.7 1.3 %collective-permute-start.2 = (f32[16,1408]{1,0:T(8,128)S(1)}, f32[16,1408]{1,0:T(8,128)S(1)}, u32[]{:S(2)}, u32[]{:S(2)}) collective-permute-start(f32[16,1408]{1,0:T(8,128)S(1)} %add.86), channel_id=1, source_target_pairs={{0,64},{1,17},{2,66},{3,19},{4,68},{5,21},{6,70},{7,23},{8,72},{9,... | collective-permute-start | bytes 270344 | tf_op jit(solution)/shard_map/ppermute | solution.py:38
  16.1 6.3 %copy-start = (bf16[1,2048,1024]{2,1,0:T(8,128)(2,1)S(1)}, bf16[1,2048,1024]{2,1,0:T(8,128)(2,1)}, u32[]{:S(2)}) copy-start(bf16[1,2048,1024]{2,1,0:T(8,128)(2,1)} %param.12) | copy-start | bytes 12582916
  18.6 1.3 %collective-permute-start.6 = (f32[136,128]{1,0:T(8,128)S(1)}, f32[136,128]{1,0:T(8,128)S(1)}, u32[]{:S(2)}, u32[]{:S(2)}) collective-permute-start(f32[136,128]{1,0:T(8,128)S(1)} %attend.2), channel_id=1, source_target_pairs={{0,32},{1,17},{2,34},{3,19},{4,36},{5,21},{6,38},{7,23},{8,40},{9,... | collective-permute-start | bytes 208904 | tf_op jit(solution)/shard_map/ppermute | solution.py:38
  20.1 1.3 %collective-permute-start.9 = (f32[136,128]{1,0:T(8,128)S(1)}, f32[136,128]{1,0:T(8,128)S(1)}, u32[]{:S(2)}, u32[]{:S(2)}) collective-permute-start(f32[136,128]{1,0:T(8,128)S(1)} %add_select_fusion.3), channel_id=1, source_target_pairs={{0,128},{1,17},{2,130},{3,19},{4,132},{5,21},{6,134},{7,23},{8,136... | collective-permute-start | bytes 208904 | tf_op jit(solution)/shard_map/ppermute | solution.py:38
  20.3 1.3 %collective-permute-start.8 = (f32[136,128]{1,0:T(8,128)S(1)}, f32[136,128]{1,0:T(8,128)S(1)}, u32[]{:S(2)}, u32[]{:S(2)}) collective-permute-start(f32[136,128]{1,0:T(8,128)S(1)} %add_select_fusion.3), channel_id=1, source_target_pairs={{0,192},{1,17},{2,194},{3,19},{4,196},{5,21},{6,198},{7,23},{8,200... | collective-permute-start | bytes 208904 | tf_op jit(solution)/shard_map/ppermute | solution.py:38
  20.7 1.3 %collective-permute-start.7 = (f32[136,128]{1,0:T(8,128)S(1)}, f32[136,128]{1,0:T(8,128)S(1)}, u32[]{:S(2)}, u32[]{:S(2)}) collective-permute-start(f32[136,128]{1,0:T(8,128)S(1)} %add_select_fusion.3), channel_id=1, source_target_pairs={{0,64},{1,17},{2,66},{3,19},{4,68},{5,21},{6,70},{7,23},{8,72},{9,... | collective-permute-start | bytes 208904 | tf_op jit(solution)/shard_map/ppermute | solution.py:38
  22.1 1.3 %collective-permute-start.10 = (f32[136,128]{1,0:T(8,128)S(1)}, f32[136,128]{1,0:T(8,128)S(1)}, u32[]{:S(2)}, u32[]{:S(2)}) collective-permute-start(f32[136,128]{1,0:T(8,128)S(1)} %add_select_fusion.2.own_ref), channel_id=1, source_target_pairs={{0,16},{1,17},{2,18},{3,19},{4,20},{5,21},{6,22},{7,23},{8,24},{9,... | collective-permute-start | bytes 208904 | tf_op jit(solution)/shard_map/ppermute | solution.py:38
  22.3 35.9 %copy-start.6 = (bf16[2,8,1024]{2,1,0:T(8,128)(2,1)S(1)}, bf16[2,8,1024]{2,1,0:T(8,128)(2,1)}, u32[]{:S(2)}) copy-start(bf16[2,8,1024]{2,1,0:T(8,128)(2,1)} %param.7) | copy-start | bytes 98308
  22.3 35.9 %copy-start.1 = (bf16[1,1024,2048]{2,1,0:T(8,128)(2,1)S(1)}, bf16[1,1024,2048]{2,1,0:T(8,128)(2,1)}, u32[]{:S(2)}) copy-start(bf16[1,1024,2048]{2,1,0:T(8,128)(2,1)} %param.10) | copy-start | bytes 12582916
  22.3 35.9 %copy-start.3 = (bf16[1,1024,1,256]{3,1,2,0:T(8,128)(2,1)S(1)}, bf16[1,1024,1,256]{3,1,2,0:T(8,128)(2,1)}, u32[]{:S(2)}) copy-start(bf16[1,1024,1,256]{3,1,2,0:T(8,128)(2,1)} %param.11) | copy-start | bytes 1572868
  22.3 35.9 %copy-start.4 = (bf16[1,1024]{1,0:T(2,128)(2,1)S(1)}, bf16[1,1024]{1,0:T(2,128)(2,1)}, u32[]{:S(2)}) copy-start(bf16[1,1024]{1,0:T(2,128)(2,1)} %gain_ref.1) | copy-start | bytes 6148
  24.4 24.8 %collective-permute-start.12 = (f32[16,1024]{1,0:T(8,128)S(1)}, f32[16,1024]{1,0:T(8,128)S(1)}, u32[]{:S(2)}, u32[]{:S(2)}) collective-permute-start(f32[16,1024]{1,0:T(8,128)S(1)} %output.2), channel_id=1, source_target_pairs={{0,15},{1,14},{2,5},{3,4},{4,3},{5,2},{6,9},{7,8},{8,7},{9,6},{10,... | collective-permute-start | bytes 196616 | tf_op jit(solution)/shard_map/ppermute | solution.py:38
  46.7 4.3 %collective-permute-start.11 = (f32[16,1024]{1,0:T(8,128)S(1)}, f32[16,1024]{1,0:T(8,128)S(1)}, u32[]{:S(2)}, u32[]{:S(2)}) collective-permute-start(f32[16,1024]{1,0:T(8,128)S(1)} %output.2), channel_id=1, source_target_pairs={{0,1},{1,0},{2,3},{3,2},{4,5},{5,4},{6,7},{7,6},{8,9},{9,8},{10,11... | collective-permute-start | bytes 196616 | tf_op jit(solution)/shard_map/ppermute | solution.py:38
  51.0 6.4 %collective-permute-start.15 = (f32[16,1024]{1,0:T(8,128)S(1)}, f32[16,1024]{1,0:T(8,128)S(1)}, u32[]{:S(2)}, u32[]{:S(2)}) collective-permute-start(f32[16,1024]{1,0:T(8,128)S(1)} %add.94), channel_id=1, source_target_pairs={{0,16},{1,5},{2,18},{3,15},{4,20},{5,9},{6,22},{7,3},{8,24},{9,13}... | collective-permute-start | bytes 196616 | tf_op jit(solution)/shard_map/ppermute | solution.py:38
  51.1 6.4 %collective-permute-start.14 = (f32[16,1024]{1,0:T(8,128)S(1)}, f32[16,1024]{1,0:T(8,128)S(1)}, u32[]{:S(2)}, u32[]{:S(2)}) collective-permute-start(f32[16,1024]{1,0:T(8,128)S(1)} %add.94), channel_id=1, source_target_pairs={{0,16},{1,3},{2,18},{3,1},{4,20},{5,7},{6,22},{7,5},{8,24},{9,11},... | collective-permute-start | bytes 196616 | tf_op jit(solution)/shard_map/ppermute | solution.py:38
  51.4 6.8 %collective-permute-start.13 = (f32[16,1024]{1,0:T(8,128)S(1)}, f32[16,1024]{1,0:T(8,128)S(1)}, u32[]{:S(2)}, u32[]{:S(2)}) collective-permute-start(f32[16,1024]{1,0:T(8,128)S(1)} %add.94), channel_id=1, source_target_pairs={{0,16},{1,7},{2,18},{3,13},{4,20},{5,11},{6,22},{7,1},{8,24},{9,15... | collective-permute-start | bytes 196616 | tf_op jit(solution)/shard_map/ppermute | solution.py:38
  59.3 1.3 %collective-permute-start.16 = (f32[16,1408]{1,0:T(8,128)S(1)}, f32[16,1408]{1,0:T(8,128)S(1)}, u32[]{:S(2)}, u32[]{:S(2)}) collective-permute-start(f32[16,1408]{1,0:T(8,128)S(1)} %get-tuple-element.20.first_ref), channel_id=1, source_target_pairs={{0,16},{1,17},{2,18},{3,19},{4,20},{5,21},{6,22},{7,23},{8,24},{9,... | collective-permute-start | bytes 270344 | tf_op jit(solution)/shard_map/ppermute | solution.py:38
  60.6 6.3 %collective-permute-start.17 = (f32[16,1408]{1,0:T(8,128)S(1)}, f32[16,1408]{1,0:T(8,128)S(1)}, u32[]{:S(2)}, u32[]{:S(2)}) collective-permute-start(f32[16,1408]{1,0:T(8,128)S(1)} %add.99), channel_id=1, source_target_pairs={{0,16},{1,33},{2,18},{3,35},{4,20},{5,37},{6,22},{7,39},{8,24},{9,... | collective-permute-start | bytes 270344 | tf_op jit(solution)/shard_map/ppermute | solution.py:38
  66.9 6.2 %collective-permute-start.20 = (f32[16,1408]{1,0:T(8,128)S(1)}, f32[16,1408]{1,0:T(8,128)S(1)}, u32[]{:S(2)}, u32[]{:S(2)}) collective-permute-start(f32[16,1408]{1,0:T(8,128)S(1)} %add.100), channel_id=1, source_target_pairs={{0,16},{1,129},{2,18},{3,131},{4,20},{5,133},{6,22},{7,135},{8,24}... | collective-permute-start | bytes 270344 | tf_op jit(solution)/shard_map/ppermute | solution.py:38
  69.0 5.8 %collective-permute-start.19 = (f32[16,1408]{1,0:T(8,128)S(1)}, f32[16,1408]{1,0:T(8,128)S(1)}, u32[]{:S(2)}, u32[]{:S(2)}) collective-permute-start(f32[16,1408]{1,0:T(8,128)S(1)} %add.100), channel_id=1, source_target_pairs={{0,16},{1,193},{2,18},{3,195},{4,20},{5,197},{6,22},{7,199},{8,24}... | collective-permute-start | bytes 270344 | tf_op jit(solution)/shard_map/ppermute | solution.py:38
  70.2 4.6 %collective-permute-start.18 = (f32[16,1408]{1,0:T(8,128)S(1)}, f32[16,1408]{1,0:T(8,128)S(1)}, u32[]{:S(2)}, u32[]{:S(2)}) collective-permute-start(f32[16,1408]{1,0:T(8,128)S(1)} %add.100), channel_id=1, source_target_pairs={{0,16},{1,65},{2,18},{3,67},{4,20},{5,69},{6,22},{7,71},{8,24},{9,... | collective-permute-start | bytes 270344 | tf_op jit(solution)/shard_map/ppermute | solution.py:38
  77.4 5.9 %collective-permute-start.21 = (f32[136,128]{1,0:T(8,128)S(1)}, f32[136,128]{1,0:T(8,128)S(1)}, u32[]{:S(2)}, u32[]{:S(2)}) collective-permute-start(f32[136,128]{1,0:T(8,128)S(1)} %attend.3), channel_id=1, source_target_pairs={{0,16},{1,33},{2,18},{3,35},{4,20},{5,37},{6,22},{7,39},{8,24},{9,... | collective-permute-start | bytes 208904 | tf_op jit(solution)/shard_map/ppermute | solution.py:38
  83.4 5.9 %collective-permute-start.24 = (f32[136,128]{1,0:T(8,128)S(1)}, f32[136,128]{1,0:T(8,128)S(1)}, u32[]{:S(2)}, u32[]{:S(2)}) collective-permute-start(f32[136,128]{1,0:T(8,128)S(1)} %add_select_fusion.1), channel_id=1, source_target_pairs={{0,16},{1,129},{2,18},{3,131},{4,20},{5,133},{6,22},{7,135},{8,24}... | collective-permute-start | bytes 208904 | tf_op jit(solution)/shard_map/ppermute | solution.py:38
  84.9 5.5 %collective-permute-start.23 = (f32[136,128]{1,0:T(8,128)S(1)}, f32[136,128]{1,0:T(8,128)S(1)}, u32[]{:S(2)}, u32[]{:S(2)}) collective-permute-start(f32[136,128]{1,0:T(8,128)S(1)} %add_select_fusion.1), channel_id=1, source_target_pairs={{0,16},{1,193},{2,18},{3,195},{4,20},{5,197},{6,22},{7,199},{8,24}... | collective-permute-start | bytes 208904 | tf_op jit(solution)/shard_map/ppermute | solution.py:38
  86.4 4.3 %collective-permute-start.22 = (f32[136,128]{1,0:T(8,128)S(1)}, f32[136,128]{1,0:T(8,128)S(1)}, u32[]{:S(2)}, u32[]{:S(2)}) collective-permute-start(f32[136,128]{1,0:T(8,128)S(1)} %add_select_fusion.1), channel_id=1, source_target_pairs={{0,16},{1,65},{2,18},{3,67},{4,20},{5,69},{6,22},{7,71},{8,24},{9,... | collective-permute-start | bytes 208904 | tf_op jit(solution)/shard_map/ppermute | solution.py:38
  87.0 3.9 %collective-permute-start.25 = (bf16[16,1024]{1,0:T(8,128)(2,1)S(1)}, bf16[16,1024]{1,0:T(8,128)(2,1)S(1)}, u32[]{:S(2)}, u32[]{:S(2)}) collective-permute-start(bf16[16,1024]{1,0:T(8,128)(2,1)S(1)} %add_convert_fusion.1.hidden_ref), channel_id=1, source_target_pairs={{0,1},{1,0},{2,3},{3,2},{4,5},{5,4},{6,7},{7,6},{8,9},{9,8},{10,11... | collective-permute-start | bytes 98312 | tf_op jit(solution)/shard_map/ppermute | solution.py:262
  90.9 1.3 %collective-permute-start.26 = (f32[136,128]{1,0:T(8,128)S(1)}, f32[136,128]{1,0:T(8,128)S(1)}, u32[]{:S(2)}, u32[]{:S(2)}) collective-permute-start(f32[136,128]{1,0:T(8,128)S(1)} %add_select_fusion.own_ref), channel_id=1, source_target_pairs={{0,16},{1,17},{2,18},{3,19},{4,20},{5,21},{6,22},{7,23},{8,24},{9,... | collective-permute-start | bytes 208904 | tf_op jit(solution)/shard_map/ppermute | solution.py:38
  93.2 6.1 %collective-permute-start.27 = (f32[16,1024]{1,0:T(8,128)S(1)}, f32[16,1024]{1,0:T(8,128)S(1)}, u32[]{:S(2)}, u32[]{:S(2)}) collective-permute-start(f32[16,1024]{1,0:T(8,128)S(1)} %output.3), channel_id=1, source_target_pairs={{0,16},{1,15},{2,18},{3,5},{4,20},{5,3},{6,22},{7,9},{8,24},{9,7},... | collective-permute-start | bytes 196616 | tf_op jit(solution)/shard_map/ppermute | solution.py:38
  99.3 6.6 %collective-permute-start.30 = (f32[16,1024]{1,0:T(8,128)S(1)}, f32[16,1024]{1,0:T(8,128)S(1)}, u32[]{:S(2)}, u32[]{:S(2)}) collective-permute-start(f32[16,1024]{1,0:T(8,128)S(1)} %add.108), channel_id=1, source_target_pairs={{0,16},{1,5},{2,18},{3,15},{4,20},{5,9},{6,22},{7,3},{8,24},{9,13}... | collective-permute-start | bytes 196616 | tf_op jit(solution)/shard_map/ppermute | solution.py:38
  100.8 7.4 %collective-permute-start.29 = (f32[16,1024]{1,0:T(8,128)S(1)}, f32[16,1024]{1,0:T(8,128)S(1)}, u32[]{:S(2)}, u32[]{:S(2)}) collective-permute-start(f32[16,1024]{1,0:T(8,128)S(1)} %add.108), channel_id=1, source_target_pairs={{0,16},{1,3},{2,18},{3,1},{4,20},{5,7},{6,22},{7,5},{8,24},{9,11},... | collective-permute-start | bytes 196616 | tf_op jit(solution)/shard_map/ppermute | solution.py:38
  103.8 6.2 %collective-permute-start.28 = (f32[16,1024]{1,0:T(8,128)S(1)}, f32[16,1024]{1,0:T(8,128)S(1)}, u32[]{:S(2)}, u32[]{:S(2)}) collective-permute-start(f32[16,1024]{1,0:T(8,128)S(1)} %add.108), channel_id=1, source_target_pairs={{0,16},{1,7},{2,18},{3,13},{4,20},{5,11},{6,22},{7,1},{8,24},{9,15... | collective-permute-start | bytes 196616 | tf_op jit(solution)/shard_map/ppermute | solution.py:38
